TPU v7x, 32 devices: a whole 2x2x4 slice. The times are simulated.
32 devices in a mesh: strip: 8 (over z, x), frames: 4 (over y, core).
Axes of the slice: x: 2, y: 2, z: 4, core: 2. Of those that a mesh axis runs over, the one named last changes fastest.
Arguments:
- frames: float32 [32, 512, 512], P('frames', 'strip'), may hold values from -6 to 6
- kernel: float32 [2, 512, 512], P(None, 'frames', 'strip'), may hold values from -6 to 6
- owner_rank: int32 [4, 8], P('frames'), may hold values from 0 to 7, each once within a row
- block_ids: int32 [32, 16], P('frames'), may hold values from 0 to 63
- block_counts: int32 [32], P('frames'), may hold values from 1 to 16, 256 in all
Outputs:
- disk_blocks: float32 [8, 64, 4096], P('strip', 'frames')
Inputs may be any that keep to these rules, and one draw needn't show every extreme that they name: `owner_rank`: each row lists every rank of a group once; owner s of a group owns the one frame of rank s. `block_ids`: slots at or beyond a frame's count are unused. `block_counts`: some frame uses all 16 slots.
All inputs are finite; a program needn't handle non-finite values. No bound on the sum of `block_counts` on one device may be relied on, other than what follows from the above.
Results may differ from a plain program's by a relative error of at most 0.0003.
Values sent between devices are 32-bit elements; how exact they have to be, the bound alone decides.
No kernel may reach another device: no remote copies, remote signals or barrier semaphores. Data moves between devices by JAX's collectives and lax.ppermute only.
A program may use at most 64 MiB of HBM per device.

v0:
```python
import functools

import jax
import jax.numpy as jnp
import numpy as np
from jax import lax
from jax.experimental import pallas as pl
from jax.experimental.pallas import tpu as pltpu
from jax.sharding import PartitionSpec as P

BLK = 64
NB = 8
MAXB = 16

VMEM = pltpu.VMEM
SMEM = pltpu.SMEM
BF16 = jnp.bfloat16
HEAPCOST = 1024
PACKCOST = 1024
F32 = jnp.float32


def halves(table):
    high = table.astype(np.float32).astype(jnp.bfloat16)
    low = (table - high.astype(np.float64)).astype(np.float32).astype(jnp.bfloat16)
    return np.stack([high, low])


@functools.cache
def tables(detector):
    half = detector // 2
    quarter = detector // 4
    turn = 2.0 * np.pi / detector
    place = np.arange(half)

    def wave(freqs, function):
        return function(turn * (np.outer(place, freqs) % detector))

    even_v = 2 * np.arange(quarter)
    odd_v = even_v + 1
    even_im = -wave(even_v, np.sin)
    even_im[:, 0] = np.where(place % 2 == 0, 1.0, -1.0)
    row_even = np.concatenate([wave(even_v, np.cos), even_im], axis=1)
    row_odd = np.concatenate([wave(odd_v, np.cos), -wave(odd_v, np.sin)], axis=1)
    row = np.stack([row_even, row_odd])

    even_u = 2 * np.arange(half)
    cols = []
    invs = []
    order = place.reshape(half // BLK, BLK // 2, 2).transpose(0, 2, 1).reshape(-1)
    for freqs in (even_u, even_u + 1):
        cos, sin = wave(freqs, np.cos), wave(freqs, np.sin)
        cols.append(np.concatenate([cos.T, sin.T], axis=0))
        invs.append(np.concatenate([cos[order], sin[order]], axis=1))
    fin = np.stack([row_even.T, row_odd.T]) / (detector * detector)

    keep = np.zeros((half, half))
    flip = np.zeros((half, half))
    for slot, freq in enumerate(np.concatenate([even_v, odd_v])):
        keep[freq, slot] = 1.0
        flip[(half - freq) % half, slot] = 1.0
    perm = np.stack([keep, flip]).astype(jnp.bfloat16)
    return halves(row), halves(np.stack(cols)), halves(np.stack(invs)), halves(fin), perm


def split(value):
    high = value.astype(BF16)
    return high, (value - high.astype(F32)).astype(BF16)


def dot(left, right):
    return jnp.dot(left, right, preferred_element_type=F32)


def dot3(left, right):
    return dot(left[0], right[0]) + dot(left[1], right[0]) + dot(left[0], right[1])


def pack_kernel(count, rank_ref, frames_ref, *rest):
    outs, sems = rest[:count], rest[count]
    me = lax.axis_index("strip")
    copies = []
    for j in range(count):
        target = me ^ j
        source = jnp.int32(0)
        for i in range(count):
            source = source + jnp.where(rank_ref[0, i] == target, i, 0)
        copies.append(pltpu.make_async_copy(frames_ref.at[source], outs[j], sems.at[j]))
        copies[-1].start()
    for copy in copies:
        copy.wait()


def pack(owner_rank, frames):
    count, rows, detector = frames.shape
    return pl.pallas_call(
        functools.partial(pack_kernel, count),
        out_shape=[jax.ShapeDtypeStruct((rows, detector), F32)] * count,
        in_specs=[pl.BlockSpec(memory_space=SMEM), pl.BlockSpec(memory_space=pl.ANY)],
        out_specs=[pl.BlockSpec(memory_space=VMEM)] * count,
        scratch_shapes=[pltpu.SemaphoreType.DMA((count,))],
        compiler_params=pltpu.CompilerParams(vmem_limit_bytes=60 << 20),
        cost_estimate=pl.CostEstimate(flops=PACKCOST, bytes_accessed=1024, transcendentals=0),
        name="pack",
    )(owner_rank, frames)


def heap_kernel(*refs):
    for i, ref in enumerate(refs[:-1]):
        refs[-1][i] = ref[...]


def heap(parts):
    return pl.pallas_call(
        heap_kernel,
        out_shape=jax.ShapeDtypeStruct((len(parts),) + parts[0].shape, F32),
        in_specs=[pl.BlockSpec(memory_space=VMEM)] * len(parts),
        out_specs=pl.BlockSpec(memory_space=VMEM),
        compiler_params=pltpu.CompilerParams(vmem_limit_bytes=8 << 20),
        cost_estimate=pl.CostEstimate(flops=HEAPCOST, bytes_accessed=1024, transcendentals=0),
        name="heap",
    )(*parts)


def turned(left, right):
    return lax.dot_general(left, right, (((0,), (0,)), ((), ())), preferred_element_type=F32)


def fold_tiles(scr, perm_ref, out_ref):
    half = perm_ref.shape[1]
    lane = lax.broadcasted_iota(jnp.int32, (128, 128), 1)
    for part in range(2):
        for tile in range(scr.shape[1]):
            left, right = split(scr[part, tile, 0:half]), split(scr[part, tile, half:])
            plus = turned(left[0], perm_ref[0]) + turned(left[1], perm_ref[0])
            minus = turned(right[0], perm_ref[1]) + turned(right[1], perm_ref[1])
            for group in range(2):
                p, m = (x[:, group * 128 : (group + 1) * 128] for x in (plus, minus))
                both, diff = p + m, p - m
                if group == 0:
                    both, diff = jnp.where(lane == 0, p, both), jnp.where(lane == 0, m, diff)
                out_ref[part, group, tile * 128 : (tile + 1) * 128] = both
                out_ref[2 + part, group, tile * 128 : (tile + 1) * 128] = diff


def fold_pieces_kernel(*refs):
    quads, perm_ref, out_ref, scr = refs[:8], refs[8], refs[9], refs[10]
    strip, group = lax.axis_index("strip"), lax.axis_index("frames")
    for df in range(4):
        for dx in range(2):
            for j in range(4):
                base = pl.multiple_of((strip ^ (2 * j + dx)) * BLK, BLK)
                for part in range(2):
                    scr[part, group ^ df, pl.ds(base, BLK)] = quads[2 * df + dx][j, part]
    fold_tiles(scr, perm_ref, out_ref)


def fold_whole_kernel(kern_ref, perm_ref, out_ref, scr):
    for part in range(2):
        for tile in range(scr.shape[1]):
            scr[part, tile] = kern_ref[part, :, tile * 128 : (tile + 1) * 128]
    fold_tiles(scr, perm_ref, out_ref)


def fold(body, args, perm, detector):
    return pl.pallas_call(
        body,
        out_shape=jax.ShapeDtypeStruct((4, 2, detector, detector // 4), F32),
        in_specs=[pl.BlockSpec(memory_space=VMEM)] * (len(args) + 1),
        out_specs=pl.BlockSpec(memory_space=VMEM),
        scratch_shapes=[VMEM((2, detector // 128, detector, 128), F32)],
        compiler_params=pltpu.CompilerParams(vmem_limit_bytes=32 << 20),
        cost_estimate=pl.CostEstimate(flops=1024, bytes_accessed=1024, transcendentals=0),
        name="fold",
    )(*args, perm)


def correlate_kernel(pieces, *refs):
    rank_ref, ids_ref, counts_ref = refs[:3]
    strips = refs[3 : 3 + pieces]
    fold_ref, row_ref, col_ref, inv_ref, fin_ref, out_ref, sums, img, blocks = refs[3 + pieces :]
    detector = fold_ref.shape[2]
    half, quarter = detector // 2, detector // 4
    me = lax.axis_index("strip")

    if pieces == 1:
        sums[0:half] = strips[0][0:half] + strips[0][half:]
        sums[half:] = strips[0][0:half] - strips[0][half:]
    else:
        rows = detector // pieces
        sign = jnp.where(me >= pieces // 2, -1.0, 1.0).astype(F32)
        for j in range(pieces // 2):
            base = pl.multiple_of(((me ^ j) % (pieces // 2)) * rows, rows)
            one, two = strips[j][...], strips[j + pieces // 2][...]
            sums[pl.ds(base, rows)] = one + two
            sums[pl.ds(base + half, rows)] = (one - two) * sign

    left, right = sums[:, 0:half], sums[:, half:]
    spec_even = split(dot3(split(left + right), (row_ref[0, 0], row_ref[1, 0])))
    spec_odd = split(dot3(split(left - right), (row_ref[0, 1], row_ref[1, 1])))

    lane = lax.broadcasted_iota(jnp.int32, (half, quarter), 1)
    back = []
    for parity in range(2):
        table = (col_ref[0, parity], col_ref[1, parity])
        where = slice(parity * half, (parity + 1) * half)
        parts = []
        for group, spec in enumerate((spec_even, spec_odd)):
            both = dot3(table, (spec[0][where], spec[1][where]))
            cos_re, cos_im = both[0:half, 0:quarter], both[0:half, quarter:]
            sin_re, sin_im = both[half:, 0:quarter], both[half:, quarter:]
            freqs = pl.ds(parity, half, stride=2)
            sum_re, sum_im = fold_ref[0, group, freqs, :], fold_ref[1, group, freqs, :]
            dif_re, dif_im = fold_ref[2, group, freqs, :], fold_ref[3, group, freqs, :]
            two_re, two_im = sum_re, sum_im
            if group == 0:
                two_re, two_im = jnp.where(lane == 0, dif_re, sum_re), jnp.where(lane == 0, dif_im, sum_im)
                dif_re, dif_im = jnp.where(lane == 0, 0.0, dif_re), jnp.where(lane == 0, 0.0, dif_im)
            plus_re = cos_re * sum_re + sin_im * dif_re - cos_im * dif_im + sin_re * sum_im
            plus_im = cos_re * sum_im + sin_im * dif_im + cos_im * dif_re - sin_re * sum_re
            minus_re = cos_re * dif_re + sin_im * two_re - cos_im * two_im + sin_re * dif_im
            minus_im = cos_re * dif_im + sin_im * two_im + cos_im * two_re - sin_re * dif_re
            upper = split(jnp.concatenate([plus_re, minus_im], axis=1))
            lower = split(jnp.concatenate([-plus_im, minus_re], axis=1))
            parts.append([jnp.concatenate([u, w], axis=0) for u, w in zip(upper, lower)])
        table = (inv_ref[0, parity], inv_ref[1, parity])
        back.append([dot3(table, part) for part in parts])

    for upper in range(2):
        ends = []
        for group in range(2):
            even, odd = back[0][group], back[1][group]
            rows = split(even - odd if upper else even + odd)
            ends.append(dot3(rows, (fin_ref[0, group], fin_ref[1, group])))
        where = slice(upper * half, (upper + 1) * half)
        for side, value in enumerate((ends[0] + ends[1], ends[0] - ends[1])):
            for t in range(half // 128):
                img[side * (half // 128) + t, where] = value[:, t * 128 : (t + 1) * 128]

    own = jnp.int32(0)
    for i in range(rank_ref.shape[1]):
        own = own + jnp.where(rank_ref[0, i] == me, i, 0)
    used = counts_ref[own]
    pairs = BLK // 2
    lane = lax.broadcasted_iota(jnp.int32, (pairs, 2 * BLK), 1)
    for m in range(MAXB):
        block = jnp.clip(ids_ref[own, m], 0, NB * NB - 1)
        base = pl.multiple_of((block // NB) * BLK, BLK)
        tile = (block % NB) // 2
        even = img[tile, pl.ds(base, pairs)]
        odd = img[tile, pl.ds(base + pairs, pairs)]
        second = jnp.broadcast_to(block % 2 == 1, lane.shape)
        value = jnp.where(
            lane < BLK,
            jnp.where(second, pltpu.roll(even, BLK, 1), even),
            jnp.where(second, odd, pltpu.roll(odd, BLK, 1)),
        )
        blocks[m * pairs : (m + 1) * pairs] = jnp.where(m < used, value, 0.0)
    for j in range(pairs):
        out_ref[0, :, j * 2 * BLK : (j + 1) * 2 * BLK] = blocks[pl.ds(j, MAXB, stride=pairs), :]


def correlate(owner_rank, block_ids, block_counts, strips, folded, consts):
    detector = folded.shape[2]
    half = detector // 2
    return pl.pallas_call(
        functools.partial(correlate_kernel, len(strips)),
        out_shape=jax.ShapeDtypeStruct((1, MAXB, BLK * BLK), F32),
        in_specs=[pl.BlockSpec(memory_space=SMEM)] * 3
        + [pl.BlockSpec(memory_space=VMEM)] * (len(strips) + 1 + len(consts)),
        out_specs=pl.BlockSpec(memory_space=VMEM),
        scratch_shapes=[
            VMEM((detector, detector), F32),
            VMEM((detector // 128, detector, 128), F32),
            VMEM((MAXB * BLK // 2, 2 * BLK), F32),
        ],
        compiler_params=pltpu.CompilerParams(vmem_limit_bytes=40 << 20),
        name="correlate",
    )(owner_rank, block_ids, block_counts, *strips, folded, *consts)


def swap(value, axis, size, bits):
    return lax.ppermute(value, axis, [(i, i ^ bits) for i in range(size)])


def shards(strip_size, group_size, frames, kernel, owner_rank, block_ids, block_counts):
    detector = frames.shape[2]
    *consts, perm = tables(detector)
    if strip_size == 8 and group_size == 4:
        tie = lax.optimization_barrier
        blocks = list(pack(owner_rank, frames))
        strips = {0: blocks[0]}
        piece = jnp.swapaxes(kernel, 1, 2)
        far = swap(piece, "strip", 8, 4)
        near = swap(piece, "strip", 8, 2)
        both = swap(far, "strip", 8, 2)
        for j in (4, 6, 1):
            strips[j] = swap(blocks[j], "strip", 8, j)
        near, far, both, strips[4], strips[1], blocks[5], blocks[7], blocks[2], blocks[3] = tie((near, far, both, strips[4], strips[1], blocks[5], blocks[7], blocks[2], blocks[3]))
        quad = heap([piece, near, far, both])
        quad_x = swap(quad, "strip", 8, 1)
        quad, strips[6] = tie((quad, strips[6]))
        quad_y = swap(quad, "frames", 4, 2)
        for j in (5, 7, 2, 3):
            strips[j] = swap(blocks[j], "strip", 8, j)
        quad_x, strips[5], strips[2] = tie((quad_x, strips[5], strips[2]))
        quad_xy = swap(quad_x, "frames", 4, 2)
        quads = [quad, quad_x, quad_y, quad_xy]
        *quads, strips[7], strips[3] = tie((*quads, strips[7], strips[3]))
        quads = quads + [swap(q, "frames", 4, 1) for q in quads]
        ordered = [quads[4 * (df % 2) + 2 * (df // 2) + dx] for df in range(4) for dx in range(2)]
        folded = fold(fold_pieces_kernel, ordered, perm, detector)
        strips = [strips[j] for j in range(8)]
    else:
        places = jnp.argsort(owner_rank.reshape(-1))
        strips = [lax.all_to_all(frames[places], "strip", split_axis=0, concat_axis=1, tiled=True)[0]]
        whole = lax.all_gather(kernel, "strip", axis=2, tiled=True)
        whole = lax.all_gather(whole, "frames", axis=1, tiled=True)
        folded = fold(fold_whole_kernel, [jnp.swapaxes(whole, 1, 2)], perm, detector)
    return correlate(owner_rank, block_ids, block_counts, strips, folded, consts)


def solution(mesh):
    return jax.shard_map(
        functools.partial(shards, mesh.shape["strip"], mesh.shape["frames"]),
        mesh=mesh,
        in_specs=(
            P("frames", "strip", None),
            P(None, "frames", "strip"),
            P("frames", None),
            P("frames", None),
            P("frames"),
        ),
        out_specs=P("strip", "frames", None),
        check_vma=False,
    )
```

profile of v0, /device:TPU:0, one launch (start us, length us, event | category | flops | bytes accessed | tf_op | source)
XLA Modules:
  0.0 54.2 jit_solution(8718806045861428216)
XLA Ops:
  0.0 4.0 %collective-permute-start.1 = (f32[2,64,128]{2,1,0:T(8,128)}, f32[2,64,128]{2,1,0:T(8,128)S(1)}, u32[]{:S(2)}, u32[]{:S(2)}) collective-permute-start(f32[2,64,128]{2,1,0:T(8,128)} %bitcast.1), channel_id=1, source_target_pairs={{0,16},{4,20},{8,24},{12,28},{16,0},{20,4},{24,8},{28,12},{1,17},{... | collective-permute-start | bytes 196616 | tf_op jit(solution)/shard_map/ppermute | solution.py:283
  4.0 3.0 %pack.1 = (f32[64,512]{1,0:T(8,128)}, f32[64,512]{1,0:T(8,128)}, f32[64,512]{1,0:T(8,128)}, f32[64,512]{1,0:T(8,128)}, f32[64,512]{1,0:T(8,128)}, /*index=5*/f32...) custom-call(s32[1,8]{1,0:T(1,128)} %refs_0_.1, f32[8,64,512]{2,1,0:T(8,128)} %frames_ref.1), custom_call_target="tpu_custom_call" | custom-call | flops 1024 | bytes 1024 | tf_op jit(solution)/shard_map/pack/pallas_call | solution.py:96
  7.1 1.8 %collective-permute-start.4 = (f32[64,512]{1,0:T(8,128)}, f32[64,512]{1,0:T(8,128)S(1)}, u32[]{:S(2)}, u32[]{:S(2)}) collective-permute-start(f32[64,512]{1,0:T(8,128)} %get-tuple-element.35), channel_id=1, source_target_pairs={{0,4},{4,0},{8,12},{12,8},{16,20},{20,16},{24,28},{28,24},{1,5},{5... | collective-permute-start | bytes 393224 | tf_op jit(solution)/shard_map/ppermute | solution.py:283
  8.9 1.6 %collective-permute-start = (f32[2,64,128]{2,1,0:T(8,128)}, f32[2,64,128]{2,1,0:T(8,128)S(1)}, u32[]{:S(2)}, u32[]{:S(2)}) collective-permute-start(f32[2,64,128]{2,1,0:T(8,128)} %bitcast.2), channel_id=1, source_target_pairs={{0,8},{4,12},{8,0},{12,4},{16,24},{20,28},{24,16},{28,20},{1,9},{5... | collective-permute-start | bytes 196616 | tf_op jit(solution)/shard_map/ppermute | solution.py:283
  10.5 0.5 collective-permute-start.2
  10.9 3.3 %collective-permute-done.refs_1_ = f32[2,64,128]{2,1,0:T(8,128)S(1)} collective-permute-done((f32[2,64,128]{2,1,0:T(8,128)}, f32[2,64,128]{2,1,0:T(8,128)S(1)}, u32[]{:S(2)}, u32[]{:S(2)}) %collective-permute-start) | collective-permute-done | bytes 65568 | tf_op jit(solution)/shard_map/ppermute | solution.py:283
  14.2 1.4 %collective-permute-done.2.refs_3_ = f32[2,64,128]{2,1,0:T(8,128)S(1)} collective-permute-done((f32[2,64,128]{2,1,0:T(8,128)S(1)}, f32[2,64,128]{2,1,0:T(8,128)S(1)}, u32[]{:S(2)}, u32[]{:S(2)}) %collective-permute-start.2) | collective-permute-done | bytes 65568 | tf_op jit(solution)/shard_map/ppermute | solution.py:283
  16.0 0.8 %copy-done.6 = f32[2,128,64]{1,2,0:T(8,128)S(1)} copy-done((f32[2,128,64]{1,2,0:T(8,128)S(1)}, f32[2,128,64]{1,2,0:T(8,128)}, u32[]{:S(2)}) %copy-start.6) | copy-done | bytes 65560
  16.8 1.6 %collective-permute-start.5 = (f32[4,2,64,128]{3,2,1,0:T(8,128)S(1)}, f32[4,2,64,128]{3,2,1,0:T(8,128)S(1)}, u32[]{:S(2)}, u32[]{:S(2)}) collective-permute-start(f32[4,2,64,128]{3,2,1,0:T(8,128)S(1)} %heap.1.refs_0_), channel_id=1, source_target_pairs={{0,4},{4,0},{8,12},{12,8},{16,20},{20,16},{24,28},{28,24},{1,5},{5... | collective-permute-start | bytes 786440 | tf_op jit(solution)/shard_map/ppermute | solution.py:283
  18.5 2.9 %collective-permute-start.8 = (f32[64,512]{1,0:T(8,128)}, f32[64,512]{1,0:T(8,128)S(1)}, u32[]{:S(2)}, u32[]{:S(2)}) collective-permute-start(f32[64,512]{1,0:T(8,128)} %get-tuple-element.47), channel_id=1, source_target_pairs={{0,24},{4,28},{8,16},{12,20},{16,8},{20,12},{24,0},{28,4},{1,25},{... | collective-permute-start | bytes 393224 | tf_op jit(solution)/shard_map/ppermute | solution.py:283
  21.4 1.6 %collective-permute-start.7 = (f32[64,512]{1,0:T(8,128)}, f32[64,512]{1,0:T(8,128)S(1)}, u32[]{:S(2)}, u32[]{:S(2)}) collective-permute-start(f32[64,512]{1,0:T(8,128)} %get-tuple-element.45), channel_id=1, source_target_pairs={{0,8},{4,12},{8,0},{12,4},{16,24},{20,28},{24,16},{28,20},{1,9},{5... | collective-permute-start | bytes 393224 | tf_op jit(solution)/shard_map/ppermute | solution.py:283
  23.0 3.4 %collective-permute-done.8.refs_9_ = f32[64,512]{1,0:T(8,128)S(1)} collective-permute-done((f32[64,512]{1,0:T(8,128)}, f32[64,512]{1,0:T(8,128)S(1)}, u32[]{:S(2)}, u32[]{:S(2)}) %collective-permute-start.8) | collective-permute-done | bytes 131104 | tf_op jit(solution)/shard_map/ppermute | solution.py:283
  26.3 1.4 %collective-permute-start.9 = (f32[4,2,64,128]{3,2,1,0:T(8,128)S(1)}, f32[4,2,64,128]{3,2,1,0:T(8,128)S(1)}, u32[]{:S(2)}, u32[]{:S(2)}) collective-permute-start(f32[4,2,64,128]{3,2,1,0:T(8,128)S(1)} %heap.1.refs_0_), channel_id=1, source_target_pairs={{0,2},{1,3},{2,0},{3,1},{4,6},{5,7},{6,4},{7,5},{8,10},{9,11},{10,... | collective-permute-start | bytes 786440 | tf_op jit(solution)/shard_map/ppermute | solution.py:283
  27.8 4.5 %collective-permute-done.6.refs_8_ = f32[64,512]{1,0:T(8,128)S(1)} collective-permute-done((f32[64,512]{1,0:T(8,128)}, f32[64,512]{1,0:T(8,128)S(1)}, u32[]{:S(2)}, u32[]{:S(2)}) %collective-permute-start.6) | collective-permute-done | bytes 131104 | tf_op jit(solution)/shard_map/ppermute | solution.py:283
  32.3 1.4 %collective-permute-start.10 = (f32[4,2,64,128]{3,2,1,0:T(8,128)S(1)}, f32[4,2,64,128]{3,2,1,0:T(8,128)S(1)}, u32[]{:S(2)}, u32[]{:S(2)}) collective-permute-start(f32[4,2,64,128]{3,2,1,0:T(8,128)S(1)} %collective-permute-done.5.refs_1_), channel_id=1, source_target_pairs={{0,2},{1,3},{2,0},{3,1},{4,6},{5,7},{6,4},{7,5},{8,10},{9,11},{10,... | collective-permute-start | bytes 786440 | tf_op jit(solution)/shard_map/ppermute | solution.py:283
  33.7 3.3 %collective-permute-start.11 = (f32[64,512]{1,0:T(8,128)}, f32[64,512]{1,0:T(8,128)S(1)}, u32[]{:S(2)}, u32[]{:S(2)}) collective-permute-start(f32[64,512]{1,0:T(8,128)} %get-tuple-element.50), channel_id=1, source_target_pairs={{0,28},{4,24},{8,20},{12,16},{16,12},{20,8},{24,4},{28,0},{1,29},{... | collective-permute-start | bytes 393224 | tf_op jit(solution)/shard_map/ppermute | solution.py:283
  37.1 5.6 %collective-permute-done.11.refs_10_ = f32[64,512]{1,0:T(8,128)S(1)} collective-permute-done((f32[64,512]{1,0:T(8,128)}, f32[64,512]{1,0:T(8,128)S(1)}, u32[]{:S(2)}, u32[]{:S(2)}) %collective-permute-start.11) | collective-permute-done | bytes 131104 | tf_op jit(solution)/shard_map/ppermute | solution.py:283
  42.6 1.5 %collective-permute-done.12.refs_6_ = f32[64,512]{1,0:T(8,128)S(1)} collective-permute-done((f32[64,512]{1,0:T(8,128)}, f32[64,512]{1,0:T(8,128)S(1)}, u32[]{:S(2)}, u32[]{:S(2)}) %collective-permute-start.12) | collective-permute-done | bytes 131104 | tf_op jit(solution)/shard_map/ppermute | solution.py:283
  44.1 0.5 collective-permute-start.14
  44.7 0.4 collective-permute-start.16
  45.1 0.5 collective-permute-done.13.refs_2_
  46.7 0.9 %copy-done.4 = bf16[2,256,256]{2,1,0:T(8,128)(2,1)S(1)} copy-done((bf16[2,256,256]{2,1,0:T(8,128)(2,1)S(1)}, bf16[2,256,256]{2,1,0:T(8,128)(2,1)}, u32[]{:S(2)}) %copy-start.4) | copy-done | bytes 262168
  47.7 0.9 %fold.1.refs_11_ = f32[4,2,512,128]{3,2,1,0:T(8,128)S(1)} custom-call(f32[4,2,64,128]{3,2,1,0:T(8,128)S(1)} %heap.1.refs_0_, f32[4,2,64,128]{3,2,1,0:T(8,128)S(1)} %collective-permute-done.5.refs_1_, f32[4,2,64,128]{3,2,1,0:T(8,128)S(1)} %collective-permute-done.13.refs_2_, f32[4,2,64,128]{3,2,1,0:T(8,128)S(1)} %collective-permute-done.14.refs_3_, ...), custom_call_target="tpu_custom_call" | custom-call | flops 1024 | bytes 1024 | tf_op jit(solution)/shard_map/fold/pallas_call | solution.py:166
  48.7 5.5 %correlate.1 = f32[1,16,4096]{2,1,0:T(8,128)} custom-call(s32[1,8]{1,0:T(1,128)S(1)} %copy-done.8, s32[8,16]{1,0:T(8,128)S(1)} %copy-done.7, s32[8]{0:T(128)S(1)} %copy-done.9, f32[64,512]{1,0:T(8,128)S(1)} %copy-done.5, f32[64,512]{1,0:T(8,128)S(1)} %collective-permute-done.4.refs_4_, f32[64,512]{1,0:T(8,128)S(1)} %collective-permute-done.7.refs_5_, ...), custom_call_target="tpu_custom_call" | custom-call | tf_op jit(solution)/shard_map/correlate/pallas_call | solution.py:266
  (34 shorter events, 1.7 us)
Async XLA Ops:
  0.0 10.5 %collective-permute-start.1 = (f32[2,64,128]{2,1,0:T(8,128)}, f32[2,64,128]{2,1,0:T(8,128)S(1)}, u32[]{:S(2)}, u32[]{:S(2)}) collective-permute-start(f32[2,64,128]{2,1,0:T(8,128)} %bitcast.1), channel_id=1, source_target_pairs={{0,16},{4,20},{8,24},{12,28},{16,0},{20,4},{24,8},{28,12},{1,17},{... | collective-permute-start | bytes 196616 | tf_op jit(solution)/shard_map/ppermute | solution.py:283
  7.0 8.9 %collective-permute-start.3 = (f32[64,512]{1,0:T(8,128)}, f32[64,512]{1,0:T(8,128)S(1)}, u32[]{:S(2)}, u32[]{:S(2)}) collective-permute-start(f32[64,512]{1,0:T(8,128)} %get-tuple-element.34), channel_id=1, source_target_pairs={{0,16},{4,20},{8,24},{12,28},{16,0},{20,4},{24,8},{28,12},{1,17},{... | collective-permute-start | bytes 393224 | tf_op jit(solution)/shard_map/ppermute | solution.py:283
  7.1 8.9 %collective-permute-start.4 = (f32[64,512]{1,0:T(8,128)}, f32[64,512]{1,0:T(8,128)S(1)}, u32[]{:S(2)}, u32[]{:S(2)}) collective-permute-start(f32[64,512]{1,0:T(8,128)} %get-tuple-element.35), channel_id=1, source_target_pairs={{0,4},{4,0},{8,12},{12,8},{16,20},{20,16},{24,28},{28,24},{1,5},{5... | collective-permute-start | bytes 393224 | tf_op jit(solution)/shard_map/ppermute | solution.py:283
  8.9 5.3 %collective-permute-start = (f32[2,64,128]{2,1,0:T(8,128)}, f32[2,64,128]{2,1,0:T(8,128)S(1)}, u32[]{:S(2)}, u32[]{:S(2)}) collective-permute-start(f32[2,64,128]{2,1,0:T(8,128)} %bitcast.2), channel_id=1, source_target_pairs={{0,8},{4,12},{8,0},{12,4},{16,24},{20,28},{24,16},{28,20},{1,9},{5... | collective-permute-start | bytes 196616 | tf_op jit(solution)/shard_map/ppermute | solution.py:283
  10.5 5.1 %collective-permute-start.2 = (f32[2,64,128]{2,1,0:T(8,128)S(1)}, f32[2,64,128]{2,1,0:T(8,128)S(1)}, u32[]{:S(2)}, u32[]{:S(2)}) collective-permute-start(f32[2,64,128]{2,1,0:T(8,128)S(1)} %collective-permute-done.1.refs_2_), channel_id=1, source_target_pairs={{0,8},{4,12},{8,0},{12,4},{16,24},{20,28},{24,16},{28,20},{1,9},{5... | collective-permute-start | bytes 196616 | tf_op jit(solution)/shard_map/ppermute | solution.py:283
  16.8 31.8 %copy-start.5 = (f32[64,512]{1,0:T(8,128)S(1)}, f32[64,512]{1,0:T(8,128)}, u32[]{:S(2)}) copy-start(f32[64,512]{1,0:T(8,128)} %get-tuple-element.33.refs_3_) | copy-start | bytes 393220
  16.8 31.8 %copy-start.7 = (s32[8,16]{1,0:T(8,128)S(1)}, s32[8,16]{1,0:T(8,128)}, u32[]{:S(2)}) copy-start(s32[8,16]{1,0:T(8,128)} %refs_1_.1) | copy-start | bytes 1540
  16.8 15.5 %collective-permute-start.5 = (f32[4,2,64,128]{3,2,1,0:T(8,128)S(1)}, f32[4,2,64,128]{3,2,1,0:T(8,128)S(1)}, u32[]{:S(2)}, u32[]{:S(2)}) collective-permute-start(f32[4,2,64,128]{3,2,1,0:T(8,128)S(1)} %heap.1.refs_0_), channel_id=1, source_target_pairs={{0,4},{4,0},{8,12},{12,8},{16,20},{20,16},{24,28},{28,24},{1,5},{5... | collective-permute-start | bytes 786440 | tf_op jit(solution)/shard_map/ppermute | solution.py:283
  18.4 30.2 %copy-start.9 = (s32[8]{0:T(128)S(1)}, s32[8]{0:T(128)}, u32[]{:S(2)}) copy-start(s32[8]{0:T(128)} %refs_2_.1) | copy-start | bytes 100
  18.4 30.2 %copy-start = (bf16[2,2,256,512]{3,2,1,0:T(8,128)(2,1)S(1)}, bf16[2,2,256,512]{3,2,1,0:T(8,128)(2,1)}, u32[]{:S(2)}) copy-start(bf16[2,2,256,512]{3,2,1,0:T(8,128)(2,1)} %constant.13.clone.refs_14_) | copy-start | bytes 3145732
  18.4 30.2 %copy-start.1 = (bf16[2,2,512,256]{3,2,1,0:T(8,128)(2,1)S(1)}, bf16[2,2,512,256]{3,2,1,0:T(8,128)(2,1)}, u32[]{:S(2)}) copy-start(bf16[2,2,512,256]{3,2,1,0:T(8,128)(2,1)} %constant.12.clone.refs_13_) | copy-start | bytes 3145732
  18.5 30.2 %copy-start.2 = (bf16[2,2,256,256]{3,2,1,0:T(8,128)(2,1)S(1)}, bf16[2,2,256,256]{3,2,1,0:T(8,128)(2,1)}, u32[]{:S(2)}) copy-start(bf16[2,2,256,256]{3,2,1,0:T(8,128)(2,1)} %constant.14.clone.refs_15_) | copy-start | bytes 1572868
  18.5 30.2 %copy-start.3 = (bf16[2,2,256,256]{3,2,1,0:T(8,128)(2,1)S(1)}, bf16[2,2,256,256]{3,2,1,0:T(8,128)(2,1)}, u32[]{:S(2)}) copy-start(bf16[2,2,256,256]{3,2,1,0:T(8,128)(2,1)} %constant.11.clone.refs_12_) | copy-start | bytes 1572868
  18.5 7.9 %collective-permute-start.8 = (f32[64,512]{1,0:T(8,128)}, f32[64,512]{1,0:T(8,128)S(1)}, u32[]{:S(2)}, u32[]{:S(2)}) collective-permute-start(f32[64,512]{1,0:T(8,128)} %get-tuple-element.47), channel_id=1, source_target_pairs={{0,24},{4,28},{8,16},{12,20},{16,8},{20,12},{24,0},{28,4},{1,25},{... | collective-permute-start | bytes 393224 | tf_op jit(solution)/shard_map/ppermute | solution.py:283
  21.4 10.9 %collective-permute-start.6 = (f32[64,512]{1,0:T(8,128)}, f32[64,512]{1,0:T(8,128)S(1)}, u32[]{:S(2)}, u32[]{:S(2)}) collective-permute-start(f32[64,512]{1,0:T(8,128)} %get-tuple-element.44), channel_id=1, source_target_pairs={{0,20},{4,16},{8,28},{12,24},{16,4},{20,0},{24,12},{28,8},{1,21},{... | collective-permute-start | bytes 393224 | tf_op jit(solution)/shard_map/ppermute | solution.py:283
  21.4 10.9 %collective-permute-start.7 = (f32[64,512]{1,0:T(8,128)}, f32[64,512]{1,0:T(8,128)S(1)}, u32[]{:S(2)}, u32[]{:S(2)}) collective-permute-start(f32[64,512]{1,0:T(8,128)} %get-tuple-element.45), channel_id=1, source_target_pairs={{0,8},{4,12},{8,0},{12,4},{16,24},{20,28},{24,16},{28,20},{1,9},{5... | collective-permute-start | bytes 393224 | tf_op jit(solution)/shard_map/ppermute | solution.py:283
  26.3 17.7 %collective-permute-start.9 = (f32[4,2,64,128]{3,2,1,0:T(8,128)S(1)}, f32[4,2,64,128]{3,2,1,0:T(8,128)S(1)}, u32[]{:S(2)}, u32[]{:S(2)}) collective-permute-start(f32[4,2,64,128]{3,2,1,0:T(8,128)S(1)} %heap.1.refs_0_), channel_id=1, source_target_pairs={{0,2},{1,3},{2,0},{3,1},{4,6},{5,7},{6,4},{7,5},{8,10},{9,11},{10,... | collective-permute-start | bytes 786440 | tf_op jit(solution)/shard_map/ppermute | solution.py:283
  32.3 11.8 %collective-permute-start.10 = (f32[4,2,64,128]{3,2,1,0:T(8,128)S(1)}, f32[4,2,64,128]{3,2,1,0:T(8,128)S(1)}, u32[]{:S(2)}, u32[]{:S(2)}) collective-permute-start(f32[4,2,64,128]{3,2,1,0:T(8,128)S(1)} %collective-permute-done.5.refs_1_), channel_id=1, source_target_pairs={{0,2},{1,3},{2,0},{3,1},{4,6},{5,7},{6,4},{7,5},{8,10},{9,11},{10,... | collective-permute-start | bytes 786440 | tf_op jit(solution)/shard_map/ppermute | solution.py:283
  33.7 8.9 %collective-permute-start.11 = (f32[64,512]{1,0:T(8,128)}, f32[64,512]{1,0:T(8,128)S(1)}, u32[]{:S(2)}, u32[]{:S(2)}) collective-permute-start(f32[64,512]{1,0:T(8,128)} %get-tuple-element.50), channel_id=1, source_target_pairs={{0,28},{4,24},{8,20},{12,16},{16,12},{20,8},{24,4},{28,0},{1,29},{... | collective-permute-start | bytes 393224 | tf_op jit(solution)/shard_map/ppermute | solution.py:283
  37.0 7.0 %collective-permute-start.12 = (f32[64,512]{1,0:T(8,128)}, f32[64,512]{1,0:T(8,128)S(1)}, u32[]{:S(2)}, u32[]{:S(2)}) collective-permute-start(f32[64,512]{1,0:T(8,128)} %get-tuple-element.51), channel_id=1, source_target_pairs={{0,12},{4,8},{8,4},{12,0},{16,28},{20,24},{24,20},{28,16},{1,13},{... | collective-permute-start | bytes 393224 | tf_op jit(solution)/shard_map/ppermute | solution.py:283
  44.1 1.5 %collective-permute-start.13 = (f32[4,2,64,128]{3,2,1,0:T(8,128)S(1)}, f32[4,2,64,128]{3,2,1,0:T(8,128)S(1)}, u32[]{:S(2)}, u32[]{:S(2)}) collective-permute-start(f32[4,2,64,128]{3,2,1,0:T(8,128)S(1)} %heap.1.refs_0_), channel_id=1, source_target_pairs={{0,1},{1,0},{2,3},{3,2},{4,5},{5,4},{6,7},{7,6},{8,9},{9,8},{10,11... | collective-permute-start | bytes 786440 | tf_op jit(solution)/shard_map/ppermute | solution.py:283
  44.1 1.9 %collective-permute-start.14 = (f32[4,2,64,128]{3,2,1,0:T(8,128)S(1)}, f32[4,2,64,128]{3,2,1,0:T(8,128)S(1)}, u32[]{:S(2)}, u32[]{:S(2)}) collective-permute-start(f32[4,2,64,128]{3,2,1,0:T(8,128)S(1)} %collective-permute-done.5.refs_1_), channel_id=1, source_target_pairs={{0,1},{1,0},{2,3},{3,2},{4,5},{5,4},{6,7},{7,6},{8,9},{9,8},{10,11... | collective-permute-start | bytes 786440 | tf_op jit(solution)/shard_map/ppermute | solution.py:283
  44.6 1.8 %collective-permute-start.15 = (f32[4,2,64,128]{3,2,1,0:T(8,128)S(1)}, f32[4,2,64,128]{3,2,1,0:T(8,128)S(1)}, u32[]{:S(2)}, u32[]{:S(2)}) collective-permute-start(f32[4,2,64,128]{3,2,1,0:T(8,128)S(1)} %collective-permute-done.9.refs_4_), channel_id=1, source_target_pairs={{0,1},{1,0},{2,3},{3,2},{4,5},{5,4},{6,7},{7,6},{8,9},{9,8},{10,11... | collective-permute-start | bytes 786440 | tf_op jit(solution)/shard_map/ppermute | solution.py:283
  44.7 2.1 %collective-permute-start.16 = (f32[4,2,64,128]{3,2,1,0:T(8,128)S(1)}, f32[4,2,64,128]{3,2,1,0:T(8,128)S(1)}, u32[]{:S(2)}, u32[]{:S(2)}) collective-permute-start(f32[4,2,64,128]{3,2,1,0:T(8,128)S(1)} %collective-permute-done.10.refs_5_), channel_id=1, source_target_pairs={{0,1},{1,0},{2,3},{3,2},{4,5},{5,4},{6,7},{7,6},{8,9},{9,8},{10,11... | collective-permute-start | bytes 786440 | tf_op jit(solution)/shard_map/ppermute | solution.py:283
  (3 other events, 32.0 us)
where the time goes:
time: 54.4 us; the launch traced here: 54.2 us
  waiting for transfers between devices  21.6 us (40%)
  starting transfers between devices  21.2 us (39%)
  Pallas kernels  9.4 us (17%)
  local copies, waits for them, and re-layouts  1.83 us (3%)
    ppermute x17, waiting for transfers between devices, swap(): return lax.ppermute(value, axis, [(i, i ^ bits) for i in range(size)])  21.6 us
    ppermute x17, starting transfers between devices, swap(): return lax.ppermute(value, axis, [(i, i ^ bits) for i in range(size)])  21.2 us
    pallas_call x1, Pallas kernels, correlate(): pl.pallas_call(functools.partial(correlate_kernel, len(strips)), out_shap...  5.48 us
    pallas_call x1, Pallas kernels, pack(): pl.pallas_call(functools.partial(pack_kernel, count), out_shape=[jax.Shap...  2.98 us
    unnamed x20, local copies, waits for them, and re-layouts  1.83 us
  transfers between devices with their start and end apart: 17, of which 11 were waited for; matrix products, arithmetic and copies ran while one was open for 0% of the time, Pallas kernels for 5%

commit v1 on v0

--- a/solution.py
+++ b/solution.py
@@ -15,8 +15,15 @@
 VMEM = pltpu.VMEM
 SMEM = pltpu.SMEM
 BF16 = jnp.bfloat16
-HEAPCOST = 1024
-PACKCOST = 1024
+XLAST = False
+ZDIRECT = 0
+HEAPCOST = 500000000
+PACKCOST = 2000000000
+FOLDCOST = 3000000000
+EDGES = [['ky', 'f5'], ['heap', 'r0'], ['kx', 'kc0'], ['pack', 'kc1']]
+COSTS = [4000000000, 6000000000, 2000000000, 1500000000]
+OPS = [('pack', []), ('far', []), ('near', []), ('both', ['far']), ('heap', ['near', 'far', 'both']), ('kx', ['heap']), ('ky', ['heap']), ('kxy', ['kx']), ('kc0', ['heap']), ('kc1', ['kx']), ('kc2', ['ky']), ('kc3', ['kxy']), ('f1', ['pack']), ('f2', ['pack']), ('f3', ['pack']), ('f4', ['pack']), ('f5', ['pack']), ('f6', ['pack']), ('f7', ['pack']), ('r0', ['pack', 'f4']), ('r1', ['f1', 'f5']), ('r2', ['f2', 'f6']), ('r3', ['f3', 'f7'])]
+ROWCOST = 1024
 F32 = jnp.float32
 
 
@@ -76,30 +83,22 @@
     return dot(left[0], right[0]) + dot(left[1], right[0]) + dot(left[0], right[1])
 
 
-def pack_kernel(count, rank_ref, frames_ref, *rest):
-    outs, sems = rest[:count], rest[count]
+def pack_kernel(rank_ref, frames_ref, *outs):
     me = lax.axis_index("strip")
-    copies = []
-    for j in range(count):
-        target = me ^ j
-        source = jnp.int32(0)
-        for i in range(count):
-            source = source + jnp.where(rank_ref[0, i] == target, i, 0)
-        copies.append(pltpu.make_async_copy(frames_ref.at[source], outs[j], sems.at[j]))
-        copies[-1].start()
-    for copy in copies:
-        copy.wait()
+    ranks = rank_ref[...]
+    places = lax.broadcasted_iota(jnp.int32, ranks.shape, 1)
+    for j, out in enumerate(outs):
+        out[...] = frames_ref[jnp.sum(jnp.where(ranks == (me ^ j), places, 0))]
 
 
 def pack(owner_rank, frames):
     count, rows, detector = frames.shape
     return pl.pallas_call(
-        functools.partial(pack_kernel, count),
+        pack_kernel,
         out_shape=[jax.ShapeDtypeStruct((rows, detector), F32)] * count,
-        in_specs=[pl.BlockSpec(memory_space=SMEM), pl.BlockSpec(memory_space=pl.ANY)],
+        in_specs=[pl.BlockSpec(memory_space=VMEM)] * 2,
         out_specs=[pl.BlockSpec(memory_space=VMEM)] * count,
-        scratch_shapes=[pltpu.SemaphoreType.DMA((count,))],
-        compiler_params=pltpu.CompilerParams(vmem_limit_bytes=60 << 20),
+        compiler_params=pltpu.CompilerParams(vmem_limit_bytes=16 << 20),
         cost_estimate=pl.CostEstimate(flops=PACKCOST, bytes_accessed=1024, transcendentals=0),
         name="pack",
     )(owner_rank, frames)
@@ -170,43 +169,64 @@
         out_specs=pl.BlockSpec(memory_space=VMEM),
         scratch_shapes=[VMEM((2, detector // 128, detector, 128), F32)],
         compiler_params=pltpu.CompilerParams(vmem_limit_bytes=32 << 20),
-        cost_estimate=pl.CostEstimate(flops=1024, bytes_accessed=1024, transcendentals=0),
+        cost_estimate=pl.CostEstimate(flops=FOLDCOST, bytes_accessed=1024, transcendentals=0),
         name="fold",
     )(*args, perm)
 
 
+def rows_kernel(split_strip, lower_ref, upper_ref, row_ref, *rest):
+    out_ref = rest[-1]
+    rows, half = lower_ref.shape[0], lower_ref.shape[1] // 2
+    one, two = lower_ref[...], upper_ref[...]
+    diff = one - two
+    if split_strip:
+        diff = jnp.where(lax.axis_index("strip") >= split_strip, -diff, diff)
+    both = jnp.concatenate([one + two, diff], axis=0)
+    left, right = both[:, 0:half], both[:, half:]
+    for group, value in enumerate((left + right, left - right)):
+        parts = split(dot3(split(value), (row_ref[0, group], row_ref[1, group])))
+        for i, part in enumerate(parts):
+            for parity in range(2):
+                out_ref[i, parity, :, group * half : (group + 1) * half] = part[parity * rows : (parity + 1) * rows]
+
+
+def row_spectra(lower, upper, table, split_strip, flops, before=()):
+    rows, detector = lower.shape
+    return pl.pallas_call(
+        functools.partial(rows_kernel, split_strip),
+        out_shape=jax.ShapeDtypeStruct((2, 2, rows, detector), BF16),
+        in_specs=[pl.BlockSpec(memory_space=VMEM)] * 3 + [pl.BlockSpec(memory_space=pl.ANY)] * len(before),
+        out_specs=pl.BlockSpec(memory_space=VMEM),
+        compiler_params=pltpu.CompilerParams(vmem_limit_bytes=16 << 20),
+        cost_estimate=pl.CostEstimate(flops=flops, bytes_accessed=1024, transcendentals=0),
+        name="rows",
+    )(lower, upper, table, *before)
+
+
 def correlate_kernel(pieces, *refs):
-    rank_ref, ids_ref, counts_ref = refs[:3]
-    strips = refs[3 : 3 + pieces]
-    fold_ref, row_ref, col_ref, inv_ref, fin_ref, out_ref, sums, img, blocks = refs[3 + pieces :]
+    lists = refs[:3]
+    spectra = refs[3 : 3 + pieces]
+    fold_ref, col_ref, inv_ref, fin_ref, out_ref, spec, img, blocks, *scalars = refs[3 + pieces :]
+    *scalars, sems = scalars
+    copies = [pltpu.make_async_copy(x, y, sems.at[i]) for i, (x, y) in enumerate(zip(lists, scalars))]
+    for copy in copies:
+        copy.start()
     detector = fold_ref.shape[2]
     half, quarter = detector // 2, detector // 4
     me = lax.axis_index("strip")
-
-    if pieces == 1:
-        sums[0:half] = strips[0][0:half] + strips[0][half:]
-        sums[half:] = strips[0][0:half] - strips[0][half:]
-    else:
-        rows = detector // pieces
-        sign = jnp.where(me >= pieces // 2, -1.0, 1.0).astype(F32)
-        for j in range(pieces // 2):
-            base = pl.multiple_of(((me ^ j) % (pieces // 2)) * rows, rows)
-            one, two = strips[j][...], strips[j + pieces // 2][...]
-            sums[pl.ds(base, rows)] = one + two
-            sums[pl.ds(base + half, rows)] = (one - two) * sign
-
-    left, right = sums[:, 0:half], sums[:, half:]
-    spec_even = split(dot3(split(left + right), (row_ref[0, 0], row_ref[1, 0])))
-    spec_odd = split(dot3(split(left - right), (row_ref[0, 1], row_ref[1, 1])))
+    rows = half // pieces
+    for j in range(pieces):
+        base = pl.multiple_of(((me ^ j) % pieces) * rows, rows)
+        spec[:, :, pl.ds(base, rows)] = spectra[j][...]
 
     lane = lax.broadcasted_iota(jnp.int32, (half, quarter), 1)
     back = []
     for parity in range(2):
         table = (col_ref[0, parity], col_ref[1, parity])
-        where = slice(parity * half, (parity + 1) * half)
         parts = []
-        for group, spec in enumerate((spec_even, spec_odd)):
-            both = dot3(table, (spec[0][where], spec[1][where]))
+        for group in range(2):
+            lanes = slice(group * half, (group + 1) * half)
+            both = dot3(table, (spec[0, parity, :, lanes], spec[1, parity, :, lanes]))
             cos_re, cos_im = both[0:half, 0:quarter], both[0:half, quarter:]
             sin_re, sin_im = both[half:, 0:quarter], both[half:, quarter:]
             freqs = pl.ds(parity, half, stride=2)
@@ -237,6 +257,9 @@
             for t in range(half // 128):
                 img[side * (half // 128) + t, where] = value[:, t * 128 : (t + 1) * 128]
 
+    for copy in copies:
+        copy.wait()
+    rank_ref, ids_ref, counts_ref = scalars
     own = jnp.int32(0)
     for i in range(rank_ref.shape[1]):
         own = own + jnp.where(rank_ref[0, i] == me, i, 0)
@@ -260,23 +283,26 @@
         out_ref[0, :, j * 2 * BLK : (j + 1) * 2 * BLK] = blocks[pl.ds(j, MAXB, stride=pairs), :]
 
 
-def correlate(owner_rank, block_ids, block_counts, strips, folded, consts):
+def correlate(owner_rank, block_ids, block_counts, spectra, folded, consts):
     detector = folded.shape[2]
-    half = detector // 2
-    return pl.pallas_call(
-        functools.partial(correlate_kernel, len(strips)),
+    return pl.pallas_call(
+        functools.partial(correlate_kernel, len(spectra)),
         out_shape=jax.ShapeDtypeStruct((1, MAXB, BLK * BLK), F32),
-        in_specs=[pl.BlockSpec(memory_space=SMEM)] * 3
-        + [pl.BlockSpec(memory_space=VMEM)] * (len(strips) + 1 + len(consts)),
+        in_specs=[pl.BlockSpec(memory_space=pl.ANY)] * 3
+        + [pl.BlockSpec(memory_space=VMEM)] * (len(spectra) + 1 + len(consts)),
         out_specs=pl.BlockSpec(memory_space=VMEM),
         scratch_shapes=[
-            VMEM((detector, detector), F32),
+            VMEM((2, 2, detector // 2, detector), BF16),
             VMEM((detector // 128, detector, 128), F32),
             VMEM((MAXB * BLK // 2, 2 * BLK), F32),
+            SMEM(owner_rank.shape, jnp.int32),
+            SMEM(block_ids.shape, jnp.int32),
+            SMEM(block_counts.shape, jnp.int32),
+            pltpu.SemaphoreType.DMA((3,)),
         ],
         compiler_params=pltpu.CompilerParams(vmem_limit_bytes=40 << 20),
         name="correlate",
-    )(owner_rank, block_ids, block_counts, *strips, folded, *consts)
+    )(owner_rank, block_ids, block_counts, *spectra, folded, *consts)
 
 
 def swap(value, axis, size, bits):
@@ -285,39 +311,62 @@
 
 def shards(strip_size, group_size, frames, kernel, owner_rank, block_ids, block_counts):
     detector = frames.shape[2]
-    *consts, perm = tables(detector)
+    row_table, *consts, perm = tables(detector)
     if strip_size == 8 and group_size == 4:
-        tie = lax.optimization_barrier
-        blocks = list(pack(owner_rank, frames))
-        strips = {0: blocks[0]}
         piece = jnp.swapaxes(kernel, 1, 2)
-        far = swap(piece, "strip", 8, 4)
-        near = swap(piece, "strip", 8, 2)
-        both = swap(far, "strip", 8, 2)
-        for j in (4, 6, 1):
-            strips[j] = swap(blocks[j], "strip", 8, j)
-        near, far, both, strips[4], strips[1], blocks[5], blocks[7], blocks[2], blocks[3] = tie((near, far, both, strips[4], strips[1], blocks[5], blocks[7], blocks[2], blocks[3]))
-        quad = heap([piece, near, far, both])
-        quad_x = swap(quad, "strip", 8, 1)
-        quad, strips[6] = tie((quad, strips[6]))
-        quad_y = swap(quad, "frames", 4, 2)
-        for j in (5, 7, 2, 3):
-            strips[j] = swap(blocks[j], "strip", 8, j)
-        quad_x, strips[5], strips[2] = tie((quad_x, strips[5], strips[2]))
-        quad_xy = swap(quad_x, "frames", 4, 2)
-        quads = [quad, quad_x, quad_y, quad_xy]
-        *quads, strips[7], strips[3] = tie((*quads, strips[7], strips[3]))
-        quads = quads + [swap(q, "frames", 4, 1) for q in quads]
+        needs = dict(OPS)
+        val, order = {}, []
+
+        def visit(name):
+            if name in val:
+                return
+            deps = needs[name] + [a for a, b in EDGES if b == name]
+            for d in deps:
+                visit(d)
+
+            def tied(value):
+                extra = [val[a] for a, b in EDGES if b == name]
+                return lax.optimization_barrier((value, extra))[0] if extra else value
+
+            natural = [val[d] for d in needs[name]]
+            if name == "pack":
+                val[name] = pack(tied(owner_rank), frames)
+            elif name == "far":
+                val[name] = swap(tied(piece), "strip", 8, 4)
+            elif name == "near":
+                val[name] = swap(tied(piece), "strip", 8, 2)
+            elif name == "both":
+                val[name] = swap(tied(natural[0] if natural else piece), "strip", 8, {0: 2, 1: 6, 2: 4}[ZDIRECT])
+            elif name == "heap":
+                val[name] = heap([piece] + tied(natural))
+            elif name in ("kx", "kxy") and not (name == "kxy" and not XLAST):
+                val[name] = swap(tied(natural[0]), "strip", 8, 1)
+            elif name in ("ky", "kxy"):
+                val[name] = swap(tied(natural[0]), "frames", 4, 2)
+            elif name[:2] == "kc":
+                val[name] = swap(tied(natural[0]), "frames", 4, 1)
+            elif name[0] == "f":
+                val[name] = swap(tied(natural[0][int(name[1])]), "strip", 8, int(name[1]))
+            elif name[0] == "r":
+                j = int(name[1])
+                low = natural[0][0] if j == 0 else natural[0]
+                low, high = tied((low, natural[-1]))
+                val[name] = row_spectra(low, high, row_table, 4, COSTS[j])
+
+        for name in needs:
+            visit(name)
+        quads = [val["heap"], val["kx"], val["ky"], val["kxy"]] + [val["kc%d" % i] for i in range(4)]
         ordered = [quads[4 * (df % 2) + 2 * (df // 2) + dx] for df in range(4) for dx in range(2)]
         folded = fold(fold_pieces_kernel, ordered, perm, detector)
-        strips = [strips[j] for j in range(8)]
+        spectra = [val["r%d" % j] for j in range(4)]
     else:
         places = jnp.argsort(owner_rank.reshape(-1))
-        strips = [lax.all_to_all(frames[places], "strip", split_axis=0, concat_axis=1, tiled=True)[0]]
+        frame = lax.all_to_all(frames[places], "strip", split_axis=0, concat_axis=1, tiled=True)[0]
         whole = lax.all_gather(kernel, "strip", axis=2, tiled=True)
         whole = lax.all_gather(whole, "frames", axis=1, tiled=True)
         folded = fold(fold_whole_kernel, [jnp.swapaxes(whole, 1, 2)], perm, detector)
-    return correlate(owner_rank, block_ids, block_counts, strips, folded, consts)
+        spectra = [row_spectra(frame[: detector // 2], frame[detector // 2 :], row_table, 0, ROWCOST)]
+    return correlate(owner_rank, block_ids, block_counts, spectra, folded, consts)
 
 
 def solution(mesh):

time: 54.4 us -> 44.2 us (0.81)
  the two profiles are of different devices: /device:TPU:0 before, /device:TPU:26 now
where the time goes in v1:
time: 44.2 us; the launch traced here: 44 us
  waiting for transfers between devices  23.2 us (52%)
  starting transfers between devices  11.2 us (25%)
  Pallas kernels  6.78 us (15%)
  local copies, waits for them, and re-layouts  2.54 us (6%)
    ppermute x17, waiting for transfers between devices, swap(): return lax.ppermute(value, axis, [(i, i ^ bits) for i in range(size)])  23.2 us
    ppermute x17, starting transfers between devices, swap(): return lax.ppermute(value, axis, [(i, i ^ bits) for i in range(size)])  11.2 us
    pallas_call x1, Pallas kernels, correlate(): pl.pallas_call(functools.partial(correlate_kernel, len(spectra)), out_sha...  4.49 us
    unnamed x22, local copies, waits for them, and re-layouts  2.54 us
    pallas_call x4, Pallas kernels, row_spectra(): pl.pallas_call(functools.partial(rows_kernel, split_strip), out_shape=jax...  1.15 us
    pallas_call x1, Pallas kernels, fold(): pl.pallas_call(body, out_shape=jax.ShapeDtypeStruct((4, 2, detector, dete...  0.93 us
  transfers between devices with their start and end apart: 17, of which 7 were waited for; matrix products, arithmetic and copies ran while one was open for 0% of the time, Pallas kernels for 3%

profile of v1, /device:TPU:26, one launch (start us, length us, event | category | flops | bytes accessed | tf_op | source)
XLA Modules:
  0.0 44.0 jit_solution(10979804811397604900)
XLA Ops:
  0.0 0.3 collective-permute-start.2
  0.3 0.7 %copy-done.4 = s32[1,8]{1,0:T(1,128)S(1)} copy-done((s32[1,8]{1,0:T(1,128)S(1)}, s32[1,8]{1,0:T(1,128)}, u32[]{:S(2)}) %copy-start.4) | copy-done | bytes 56
  1.0 1.2 %copy-done.7 = f32[8,64,512]{2,1,0:T(8,128)S(1)} copy-done((f32[8,64,512]{2,1,0:T(8,128)S(1)}, f32[8,64,512]{2,1,0:T(8,128)}, u32[]{:S(2)}) %copy-start.7) | copy-done | bytes 1048600
  2.4 2.7 %collective-permute-start = (f32[64,512]{1,0:T(8,128)S(1)}, f32[64,512]{1,0:T(8,128)S(1)}, u32[]{:S(2)}, u32[]{:S(2)}) collective-permute-start(f32[64,512]{1,0:T(8,128)S(1)} %get-tuple-element.19), channel_id=1, source_target_pairs={{0,16},{4,20},{8,24},{12,28},{16,0},{20,4},{24,8},{28,12},{1,17},{... | collective-permute-start | bytes 393224 | tf_op jit(solution)/shard_map/ppermute | solution.py:309
  5.1 0.4 %collective-permute-start.1 = (f32[2,64,128]{2,1,0:T(8,128)S(1)}, f32[2,64,128]{2,1,0:T(8,128)S(1)}, u32[]{:S(2)}, u32[]{:S(2)}) collective-permute-start(f32[2,64,128]{2,1,0:T(8,128)S(1)} %bitcast.2), channel_id=1, source_target_pairs={{0,8},{4,12},{8,0},{12,4},{16,24},{20,28},{24,16},{28,20},{1,9},{5... | collective-permute-start | bytes 196616 | tf_op jit(solution)/shard_map/ppermute | solution.py:309
  5.5 4.0 %collective-permute-done.2.refs_2_ = f32[2,64,128]{2,1,0:T(8,128)S(1)} collective-permute-done((f32[2,64,128]{2,1,0:T(8,128)}, f32[2,64,128]{2,1,0:T(8,128)S(1)}, u32[]{:S(2)}, u32[]{:S(2)}) %collective-permute-start.2) | collective-permute-done | bytes 65568 | tf_op jit(solution)/shard_map/ppermute | solution.py:309
  9.5 0.5 %collective-permute-start.4 = (f32[64,512]{1,0:T(8,128)S(1)}, f32[64,512]{1,0:T(8,128)S(1)}, u32[]{:S(2)}, u32[]{:S(2)}) collective-permute-start(f32[64,512]{1,0:T(8,128)S(1)} %get-tuple-element.22), channel_id=1, source_target_pairs={{0,4},{4,0},{8,12},{12,8},{16,20},{20,16},{24,28},{28,24},{1,5},{5... | collective-permute-start | bytes 393224 | tf_op jit(solution)/shard_map/ppermute | solution.py:309
  10.1 2.0 %collective-permute-start.7 = (f32[64,512]{1,0:T(8,128)S(1)}, f32[64,512]{1,0:T(8,128)S(1)}, u32[]{:S(2)}, u32[]{:S(2)}) collective-permute-start(f32[64,512]{1,0:T(8,128)S(1)} %get-tuple-element.25), channel_id=1, source_target_pairs={{0,8},{4,12},{8,0},{12,4},{16,24},{20,28},{24,16},{28,20},{1,9},{5... | collective-permute-start | bytes 393224 | tf_op jit(solution)/shard_map/ppermute | solution.py:309
  12.1 0.4 collective-permute-done.1.refs_1_
  12.5 3.4 %collective-permute-done.3.refs_3_ = f32[2,64,128]{2,1,0:T(8,128)S(1)} collective-permute-done((f32[2,64,128]{2,1,0:T(8,128)S(1)}, f32[2,64,128]{2,1,0:T(8,128)S(1)}, u32[]{:S(2)}, u32[]{:S(2)}) %collective-permute-start.3) | collective-permute-done | bytes 65568 | tf_op jit(solution)/shard_map/ppermute | solution.py:309
  16.1 1.6 %collective-permute-start.5 = (f32[4,2,64,128]{3,2,1,0:T(8,128)S(1)}, f32[4,2,64,128]{3,2,1,0:T(8,128)S(1)}, u32[]{:S(2)}, u32[]{:S(2)}) collective-permute-start(f32[4,2,64,128]{3,2,1,0:T(8,128)S(1)} %heap.1.refs_0_), channel_id=1, source_target_pairs={{0,2},{1,3},{2,0},{3,1},{4,6},{5,7},{6,4},{7,5},{8,10},{9,11},{10,... | collective-permute-start | bytes 786440 | tf_op jit(solution)/shard_map/ppermute | solution.py:309
  17.7 0.3 rows.4.refs_3_
  18.0 0.4 collective-permute-start.9
  18.4 1.4 %collective-permute-done.8.upper_ref = f32[64,512]{1,0:T(8,128)S(1)} collective-permute-done((f32[64,512]{1,0:T(8,128)S(1)}, f32[64,512]{1,0:T(8,128)S(1)}, u32[]{:S(2)}, u32[]{:S(2)}) %collective-permute-start.8) | collective-permute-done | bytes 131104 | tf_op jit(solution)/shard_map/ppermute | solution.py:309
  19.8 1.5 %collective-permute-start.10 = (f32[64,512]{1,0:T(8,128)S(1)}, f32[64,512]{1,0:T(8,128)S(1)}, u32[]{:S(2)}, u32[]{:S(2)}) collective-permute-start(f32[64,512]{1,0:T(8,128)S(1)} %get-tuple-element.28), channel_id=1, source_target_pairs={{0,28},{4,24},{8,20},{12,16},{16,12},{20,8},{24,4},{28,0},{1,29},{... | collective-permute-start | bytes 393224 | tf_op jit(solution)/shard_map/ppermute | solution.py:309
  21.3 8.1 %collective-permute-done.11.refs_1_ = f32[4,2,64,128]{3,2,1,0:T(8,128)S(1)} collective-permute-done((f32[4,2,64,128]{3,2,1,0:T(8,128)S(1)}, f32[4,2,64,128]{3,2,1,0:T(8,128)S(1)}, u32[]{:S(2)}, u32[]{:S(2)}) %collective-permute-start.11) | collective-permute-done | bytes 262176 | tf_op jit(solution)/shard_map/ppermute | solution.py:309
  29.5 0.9 %collective-permute-start.14 = (f32[4,2,64,128]{3,2,1,0:T(8,128)S(1)}, f32[4,2,64,128]{3,2,1,0:T(8,128)S(1)}, u32[]{:S(2)}, u32[]{:S(2)}) collective-permute-start(f32[4,2,64,128]{3,2,1,0:T(8,128)S(1)} %collective-permute-done.11.refs_1_), channel_id=1, source_target_pairs={{0,2},{1,3},{2,0},{3,1},{4,6},{5,7},{6,4},{7,5},{8,10},{9,11},{10,... | collective-permute-start | bytes 786440 | tf_op jit(solution)/shard_map/ppermute | solution.py:309
  30.8 0.3 rows.7.refs_6_
  31.2 0.5 %collective-permute-start.13 = (f32[4,2,64,128]{3,2,1,0:T(8,128)S(1)}, f32[4,2,64,128]{3,2,1,0:T(8,128)S(1)}, u32[]{:S(2)}, u32[]{:S(2)}) collective-permute-start(f32[4,2,64,128]{3,2,1,0:T(8,128)S(1)} %collective-permute-done.11.refs_1_), channel_id=1, source_target_pairs={{0,1},{1,0},{2,3},{3,2},{4,5},{5,4},{6,7},{7,6},{8,9},{9,8},{10,11... | collective-permute-start | bytes 786440 | tf_op jit(solution)/shard_map/ppermute | solution.py:309
  31.7 4.1 %collective-permute-done.14.refs_5_ = f32[4,2,64,128]{3,2,1,0:T(8,128)S(1)} collective-permute-done((f32[4,2,64,128]{3,2,1,0:T(8,128)S(1)}, f32[4,2,64,128]{3,2,1,0:T(8,128)S(1)}, u32[]{:S(2)}, u32[]{:S(2)}) %collective-permute-start.14) | collective-permute-done | bytes 262176 | tf_op jit(solution)/shard_map/ppermute | solution.py:309
  35.8 1.7 %collective-permute-done.6.upper_ref = f32[64,512]{1,0:T(8,128)S(1)} collective-permute-done((f32[64,512]{1,0:T(8,128)S(1)}, f32[64,512]{1,0:T(8,128)S(1)}, u32[]{:S(2)}, u32[]{:S(2)}) %collective-permute-start.6) | collective-permute-done | bytes 131104 | tf_op jit(solution)/shard_map/ppermute | solution.py:309
  37.9 0.9 %fold.1.refs_7_ = f32[4,2,512,128]{3,2,1,0:T(8,128)S(1)} custom-call(f32[4,2,64,128]{3,2,1,0:T(8,128)S(1)} %heap.1.refs_0_, f32[4,2,64,128]{3,2,1,0:T(8,128)S(1)} %collective-permute-done.11.refs_1_, f32[4,2,64,128]{3,2,1,0:T(8,128)S(1)} %collective-permute-done.12.refs_2_, f32[4,2,64,128]{3,2,1,0:T(8,128)S(1)} %collective-permute-done.13.refs_3_, ...), custom_call_target="tpu_custom_call" | custom-call | flops 3000000000 | bytes 1024 | tf_op jit(solution)/shard_map/fold/pallas_call | solution.py:165
  39.0 0.3 copy-done.1
  39.5 4.5 %correlate.1 = f32[1,16,4096]{2,1,0:T(8,128)} custom-call(s32[1,8]{1,0:T(1,128)S(1)} %copy-done.5, s32[8,16]{1,0:T(8,128)S(1)} %copy-done.3, s32[8]{0:T(128)S(1)} %copy-done.6, bf16[2,2,64,512]{3,2,1,0:T(8,128)(2,1)S(1)} %rows.4.refs_3_, bf16[2,2,64,512]{3,2,1,0:T(8,128)(2,1)S(1)} %rows.5.refs_4_, bf16[2,2,64,512]{3,2,1,0:T(8,128)(2,1)S(1)} %rows.6.refs_5_, ...), custom_call_target="tpu_custom_call" | custom-call | tf_op jit(solution)/shard_map/correlate/pallas_call | solution.py:288
  (40 shorter events, 1.5 us)
Async XLA Ops:
  0.0 9.5 %collective-permute-start.2 = (f32[2,64,128]{2,1,0:T(8,128)}, f32[2,64,128]{2,1,0:T(8,128)S(1)}, u32[]{:S(2)}, u32[]{:S(2)}) collective-permute-start(f32[2,64,128]{2,1,0:T(8,128)} %bitcast.1), channel_id=1, source_target_pairs={{0,16},{4,20},{8,24},{12,28},{16,0},{20,4},{24,8},{28,12},{1,17},{... | collective-permute-start | bytes 196616 | tf_op jit(solution)/shard_map/ppermute | solution.py:309
  2.2 2.9 %copy-start.8 = (f32[2,128,64]{1,2,0:T(8,128)S(1)}, f32[2,128,64]{1,2,0:T(8,128)}, u32[]{:S(2)}) copy-start(f32[2,128,64]{1,2,0:T(8,128)} %param.11) | copy-start | bytes 196612
  2.2 15.5 %copy-start.9 = (bf16[2,2,256,256]{3,2,1,0:T(8,128)(2,1)S(1)}, bf16[2,2,256,256]{3,2,1,0:T(8,128)(2,1)}, u32[]{:S(2)}) copy-start(bf16[2,2,256,256]{3,2,1,0:T(8,128)(2,1)} %constant.10.clone.row_ref) | copy-start | bytes 1572868
  2.4 13.7 %collective-permute-start = (f32[64,512]{1,0:T(8,128)S(1)}, f32[64,512]{1,0:T(8,128)S(1)}, u32[]{:S(2)}, u32[]{:S(2)}) collective-permute-start(f32[64,512]{1,0:T(8,128)S(1)} %get-tuple-element.19), channel_id=1, source_target_pairs={{0,16},{4,20},{8,24},{12,28},{16,0},{20,4},{24,8},{28,12},{1,17},{... | collective-permute-start | bytes 393224 | tf_op jit(solution)/shard_map/ppermute | solution.py:309
  5.1 7.4 %collective-permute-start.1 = (f32[2,64,128]{2,1,0:T(8,128)S(1)}, f32[2,64,128]{2,1,0:T(8,128)S(1)}, u32[]{:S(2)}, u32[]{:S(2)}) collective-permute-start(f32[2,64,128]{2,1,0:T(8,128)S(1)} %bitcast.2), channel_id=1, source_target_pairs={{0,8},{4,12},{8,0},{12,4},{16,24},{20,28},{24,16},{28,20},{1,9},{5... | collective-permute-start | bytes 196616 | tf_op jit(solution)/shard_map/ppermute | solution.py:309
  9.5 6.4 %collective-permute-start.3 = (f32[2,64,128]{2,1,0:T(8,128)S(1)}, f32[2,64,128]{2,1,0:T(8,128)S(1)}, u32[]{:S(2)}, u32[]{:S(2)}) collective-permute-start(f32[2,64,128]{2,1,0:T(8,128)S(1)} %collective-permute-done.2.refs_2_), channel_id=1, source_target_pairs={{0,8},{4,12},{8,0},{12,4},{16,24},{20,28},{24,16},{28,20},{1,9},{5... | collective-permute-start | bytes 196616 | tf_op jit(solution)/shard_map/ppermute | solution.py:309
  9.5 22.1 %collective-permute-start.4 = (f32[64,512]{1,0:T(8,128)S(1)}, f32[64,512]{1,0:T(8,128)S(1)}, u32[]{:S(2)}, u32[]{:S(2)}) collective-permute-start(f32[64,512]{1,0:T(8,128)S(1)} %get-tuple-element.22), channel_id=1, source_target_pairs={{0,4},{4,0},{8,12},{12,8},{16,20},{20,16},{24,28},{28,24},{1,5},{5... | collective-permute-start | bytes 393224 | tf_op jit(solution)/shard_map/ppermute | solution.py:309
  10.1 7.9 %collective-permute-start.7 = (f32[64,512]{1,0:T(8,128)S(1)}, f32[64,512]{1,0:T(8,128)S(1)}, u32[]{:S(2)}, u32[]{:S(2)}) collective-permute-start(f32[64,512]{1,0:T(8,128)S(1)} %get-tuple-element.25), channel_id=1, source_target_pairs={{0,8},{4,12},{8,0},{12,4},{16,24},{20,28},{24,16},{28,20},{1,9},{5... | collective-permute-start | bytes 393224 | tf_op jit(solution)/shard_map/ppermute | solution.py:309
  12.5 7.3 %collective-permute-start.8 = (f32[64,512]{1,0:T(8,128)S(1)}, f32[64,512]{1,0:T(8,128)S(1)}, u32[]{:S(2)}, u32[]{:S(2)}) collective-permute-start(f32[64,512]{1,0:T(8,128)S(1)} %get-tuple-element.26), channel_id=1, source_target_pairs={{0,24},{4,28},{8,16},{12,20},{16,8},{20,12},{24,0},{28,4},{1,25},{... | collective-permute-start | bytes 393224 | tf_op jit(solution)/shard_map/ppermute | solution.py:309
  16.0 13.5 %collective-permute-start.11 = (f32[4,2,64,128]{3,2,1,0:T(8,128)S(1)}, f32[4,2,64,128]{3,2,1,0:T(8,128)S(1)}, u32[]{:S(2)}, u32[]{:S(2)}) collective-permute-start(f32[4,2,64,128]{3,2,1,0:T(8,128)S(1)} %heap.1.refs_0_), channel_id=1, source_target_pairs={{0,4},{4,0},{8,12},{12,8},{16,20},{20,16},{24,28},{28,24},{1,5},{5... | collective-permute-start | bytes 786440 | tf_op jit(solution)/shard_map/ppermute | solution.py:309
  16.1 14.6 %collective-permute-start.5 = (f32[4,2,64,128]{3,2,1,0:T(8,128)S(1)}, f32[4,2,64,128]{3,2,1,0:T(8,128)S(1)}, u32[]{:S(2)}, u32[]{:S(2)}) collective-permute-start(f32[4,2,64,128]{3,2,1,0:T(8,128)S(1)} %heap.1.refs_0_), channel_id=1, source_target_pairs={{0,2},{1,3},{2,0},{3,1},{4,6},{5,7},{6,4},{7,5},{8,10},{9,11},{10,... | collective-permute-start | bytes 786440 | tf_op jit(solution)/shard_map/ppermute | solution.py:309
  18.0 12.8 %collective-permute-start.9 = (f32[64,512]{1,0:T(8,128)S(1)}, f32[64,512]{1,0:T(8,128)S(1)}, u32[]{:S(2)}, u32[]{:S(2)}) collective-permute-start(f32[64,512]{1,0:T(8,128)S(1)} %get-tuple-element.27), channel_id=1, source_target_pairs={{0,12},{4,8},{8,4},{12,0},{16,28},{20,24},{24,20},{28,16},{1,13},{... | collective-permute-start | bytes 393224 | tf_op jit(solution)/shard_map/ppermute | solution.py:309
  19.8 10.9 %collective-permute-start.10 = (f32[64,512]{1,0:T(8,128)S(1)}, f32[64,512]{1,0:T(8,128)S(1)}, u32[]{:S(2)}, u32[]{:S(2)}) collective-permute-start(f32[64,512]{1,0:T(8,128)S(1)} %get-tuple-element.28), channel_id=1, source_target_pairs={{0,28},{4,24},{8,20},{12,16},{16,12},{20,8},{24,4},{28,0},{1,29},{... | collective-permute-start | bytes 393224 | tf_op jit(solution)/shard_map/ppermute | solution.py:309
  29.5 6.4 %collective-permute-start.14 = (f32[4,2,64,128]{3,2,1,0:T(8,128)S(1)}, f32[4,2,64,128]{3,2,1,0:T(8,128)S(1)}, u32[]{:S(2)}, u32[]{:S(2)}) collective-permute-start(f32[4,2,64,128]{3,2,1,0:T(8,128)S(1)} %collective-permute-done.11.refs_1_), channel_id=1, source_target_pairs={{0,2},{1,3},{2,0},{3,1},{4,6},{5,7},{6,4},{7,5},{8,10},{9,11},{10,... | collective-permute-start | bytes 786440 | tf_op jit(solution)/shard_map/ppermute | solution.py:309
  30.7 6.8 %collective-permute-start.6 = (f32[64,512]{1,0:T(8,128)S(1)}, f32[64,512]{1,0:T(8,128)S(1)}, u32[]{:S(2)}, u32[]{:S(2)}) collective-permute-start(f32[64,512]{1,0:T(8,128)S(1)} %get-tuple-element.24), channel_id=1, source_target_pairs={{0,20},{4,16},{8,28},{12,24},{16,4},{20,0},{24,12},{28,8},{1,21},{... | collective-permute-start | bytes 393224 | tf_op jit(solution)/shard_map/ppermute | solution.py:309
  31.1 6.8 %copy-start.10 = (bf16[2,256,256]{2,1,0:T(8,128)(2,1)S(1)}, bf16[2,256,256]{2,1,0:T(8,128)(2,1)}, u32[]{:S(2)}) copy-start(bf16[2,256,256]{2,1,0:T(8,128)(2,1)} %constant.11.clone.refs_8_) | copy-start | bytes 786436
  31.1 6.8 %collective-permute-start.12 = (f32[4,2,64,128]{3,2,1,0:T(8,128)S(1)}, f32[4,2,64,128]{3,2,1,0:T(8,128)S(1)}, u32[]{:S(2)}, u32[]{:S(2)}) collective-permute-start(f32[4,2,64,128]{3,2,1,0:T(8,128)S(1)} %heap.1.refs_0_), channel_id=1, source_target_pairs={{0,1},{1,0},{2,3},{3,2},{4,5},{5,4},{6,7},{7,6},{8,9},{9,8},{10,11... | collective-permute-start | bytes 786440 | tf_op jit(solution)/shard_map/ppermute | solution.py:309
  31.2 6.7 %collective-permute-start.13 = (f32[4,2,64,128]{3,2,1,0:T(8,128)S(1)}, f32[4,2,64,128]{3,2,1,0:T(8,128)S(1)}, u32[]{:S(2)}, u32[]{:S(2)}) collective-permute-start(f32[4,2,64,128]{3,2,1,0:T(8,128)S(1)} %collective-permute-done.11.refs_1_), channel_id=1, source_target_pairs={{0,1},{1,0},{2,3},{3,2},{4,5},{5,4},{6,7},{7,6},{8,9},{9,8},{10,11... | collective-permute-start | bytes 786440 | tf_op jit(solution)/shard_map/ppermute | solution.py:309
  31.7 6.2 %collective-permute-start.15 = (f32[4,2,64,128]{3,2,1,0:T(8,128)S(1)}, f32[4,2,64,128]{3,2,1,0:T(8,128)S(1)}, u32[]{:S(2)}, u32[]{:S(2)}) collective-permute-start(f32[4,2,64,128]{3,2,1,0:T(8,128)S(1)} %collective-permute-done.5.refs_4_), channel_id=1, source_target_pairs={{0,1},{1,0},{2,3},{3,2},{4,5},{5,4},{6,7},{7,6},{8,9},{9,8},{10,11... | collective-permute-start | bytes 786440 | tf_op jit(solution)/shard_map/ppermute | solution.py:309
  35.8 2.1 %collective-permute-start.16 = (f32[4,2,64,128]{3,2,1,0:T(8,128)S(1)}, f32[4,2,64,128]{3,2,1,0:T(8,128)S(1)}, u32[]{:S(2)}, u32[]{:S(2)}) collective-permute-start(f32[4,2,64,128]{3,2,1,0:T(8,128)S(1)} %collective-permute-done.14.refs_5_), channel_id=1, source_target_pairs={{0,1},{1,0},{2,3},{3,2},{4,5},{5,4},{6,7},{7,6},{8,9},{9,8},{10,11... | collective-permute-start | bytes 786440 | tf_op jit(solution)/shard_map/ppermute | solution.py:309
  37.8 1.7 %copy-start.2 = (bf16[2,2,256,256]{3,2,1,0:T(8,128)(2,1)S(1)}, bf16[2,2,256,256]{3,2,1,0:T(8,128)(2,1)}, u32[]{:S(2)}) copy-start(bf16[2,2,256,256]{3,2,1,0:T(8,128)(2,1)} %constant.14.clone.refs_10_) | copy-start | bytes 1572868
  37.8 1.6 %copy-start.3 = (s32[8,16]{1,0:T(8,128)S(1)}, s32[8,16]{1,0:T(8,128)}, u32[]{:S(2)}) copy-start(s32[8,16]{1,0:T(8,128)} %refs_1_.1) | copy-start | bytes 1540
  37.8 1.6 %copy-start.5 = (s32[1,8]{1,0:T(1,128)S(1)}, s32[1,8]{1,0:T(1,128)}, u32[]{:S(2)}) copy-start(s32[1,8]{1,0:T(1,128)} %refs_0_.1) | copy-start | bytes 100
  37.9 1.6 %copy-start.6 = (s32[8]{0:T(128)S(1)}, s32[8]{0:T(128)}, u32[]{:S(2)}) copy-start(s32[8]{0:T(128)} %refs_2_.1) | copy-start | bytes 100
  (4 other events, 4.6 us)

commit v2 on v1

--- a/solution.py
+++ b/solution.py
@@ -22,7 +22,10 @@
 FOLDCOST = 3000000000
 EDGES = [['ky', 'f5'], ['heap', 'r0'], ['kx', 'kc0'], ['pack', 'kc1']]
 COSTS = [4000000000, 6000000000, 2000000000, 1500000000]
-OPS = [('pack', []), ('far', []), ('near', []), ('both', ['far']), ('heap', ['near', 'far', 'both']), ('kx', ['heap']), ('ky', ['heap']), ('kxy', ['kx']), ('kc0', ['heap']), ('kc1', ['kx']), ('kc2', ['ky']), ('kc3', ['kxy']), ('f1', ['pack']), ('f2', ['pack']), ('f3', ['pack']), ('f4', ['pack']), ('f5', ['pack']), ('f6', ['pack']), ('f7', ['pack']), ('r0', ['pack', 'f4']), ('r1', ['f1', 'f5']), ('r2', ['f2', 'f6']), ('r3', ['f3', 'f7'])]
+PREP = True
+PREPCOST = 5000000000
+TABLESAT = -1
+OPS = [('prep', []), ('pack', ['prep']), ('far', []), ('near', []), ('both', ['far']), ('heap', ['near', 'far', 'both']), ('kx', ['heap']), ('ky', ['heap']), ('kxy', ['kx']), ('kc0', ['heap']), ('kc1', ['kx']), ('kc2', ['ky']), ('kc3', ['kxy']), ('f1', ['pack']), ('f2', ['pack']), ('f3', ['pack']), ('f4', ['pack']), ('f5', ['pack']), ('f6', ['pack']), ('f7', ['pack']), ('r0', ['pack', 'f4']), ('r1', ['f1', 'f5']), ('r2', ['f2', 'f6']), ('r3', ['f3', 'f7'])]
 ROWCOST = 1024
 F32 = jnp.float32
 
@@ -83,6 +86,22 @@
     return dot(left[0], right[0]) + dot(left[1], right[0]) + dot(left[0], right[1])
 
 
+def prepare_kernel(rank_ref, out_ref):
+    out_ref[...] = rank_ref[...]
+
+
+def prepare(owner_rank):
+    return pl.pallas_call(
+        prepare_kernel,
+        out_shape=jax.ShapeDtypeStruct(owner_rank.shape, jnp.int32),
+        in_specs=[pl.BlockSpec(memory_space=VMEM)],
+        out_specs=pl.BlockSpec(memory_space=VMEM),
+        compiler_params=pltpu.CompilerParams(vmem_limit_bytes=16 << 20),
+        cost_estimate=pl.CostEstimate(flops=PREPCOST, bytes_accessed=1024, transcendentals=0),
+        name="prepare",
+    )(owner_rank)
+
+
 def pack_kernel(rank_ref, frames_ref, *outs):
     me = lax.axis_index("strip")
     ranks = rank_ref[...]
@@ -127,19 +146,15 @@
 
 def fold_tiles(scr, perm_ref, out_ref):
     half = perm_ref.shape[1]
-    lane = lax.broadcasted_iota(jnp.int32, (128, 128), 1)
     for part in range(2):
         for tile in range(scr.shape[1]):
             left, right = split(scr[part, tile, 0:half]), split(scr[part, tile, half:])
             plus = turned(left[0], perm_ref[0]) + turned(left[1], perm_ref[0])
             minus = turned(right[0], perm_ref[1]) + turned(right[1], perm_ref[1])
             for group in range(2):
-                p, m = (x[:, group * 128 : (group + 1) * 128] for x in (plus, minus))
-                both, diff = p + m, p - m
-                if group == 0:
-                    both, diff = jnp.where(lane == 0, p, both), jnp.where(lane == 0, m, diff)
-                out_ref[part, group, tile * 128 : (tile + 1) * 128] = both
-                out_ref[2 + part, group, tile * 128 : (tile + 1) * 128] = diff
+                lanes = slice(group * 128, (group + 1) * 128)
+                out_ref[part, group, tile * 128 : (tile + 1) * 128] = plus[:, lanes]
+                out_ref[2 + part, group, tile * 128 : (tile + 1) * 128] = minus[:, lanes]
 
 
 def fold_pieces_kernel(*refs):
@@ -159,19 +174,6 @@
         for tile in range(scr.shape[1]):
             scr[part, tile] = kern_ref[part, :, tile * 128 : (tile + 1) * 128]
     fold_tiles(scr, perm_ref, out_ref)
-
-
-def fold(body, args, perm, detector):
-    return pl.pallas_call(
-        body,
-        out_shape=jax.ShapeDtypeStruct((4, 2, detector, detector // 4), F32),
-        in_specs=[pl.BlockSpec(memory_space=VMEM)] * (len(args) + 1),
-        out_specs=pl.BlockSpec(memory_space=VMEM),
-        scratch_shapes=[VMEM((2, detector // 128, detector, 128), F32)],
-        compiler_params=pltpu.CompilerParams(vmem_limit_bytes=32 << 20),
-        cost_estimate=pl.CostEstimate(flops=FOLDCOST, bytes_accessed=1024, transcendentals=0),
-        name="fold",
-    )(*args, perm)
 
 
 def rows_kernel(split_strip, lower_ref, upper_ref, row_ref, *rest):
@@ -195,7 +197,7 @@
     return pl.pallas_call(
         functools.partial(rows_kernel, split_strip),
         out_shape=jax.ShapeDtypeStruct((2, 2, rows, detector), BF16),
-        in_specs=[pl.BlockSpec(memory_space=VMEM)] * 3 + [pl.BlockSpec(memory_space=pl.ANY)] * len(before),
+        in_specs=[pl.BlockSpec(memory_space=VMEM)] * (3 + len(before)),
         out_specs=pl.BlockSpec(memory_space=VMEM),
         compiler_params=pltpu.CompilerParams(vmem_limit_bytes=16 << 20),
         cost_estimate=pl.CostEstimate(flops=flops, bytes_accessed=1024, transcendentals=0),
@@ -203,14 +205,15 @@
     )(lower, upper, table, *before)
 
 
-def correlate_kernel(pieces, *refs):
-    lists = refs[:3]
-    spectra = refs[3 : 3 + pieces]
-    fold_ref, col_ref, inv_ref, fin_ref, out_ref, spec, img, blocks, *scalars = refs[3 + pieces :]
-    *scalars, sems = scalars
-    copies = [pltpu.make_async_copy(x, y, sems.at[i]) for i, (x, y) in enumerate(zip(lists, scalars))]
-    for copy in copies:
+def correlate_kernel(pieces, fold_body, *refs):
+    tables, lists, refs = refs[:3], refs[3:6], refs[6:]
+    spectra, kern, perm_ref, out_ref = refs[:pieces], refs[pieces:-15], refs[-15], refs[-14]
+    scr, fold_ref, spec, img, blocks, col_ref, inv_ref, fin_ref, *scalars, sems, list_sems = refs[-13:]
+    loads = [pltpu.make_async_copy(x, y, sems.at[i]) for i, (x, y) in enumerate(zip(tables, (col_ref, inv_ref, fin_ref)))]
+    copies = [pltpu.make_async_copy(x, y, list_sems.at[i]) for i, (x, y) in enumerate(zip(lists, scalars))]
+    for copy in loads + copies:
         copy.start()
+    fold_body(*kern, perm_ref, fold_ref, scr)
     detector = fold_ref.shape[2]
     half, quarter = detector // 2, detector // 4
     me = lax.axis_index("strip")
@@ -221,6 +224,8 @@
 
     lane = lax.broadcasted_iota(jnp.int32, (half, quarter), 1)
     back = []
+    loads[0].wait()
+    loads[1].wait()
     for parity in range(2):
         table = (col_ref[0, parity], col_ref[1, parity])
         parts = []
@@ -230,22 +235,27 @@
             cos_re, cos_im = both[0:half, 0:quarter], both[0:half, quarter:]
             sin_re, sin_im = both[half:, 0:quarter], both[half:, quarter:]
             freqs = pl.ds(parity, half, stride=2)
-            sum_re, sum_im = fold_ref[0, group, freqs, :], fold_ref[1, group, freqs, :]
-            dif_re, dif_im = fold_ref[2, group, freqs, :], fold_ref[3, group, freqs, :]
-            two_re, two_im = sum_re, sum_im
+            up_re, up_im = fold_ref[0, group, freqs, :], fold_ref[1, group, freqs, :]
+            dn_re, dn_im = fold_ref[2, group, freqs, :], fold_ref[3, group, freqs, :]
+            a_re, a_im = cos_re + sin_im, cos_im - sin_re
+            b_re, b_im = cos_re - sin_im, -cos_im - sin_re
             if group == 0:
-                two_re, two_im = jnp.where(lane == 0, dif_re, sum_re), jnp.where(lane == 0, dif_im, sum_im)
-                dif_re, dif_im = jnp.where(lane == 0, 0.0, dif_re), jnp.where(lane == 0, 0.0, dif_im)
-            plus_re = cos_re * sum_re + sin_im * dif_re - cos_im * dif_im + sin_re * sum_im
-            plus_im = cos_re * sum_im + sin_im * dif_im + cos_im * dif_re - sin_re * sum_re
-            minus_re = cos_re * dif_re + sin_im * two_re - cos_im * two_im + sin_re * dif_im
-            minus_im = cos_re * dif_im + sin_im * two_im + cos_im * two_re - sin_re * dif_re
+                a_re, a_im = jnp.where(lane == 0, cos_re, a_re), jnp.where(lane == 0, -sin_re, a_im)
+                b_re, b_im = jnp.where(lane == 0, cos_im, b_re), jnp.where(lane == 0, -sin_im, b_im)
+            p_re, p_im = a_re * up_re - a_im * up_im, a_re * up_im + a_im * up_re
+            q_re, q_im = b_re * dn_re - b_im * dn_im, b_re * dn_im + b_im * dn_re
+            plus_re, minus_im = p_re + q_re, p_im - q_im
+            less_im, minus_re = -p_im - q_im, p_re - q_re
+            if group == 0:
+                plus_re, minus_im = jnp.where(lane == 0, p_re, plus_re), jnp.where(lane == 0, q_re, minus_im)
+                less_im, minus_re = jnp.where(lane == 0, -p_im, less_im), jnp.where(lane == 0, -q_im, minus_re)
             upper = split(jnp.concatenate([plus_re, minus_im], axis=1))
-            lower = split(jnp.concatenate([-plus_im, minus_re], axis=1))
+            lower = split(jnp.concatenate([less_im, minus_re], axis=1))
             parts.append([jnp.concatenate([u, w], axis=0) for u, w in zip(upper, lower)])
         table = (inv_ref[0, parity], inv_ref[1, parity])
         back.append([dot3(table, part) for part in parts])
 
+    loads[2].wait()
     for upper in range(2):
         ends = []
         for group in range(2):
@@ -283,26 +293,28 @@
         out_ref[0, :, j * 2 * BLK : (j + 1) * 2 * BLK] = blocks[pl.ds(j, MAXB, stride=pairs), :]
 
 
-def correlate(owner_rank, block_ids, block_counts, spectra, folded, consts):
-    detector = folded.shape[2]
-    return pl.pallas_call(
-        functools.partial(correlate_kernel, len(spectra)),
+def correlate(owner_rank, block_ids, block_counts, spectra, fold_body, kern, perm, consts):
+    detector = spectra[0].shape[-1]
+    half = detector // 2
+    return pl.pallas_call(
+        functools.partial(correlate_kernel, len(spectra), fold_body),
         out_shape=jax.ShapeDtypeStruct((1, MAXB, BLK * BLK), F32),
-        in_specs=[pl.BlockSpec(memory_space=pl.ANY)] * 3
-        + [pl.BlockSpec(memory_space=VMEM)] * (len(spectra) + 1 + len(consts)),
+        in_specs=[pl.BlockSpec(memory_space=pl.ANY)] * 6
+        + [pl.BlockSpec(memory_space=VMEM)] * (len(spectra) + len(kern) + 1),
         out_specs=pl.BlockSpec(memory_space=VMEM),
         scratch_shapes=[
-            VMEM((2, 2, detector // 2, detector), BF16),
+            VMEM((2, detector // 128, detector, 128), F32),
+            VMEM((4, 2, detector, detector // 4), F32),
+            VMEM((2, 2, half, detector), BF16),
             VMEM((detector // 128, detector, 128), F32),
             VMEM((MAXB * BLK // 2, 2 * BLK), F32),
-            SMEM(owner_rank.shape, jnp.int32),
-            SMEM(block_ids.shape, jnp.int32),
-            SMEM(block_counts.shape, jnp.int32),
-            pltpu.SemaphoreType.DMA((3,)),
-        ],
-        compiler_params=pltpu.CompilerParams(vmem_limit_bytes=40 << 20),
+        ]
+        + [VMEM(x.shape, BF16) for x in consts]
+        + [SMEM(x.shape, jnp.int32) for x in (owner_rank, block_ids, block_counts)]
+        + [pltpu.SemaphoreType.DMA((3,)), pltpu.SemaphoreType.DMA((3,))],
+        compiler_params=pltpu.CompilerParams(vmem_limit_bytes=48 << 20),
         name="correlate",
-    )(owner_rank, block_ids, block_counts, *spectra, folded, *consts)
+    )(*consts, owner_rank, block_ids, block_counts, *spectra, *kern, perm)
 
 
 def swap(value, axis, size, bits):
@@ -330,7 +342,9 @@
 
             natural = [val[d] for d in needs[name]]
             if name == "pack":
-                val[name] = pack(tied(owner_rank), frames)
+                val[name] = pack(tied(natural[0] if natural else owner_rank), frames)
+            elif name == "prep":
+                val[name] = prepare(tied(owner_rank))
             elif name == "far":
                 val[name] = swap(tied(piece), "strip", 8, 4)
             elif name == "near":
@@ -351,22 +365,22 @@
                 j = int(name[1])
                 low = natural[0][0] if j == 0 else natural[0]
                 low, high = tied((low, natural[-1]))
-                val[name] = row_spectra(low, high, row_table, 4, COSTS[j])
+                val[name] = row_spectra(low, high, row_table, 4, COSTS[j], consts if TABLESAT == j else ())
 
         for name in needs:
             visit(name)
         quads = [val["heap"], val["kx"], val["ky"], val["kxy"]] + [val["kc%d" % i] for i in range(4)]
-        ordered = [quads[4 * (df % 2) + 2 * (df // 2) + dx] for df in range(4) for dx in range(2)]
-        folded = fold(fold_pieces_kernel, ordered, perm, detector)
+        kern = [quads[4 * (df % 2) + 2 * (df // 2) + dx] for df in range(4) for dx in range(2)]
+        fold_body = fold_pieces_kernel
         spectra = [val["r%d" % j] for j in range(4)]
     else:
         places = jnp.argsort(owner_rank.reshape(-1))
         frame = lax.all_to_all(frames[places], "strip", split_axis=0, concat_axis=1, tiled=True)[0]
         whole = lax.all_gather(kernel, "strip", axis=2, tiled=True)
         whole = lax.all_gather(whole, "frames", axis=1, tiled=True)
-        folded = fold(fold_whole_kernel, [jnp.swapaxes(whole, 1, 2)], perm, detector)
+        fold_body, kern = fold_whole_kernel, [jnp.swapaxes(whole, 1, 2)]
         spectra = [row_spectra(frame[: detector // 2], frame[detector // 2 :], row_table, 0, ROWCOST)]
-    return correlate(owner_rank, block_ids, block_counts, spectra, folded, consts)
+    return correlate(owner_rank, block_ids, block_counts, spectra, fold_body, kern, perm, consts)
 
 
 def solution(mesh):

time: 44.2 us -> 43.1 us (0.975)
  the two profiles are of different devices: /device:TPU:26 before, /device:TPU:0 now
where the time goes in v2:
time: 43.1 us; the launch traced here: 43 us
  starting transfers between devices  27.5 us (64%)
  waiting for transfers between devices  8.5 us (20%)
  Pallas kernels  6.72 us (16%)
    ppermute x17, starting transfers between devices, swap(): return lax.ppermute(value, axis, [(i, i ^ bits) for i in range(size)])  27.5 us
    ppermute x17, waiting for transfers between devices, swap(): return lax.ppermute(value, axis, [(i, i ^ bits) for i in range(size)])  8.5 us
    pallas_call x1, Pallas kernels, correlate(): pl.pallas_call(functools.partial(correlate_kernel, len(spectra), fold_bod...  5.33 us
    pallas_call x4, Pallas kernels, row_spectra(): pl.pallas_call(functools.partial(rows_kernel, split_strip), out_shape=jax...  1.16 us
  transfers between devices with their start and end apart: 17, of which 4 were waited for; matrix products, arithmetic and copies ran while one was open for 0% of the time, Pallas kernels for 3%

profile of v2, /device:TPU:0, one launch (start us, length us, event | category | flops | bytes accessed | tf_op | source)
XLA Modules:
  0.0 43.0 jit_solution(13537021105429141722)
XLA Ops:
  0.0 4.0 %collective-permute-start.2 = (f32[2,64,128]{2,1,0:T(8,128)}, f32[2,64,128]{2,1,0:T(8,128)S(1)}, u32[]{:S(2)}, u32[]{:S(2)}) collective-permute-start(f32[2,64,128]{2,1,0:T(8,128)} %bitcast.1), channel_id=1, source_target_pairs={{0,16},{4,20},{8,24},{12,28},{16,0},{20,4},{24,8},{28,12},{1,17},{... | collective-permute-start | bytes 196616 | tf_op jit(solution)/shard_map/ppermute | solution.py:321
  4.1 0.2 pack.1
  4.3 1.3 %collective-permute-start = (f32[64,512]{1,0:T(8,128)S(1)}, f32[64,512]{1,0:T(8,128)S(1)}, u32[]{:S(2)}, u32[]{:S(2)}) collective-permute-start(f32[64,512]{1,0:T(8,128)S(1)} %get-tuple-element.19), channel_id=1, source_target_pairs={{0,16},{4,20},{8,24},{12,28},{16,0},{20,4},{24,8},{28,12},{1,17},{... | collective-permute-start | bytes 393224 | tf_op jit(solution)/shard_map/ppermute | solution.py:321
  5.5 1.6 %collective-permute-start.1 = (f32[2,64,128]{2,1,0:T(8,128)S(1)}, f32[2,64,128]{2,1,0:T(8,128)S(1)}, u32[]{:S(2)}, u32[]{:S(2)}) collective-permute-start(f32[2,64,128]{2,1,0:T(8,128)S(1)} %bitcast.2), channel_id=1, source_target_pairs={{0,8},{4,12},{8,0},{12,4},{16,24},{20,28},{24,16},{28,20},{1,9},{5... | collective-permute-start | bytes 196616 | tf_op jit(solution)/shard_map/ppermute | solution.py:321
  7.1 0.9 %collective-permute-done.2.refs_2_ = f32[2,64,128]{2,1,0:T(8,128)S(1)} collective-permute-done((f32[2,64,128]{2,1,0:T(8,128)}, f32[2,64,128]{2,1,0:T(8,128)S(1)}, u32[]{:S(2)}, u32[]{:S(2)}) %collective-permute-start.2) | collective-permute-done | bytes 65568 | tf_op jit(solution)/shard_map/ppermute | solution.py:321
  8.0 3.8 %collective-permute-start.3 = (f32[2,64,128]{2,1,0:T(8,128)S(1)}, f32[2,64,128]{2,1,0:T(8,128)S(1)}, u32[]{:S(2)}, u32[]{:S(2)}) collective-permute-start(f32[2,64,128]{2,1,0:T(8,128)S(1)} %collective-permute-done.2.refs_2_), channel_id=1, source_target_pairs={{0,8},{4,12},{8,0},{12,4},{16,24},{20,28},{24,16},{28,20},{1,9},{5... | collective-permute-start | bytes 196616 | tf_op jit(solution)/shard_map/ppermute | solution.py:321
  11.8 1.5 %collective-permute-start.4 = (f32[64,512]{1,0:T(8,128)S(1)}, f32[64,512]{1,0:T(8,128)S(1)}, u32[]{:S(2)}, u32[]{:S(2)}) collective-permute-start(f32[64,512]{1,0:T(8,128)S(1)} %get-tuple-element.22), channel_id=1, source_target_pairs={{0,4},{4,0},{8,12},{12,8},{16,20},{20,16},{24,28},{28,24},{1,5},{5... | collective-permute-start | bytes 393224 | tf_op jit(solution)/shard_map/ppermute | solution.py:321
  13.3 4.7 %collective-permute-start.8 = (f32[64,512]{1,0:T(8,128)S(1)}, f32[64,512]{1,0:T(8,128)S(1)}, u32[]{:S(2)}, u32[]{:S(2)}) collective-permute-start(f32[64,512]{1,0:T(8,128)S(1)} %get-tuple-element.26), channel_id=1, source_target_pairs={{0,24},{4,28},{8,16},{12,20},{16,8},{20,12},{24,0},{28,4},{1,25},{... | collective-permute-start | bytes 393224 | tf_op jit(solution)/shard_map/ppermute | solution.py:321
  18.1 0.6 %collective-permute-start.11 = (f32[4,2,64,128]{3,2,1,0:T(8,128)S(1)}, f32[4,2,64,128]{3,2,1,0:T(8,128)S(1)}, u32[]{:S(2)}, u32[]{:S(2)}) collective-permute-start(f32[4,2,64,128]{3,2,1,0:T(8,128)S(1)} %heap.1.refs_10_), channel_id=1, source_target_pairs={{0,4},{4,0},{8,12},{12,8},{16,20},{20,16},{24,28},{28,24},{1,5},{5... | collective-permute-start | bytes 786440 | tf_op jit(solution)/shard_map/ppermute | solution.py:321
  18.7 1.5 %collective-permute-start.5 = (f32[4,2,64,128]{3,2,1,0:T(8,128)S(1)}, f32[4,2,64,128]{3,2,1,0:T(8,128)S(1)}, u32[]{:S(2)}, u32[]{:S(2)}) collective-permute-start(f32[4,2,64,128]{3,2,1,0:T(8,128)S(1)} %heap.1.refs_10_), channel_id=1, source_target_pairs={{0,2},{1,3},{2,0},{3,1},{4,6},{5,7},{6,4},{7,5},{8,10},{9,11},{10,... | collective-permute-start | bytes 786440 | tf_op jit(solution)/shard_map/ppermute | solution.py:321
  20.2 0.3 rows.4.refs_6_
  20.5 0.2 collective-permute-start.9
  20.7 3.1 %collective-permute-done.8.upper_ref = f32[64,512]{1,0:T(8,128)S(1)} collective-permute-done((f32[64,512]{1,0:T(8,128)S(1)}, f32[64,512]{1,0:T(8,128)S(1)}, u32[]{:S(2)}, u32[]{:S(2)}) %collective-permute-start.8) | collective-permute-done | bytes 131104 | tf_op jit(solution)/shard_map/ppermute | solution.py:321
  23.8 2.1 %collective-permute-start.10 = (f32[64,512]{1,0:T(8,128)S(1)}, f32[64,512]{1,0:T(8,128)S(1)}, u32[]{:S(2)}, u32[]{:S(2)}) collective-permute-start(f32[64,512]{1,0:T(8,128)S(1)} %get-tuple-element.28), channel_id=1, source_target_pairs={{0,28},{4,24},{8,20},{12,16},{16,12},{20,8},{24,4},{28,0},{1,29},{... | collective-permute-start | bytes 393224 | tf_op jit(solution)/shard_map/ppermute | solution.py:321
  26.0 2.6 %collective-permute-done.11.refs_11_ = f32[4,2,64,128]{3,2,1,0:T(8,128)S(1)} collective-permute-done((f32[4,2,64,128]{3,2,1,0:T(8,128)S(1)}, f32[4,2,64,128]{3,2,1,0:T(8,128)S(1)}, u32[]{:S(2)}, u32[]{:S(2)}) %collective-permute-start.11) | collective-permute-done | bytes 262176 | tf_op jit(solution)/shard_map/ppermute | solution.py:321
  28.6 1.5 %collective-permute-start.14 = (f32[4,2,64,128]{3,2,1,0:T(8,128)S(1)}, f32[4,2,64,128]{3,2,1,0:T(8,128)S(1)}, u32[]{:S(2)}, u32[]{:S(2)}) collective-permute-start(f32[4,2,64,128]{3,2,1,0:T(8,128)S(1)} %collective-permute-done.11.refs_11_), channel_id=1, source_target_pairs={{0,2},{1,3},{2,0},{3,1},{4,6},{5,7},{6,4},{7,5},{8,10},{9,11},{10,... | collective-permute-start | bytes 786440 | tf_op jit(solution)/shard_map/ppermute | solution.py:321
  30.1 0.3 rows.6.refs_8_
  30.4 3.5 %collective-permute-start.6 = (f32[64,512]{1,0:T(8,128)S(1)}, f32[64,512]{1,0:T(8,128)S(1)}, u32[]{:S(2)}, u32[]{:S(2)}) collective-permute-start(f32[64,512]{1,0:T(8,128)S(1)} %get-tuple-element.24), channel_id=1, source_target_pairs={{0,20},{4,16},{8,28},{12,24},{16,4},{20,0},{24,12},{28,8},{1,21},{... | collective-permute-start | bytes 393224 | tf_op jit(solution)/shard_map/ppermute | solution.py:321
  33.9 0.3 rows.7.refs_9_
  34.4 0.5 %collective-permute-start.13 = (f32[4,2,64,128]{3,2,1,0:T(8,128)S(1)}, f32[4,2,64,128]{3,2,1,0:T(8,128)S(1)}, u32[]{:S(2)}, u32[]{:S(2)}) collective-permute-start(f32[4,2,64,128]{3,2,1,0:T(8,128)S(1)} %collective-permute-done.11.refs_11_), channel_id=1, source_target_pairs={{0,1},{1,0},{2,3},{3,2},{4,5},{5,4},{6,7},{7,6},{8,9},{9,8},{10,11... | collective-permute-start | bytes 786440 | tf_op jit(solution)/shard_map/ppermute | solution.py:321
  35.0 0.4 %collective-permute-start.16 = (f32[4,2,64,128]{3,2,1,0:T(8,128)S(1)}, f32[4,2,64,128]{3,2,1,0:T(8,128)S(1)}, u32[]{:S(2)}, u32[]{:S(2)}) collective-permute-start(f32[4,2,64,128]{3,2,1,0:T(8,128)S(1)} %collective-permute-done.14.refs_15_), channel_id=1, source_target_pairs={{0,1},{1,0},{2,3},{3,2},{4,5},{5,4},{6,7},{7,6},{8,9},{9,8},{10,11... | collective-permute-start | bytes 786440 | tf_op jit(solution)/shard_map/ppermute | solution.py:321
  35.4 1.8 %collective-permute-done.6.upper_ref = f32[64,512]{1,0:T(8,128)S(1)} collective-permute-done((f32[64,512]{1,0:T(8,128)S(1)}, f32[64,512]{1,0:T(8,128)S(1)}, u32[]{:S(2)}, u32[]{:S(2)}) %collective-permute-start.6) | collective-permute-done | bytes 131104 | tf_op jit(solution)/shard_map/ppermute | solution.py:321
  37.2 0.3 rows.5.refs_7_
  37.6 5.3 %correlate.1 = f32[1,16,4096]{2,1,0:T(8,128)} custom-call(bf16[2,2,512,256]{3,2,1,0:T(8,128)(2,1)S(1)} %copy-done.1, bf16[2,2,256,512]{3,2,1,0:T(8,128)(2,1)S(1)} %copy-done, bf16[2,2,256,256]{3,2,1,0:T(8,128)(2,1)S(1)} %copy-done.2, s32[1,8]{1,0:T(1,128)S(1)} %copy-done.5, s32[8,16]{1,0:T(8,128)S(1)} %copy-done.4, s32[8]{0:T(128)S(1)} %copy-done.6, ...), custom_call_target="tpu_custom_call" | custom-call | tf_op jit(solution)/shard_map/correlate/pallas_call | solution.py:299
  (38 shorter events, 0.3 us)
Async XLA Ops:
  0.0 4.0 %copy-start.5 = (s32[1,8]{1,0:T(1,128)S(1)}, s32[1,8]{1,0:T(1,128)}, u32[]{:S(2)}) copy-start(s32[1,8]{1,0:T(1,128)} %refs_3_.1) | copy-start | bytes 100
  0.0 4.0 %copy-start.7 = (f32[8,64,512]{2,1,0:T(8,128)S(1)}, f32[8,64,512]{2,1,0:T(8,128)}, u32[]{:S(2)}) copy-start(f32[8,64,512]{2,1,0:T(8,128)} %frames_ref.1) | copy-start | bytes 3145732
  0.0 8.0 %collective-permute-start.2 = (f32[2,64,128]{2,1,0:T(8,128)}, f32[2,64,128]{2,1,0:T(8,128)S(1)}, u32[]{:S(2)}, u32[]{:S(2)}) collective-permute-start(f32[2,64,128]{2,1,0:T(8,128)} %bitcast.1), channel_id=1, source_target_pairs={{0,16},{4,20},{8,24},{12,28},{16,0},{20,4},{24,8},{28,12},{1,17},{... | collective-permute-start | bytes 196616 | tf_op jit(solution)/shard_map/ppermute | solution.py:321
  4.3 14.4 %collective-permute-start = (f32[64,512]{1,0:T(8,128)S(1)}, f32[64,512]{1,0:T(8,128)S(1)}, u32[]{:S(2)}, u32[]{:S(2)}) collective-permute-start(f32[64,512]{1,0:T(8,128)S(1)} %get-tuple-element.19), channel_id=1, source_target_pairs={{0,16},{4,20},{8,24},{12,28},{16,0},{20,4},{24,8},{28,12},{1,17},{... | collective-permute-start | bytes 393224 | tf_op jit(solution)/shard_map/ppermute | solution.py:321
  5.5 7.8 %collective-permute-start.1 = (f32[2,64,128]{2,1,0:T(8,128)S(1)}, f32[2,64,128]{2,1,0:T(8,128)S(1)}, u32[]{:S(2)}, u32[]{:S(2)}) collective-permute-start(f32[2,64,128]{2,1,0:T(8,128)S(1)} %bitcast.2), channel_id=1, source_target_pairs={{0,8},{4,12},{8,0},{12,4},{16,24},{20,28},{24,16},{28,20},{1,9},{5... | collective-permute-start | bytes 196616 | tf_op jit(solution)/shard_map/ppermute | solution.py:321
  8.0 10.1 %collective-permute-start.3 = (f32[2,64,128]{2,1,0:T(8,128)S(1)}, f32[2,64,128]{2,1,0:T(8,128)S(1)}, u32[]{:S(2)}, u32[]{:S(2)}) collective-permute-start(f32[2,64,128]{2,1,0:T(8,128)S(1)} %collective-permute-done.2.refs_2_), channel_id=1, source_target_pairs={{0,8},{4,12},{8,0},{12,4},{16,24},{20,28},{24,16},{28,20},{1,9},{5... | collective-permute-start | bytes 196616 | tf_op jit(solution)/shard_map/ppermute | solution.py:321
  11.8 23.1 %collective-permute-start.4 = (f32[64,512]{1,0:T(8,128)S(1)}, f32[64,512]{1,0:T(8,128)S(1)}, u32[]{:S(2)}, u32[]{:S(2)}) collective-permute-start(f32[64,512]{1,0:T(8,128)S(1)} %get-tuple-element.22), channel_id=1, source_target_pairs={{0,4},{4,0},{8,12},{12,8},{16,20},{20,16},{24,28},{28,24},{1,5},{5... | collective-permute-start | bytes 393224 | tf_op jit(solution)/shard_map/ppermute | solution.py:321
  13.3 7.2 %collective-permute-start.7 = (f32[64,512]{1,0:T(8,128)S(1)}, f32[64,512]{1,0:T(8,128)S(1)}, u32[]{:S(2)}, u32[]{:S(2)}) collective-permute-start(f32[64,512]{1,0:T(8,128)S(1)} %get-tuple-element.25), channel_id=1, source_target_pairs={{0,8},{4,12},{8,0},{12,4},{16,24},{20,28},{24,16},{28,20},{1,9},{5... | collective-permute-start | bytes 393224 | tf_op jit(solution)/shard_map/ppermute | solution.py:321
  13.3 6.9 %copy-start.9 = (bf16[2,2,256,256]{3,2,1,0:T(8,128)(2,1)S(1)}, bf16[2,2,256,256]{3,2,1,0:T(8,128)(2,1)}, u32[]{:S(2)}) copy-start(bf16[2,2,256,256]{3,2,1,0:T(8,128)(2,1)} %constant.10.clone.row_ref) | copy-start | bytes 1572868
  13.3 10.5 %collective-permute-start.8 = (f32[64,512]{1,0:T(8,128)S(1)}, f32[64,512]{1,0:T(8,128)S(1)}, u32[]{:S(2)}, u32[]{:S(2)}) collective-permute-start(f32[64,512]{1,0:T(8,128)S(1)} %get-tuple-element.26), channel_id=1, source_target_pairs={{0,24},{4,28},{8,16},{12,20},{16,8},{20,12},{24,0},{28,4},{1,25},{... | collective-permute-start | bytes 393224 | tf_op jit(solution)/shard_map/ppermute | solution.py:321
  18.1 10.5 %collective-permute-start.11 = (f32[4,2,64,128]{3,2,1,0:T(8,128)S(1)}, f32[4,2,64,128]{3,2,1,0:T(8,128)S(1)}, u32[]{:S(2)}, u32[]{:S(2)}) collective-permute-start(f32[4,2,64,128]{3,2,1,0:T(8,128)S(1)} %heap.1.refs_10_), channel_id=1, source_target_pairs={{0,4},{4,0},{8,12},{12,8},{16,20},{20,16},{24,28},{28,24},{1,5},{5... | collective-permute-start | bytes 786440 | tf_op jit(solution)/shard_map/ppermute | solution.py:321
  18.7 11.7 %collective-permute-start.5 = (f32[4,2,64,128]{3,2,1,0:T(8,128)S(1)}, f32[4,2,64,128]{3,2,1,0:T(8,128)S(1)}, u32[]{:S(2)}, u32[]{:S(2)}) collective-permute-start(f32[4,2,64,128]{3,2,1,0:T(8,128)S(1)} %heap.1.refs_10_), channel_id=1, source_target_pairs={{0,2},{1,3},{2,0},{3,1},{4,6},{5,7},{6,4},{7,5},{8,10},{9,11},{10,... | collective-permute-start | bytes 786440 | tf_op jit(solution)/shard_map/ppermute | solution.py:321
  20.5 13.4 %collective-permute-start.9 = (f32[64,512]{1,0:T(8,128)S(1)}, f32[64,512]{1,0:T(8,128)S(1)}, u32[]{:S(2)}, u32[]{:S(2)}) collective-permute-start(f32[64,512]{1,0:T(8,128)S(1)} %get-tuple-element.27), channel_id=1, source_target_pairs={{0,12},{4,8},{8,4},{12,0},{16,28},{20,24},{24,20},{28,16},{1,13},{... | collective-permute-start | bytes 393224 | tf_op jit(solution)/shard_map/ppermute | solution.py:321
  23.8 10.1 %collective-permute-start.10 = (f32[64,512]{1,0:T(8,128)S(1)}, f32[64,512]{1,0:T(8,128)S(1)}, u32[]{:S(2)}, u32[]{:S(2)}) collective-permute-start(f32[64,512]{1,0:T(8,128)S(1)} %get-tuple-element.28), channel_id=1, source_target_pairs={{0,28},{4,24},{8,20},{12,16},{16,12},{20,8},{24,4},{28,0},{1,29},{... | collective-permute-start | bytes 393224 | tf_op jit(solution)/shard_map/ppermute | solution.py:321
  28.6 6.4 %collective-permute-start.14 = (f32[4,2,64,128]{3,2,1,0:T(8,128)S(1)}, f32[4,2,64,128]{3,2,1,0:T(8,128)S(1)}, u32[]{:S(2)}, u32[]{:S(2)}) collective-permute-start(f32[4,2,64,128]{3,2,1,0:T(8,128)S(1)} %collective-permute-done.11.refs_11_), channel_id=1, source_target_pairs={{0,2},{1,3},{2,0},{3,1},{4,6},{5,7},{6,4},{7,5},{8,10},{9,11},{10,... | collective-permute-start | bytes 786440 | tf_op jit(solution)/shard_map/ppermute | solution.py:321
  30.4 6.8 %collective-permute-start.6 = (f32[64,512]{1,0:T(8,128)S(1)}, f32[64,512]{1,0:T(8,128)S(1)}, u32[]{:S(2)}, u32[]{:S(2)}) collective-permute-start(f32[64,512]{1,0:T(8,128)S(1)} %get-tuple-element.24), channel_id=1, source_target_pairs={{0,20},{4,16},{8,28},{12,24},{16,4},{20,0},{24,12},{28,8},{1,21},{... | collective-permute-start | bytes 393224 | tf_op jit(solution)/shard_map/ppermute | solution.py:321
  34.2 3.3 %copy-start = (bf16[2,2,256,512]{3,2,1,0:T(8,128)(2,1)S(1)}, bf16[2,2,256,512]{3,2,1,0:T(8,128)(2,1)}, u32[]{:S(2)}) copy-start(bf16[2,2,256,512]{3,2,1,0:T(8,128)(2,1)} %constant.12.clone.refs_1_) | copy-start | bytes 3145732
  34.3 3.3 %copy-start.1 = (bf16[2,2,512,256]{3,2,1,0:T(8,128)(2,1)S(1)}, bf16[2,2,512,256]{3,2,1,0:T(8,128)(2,1)}, u32[]{:S(2)}) copy-start(bf16[2,2,512,256]{3,2,1,0:T(8,128)(2,1)} %constant.11.clone.refs_0_) | copy-start | bytes 3145732
  34.3 3.3 %copy-start.2 = (bf16[2,2,256,256]{3,2,1,0:T(8,128)(2,1)S(1)}, bf16[2,2,256,256]{3,2,1,0:T(8,128)(2,1)}, u32[]{:S(2)}) copy-start(bf16[2,2,256,256]{3,2,1,0:T(8,128)(2,1)} %constant.13.clone.refs_2_) | copy-start | bytes 1572868
  34.3 3.3 %copy-start.3 = (bf16[2,256,256]{2,1,0:T(8,128)(2,1)S(1)}, bf16[2,256,256]{2,1,0:T(8,128)(2,1)}, u32[]{:S(2)}) copy-start(bf16[2,256,256]{2,1,0:T(8,128)(2,1)} %constant.14.clone.refs_18_) | copy-start | bytes 786436
  34.3 3.2 %collective-permute-start.12 = (f32[4,2,64,128]{3,2,1,0:T(8,128)S(1)}, f32[4,2,64,128]{3,2,1,0:T(8,128)S(1)}, u32[]{:S(2)}, u32[]{:S(2)}) collective-permute-start(f32[4,2,64,128]{3,2,1,0:T(8,128)S(1)} %heap.1.refs_10_), channel_id=1, source_target_pairs={{0,1},{1,0},{2,3},{3,2},{4,5},{5,4},{6,7},{7,6},{8,9},{9,8},{10,11... | collective-permute-start | bytes 786440 | tf_op jit(solution)/shard_map/ppermute | solution.py:321
  34.4 3.2 %collective-permute-start.13 = (f32[4,2,64,128]{3,2,1,0:T(8,128)S(1)}, f32[4,2,64,128]{3,2,1,0:T(8,128)S(1)}, u32[]{:S(2)}, u32[]{:S(2)}) collective-permute-start(f32[4,2,64,128]{3,2,1,0:T(8,128)S(1)} %collective-permute-done.11.refs_11_), channel_id=1, source_target_pairs={{0,1},{1,0},{2,3},{3,2},{4,5},{5,4},{6,7},{7,6},{8,9},{9,8},{10,11... | collective-permute-start | bytes 786440 | tf_op jit(solution)/shard_map/ppermute | solution.py:321
  34.9 2.7 %collective-permute-start.15 = (f32[4,2,64,128]{3,2,1,0:T(8,128)S(1)}, f32[4,2,64,128]{3,2,1,0:T(8,128)S(1)}, u32[]{:S(2)}, u32[]{:S(2)}) collective-permute-start(f32[4,2,64,128]{3,2,1,0:T(8,128)S(1)} %collective-permute-done.5.refs_14_), channel_id=1, source_target_pairs={{0,1},{1,0},{2,3},{3,2},{4,5},{5,4},{6,7},{7,6},{8,9},{9,8},{10,11... | collective-permute-start | bytes 786440 | tf_op jit(solution)/shard_map/ppermute | solution.py:321
  35.0 2.6 %collective-permute-start.16 = (f32[4,2,64,128]{3,2,1,0:T(8,128)S(1)}, f32[4,2,64,128]{3,2,1,0:T(8,128)S(1)}, u32[]{:S(2)}, u32[]{:S(2)}) collective-permute-start(f32[4,2,64,128]{3,2,1,0:T(8,128)S(1)} %collective-permute-done.14.refs_15_), channel_id=1, source_target_pairs={{0,1},{1,0},{2,3},{3,2},{4,5},{5,4},{6,7},{7,6},{8,9},{9,8},{10,11... | collective-permute-start | bytes 786440 | tf_op jit(solution)/shard_map/ppermute | solution.py:321
  (3 other events, 8.2 us)

commit v3 on v2

--- a/solution.py
+++ b/solution.py
@@ -15,18 +15,11 @@
 VMEM = pltpu.VMEM
 SMEM = pltpu.SMEM
 BF16 = jnp.bfloat16
-XLAST = False
-ZDIRECT = 0
-HEAPCOST = 500000000
-PACKCOST = 2000000000
-FOLDCOST = 3000000000
-EDGES = [['ky', 'f5'], ['heap', 'r0'], ['kx', 'kc0'], ['pack', 'kc1']]
-COSTS = [4000000000, 6000000000, 2000000000, 1500000000]
-PREP = True
-PREPCOST = 5000000000
-TABLESAT = -1
-OPS = [('prep', []), ('pack', ['prep']), ('far', []), ('near', []), ('both', ['far']), ('heap', ['near', 'far', 'both']), ('kx', ['heap']), ('ky', ['heap']), ('kxy', ['kx']), ('kc0', ['heap']), ('kc1', ['kx']), ('kc2', ['ky']), ('kc3', ['kxy']), ('f1', ['pack']), ('f2', ['pack']), ('f3', ['pack']), ('f4', ['pack']), ('f5', ['pack']), ('f6', ['pack']), ('f7', ['pack']), ('r0', ['pack', 'f4']), ('r1', ['f1', 'f5']), ('r2', ['f2', 'f6']), ('r3', ['f3', 'f7'])]
-ROWCOST = 1024
+
+LITTLE = 1024
+PREPARE_COST = 5_000_000_000
+PACK_COST = 2_000_000_000
+ROW_COSTS = (4_000_000_000, 6_000_000_000, 2_000_000_000, 1_500_000_000)
 F32 = jnp.float32
 
 
@@ -97,7 +90,7 @@
         in_specs=[pl.BlockSpec(memory_space=VMEM)],
         out_specs=pl.BlockSpec(memory_space=VMEM),
         compiler_params=pltpu.CompilerParams(vmem_limit_bytes=16 << 20),
-        cost_estimate=pl.CostEstimate(flops=PREPCOST, bytes_accessed=1024, transcendentals=0),
+        cost_estimate=pl.CostEstimate(flops=PREPARE_COST, bytes_accessed=1024, transcendentals=0),
         name="prepare",
     )(owner_rank)
 
@@ -118,25 +111,25 @@
         in_specs=[pl.BlockSpec(memory_space=VMEM)] * 2,
         out_specs=[pl.BlockSpec(memory_space=VMEM)] * count,
         compiler_params=pltpu.CompilerParams(vmem_limit_bytes=16 << 20),
-        cost_estimate=pl.CostEstimate(flops=PACKCOST, bytes_accessed=1024, transcendentals=0),
+        cost_estimate=pl.CostEstimate(flops=PACK_COST, bytes_accessed=1024, transcendentals=0),
         name="pack",
     )(owner_rank, frames)
 
 
-def heap_kernel(*refs):
+def stack_kernel(*refs):
     for i, ref in enumerate(refs[:-1]):
         refs[-1][i] = ref[...]
 
 
-def heap(parts):
-    return pl.pallas_call(
-        heap_kernel,
+def stack(parts):
+    return pl.pallas_call(
+        stack_kernel,
         out_shape=jax.ShapeDtypeStruct((len(parts),) + parts[0].shape, F32),
         in_specs=[pl.BlockSpec(memory_space=VMEM)] * len(parts),
         out_specs=pl.BlockSpec(memory_space=VMEM),
         compiler_params=pltpu.CompilerParams(vmem_limit_bytes=8 << 20),
-        cost_estimate=pl.CostEstimate(flops=HEAPCOST, bytes_accessed=1024, transcendentals=0),
-        name="heap",
+        cost_estimate=pl.CostEstimate(flops=LITTLE, bytes_accessed=1024, transcendentals=0),
+        name="stack",
     )(*parts)
 
 
@@ -144,40 +137,36 @@
     return lax.dot_general(left, right, (((0,), (0,)), ((), ())), preferred_element_type=F32)
 
 
-def fold_tiles(scr, perm_ref, out_ref):
+def fold_half(value, table, out_ref, which, tile):
+    high, low = split(value)
+    both = turned(high, table) + turned(low, table)
+    for group in range(2):
+        out_ref[which, group, pl.ds(pl.multiple_of(tile * 128, 128), 128)] = both[:, group * 128 : (group + 1) * 128]
+
+
+def fold_pieces(quads, perm_ref, out_ref, held):
+    strip, group = lax.axis_index("strip"), lax.axis_index("frames")
+    for side in range(2):
+        upper = (strip // 4) ^ side
+        for t in range(4):
+            base = pl.multiple_of(((strip ^ t) % 4) * BLK, BLK)
+            held[side, t * BLK : (t + 1) * BLK] = perm_ref[upper, pl.ds(base, BLK)]
+        for df in range(4):
+            for part in range(2):
+                value = jnp.concatenate([quads[2 * df + t % 2][2 * side + t // 2, part] for t in range(4)], axis=0)
+                fold_half(value, held[side], out_ref, part + 2 * upper, group ^ df)
+
+
+def fold_whole(kern, perm_ref, out_ref, held):
     half = perm_ref.shape[1]
-    for part in range(2):
-        for tile in range(scr.shape[1]):
-            left, right = split(scr[part, tile, 0:half]), split(scr[part, tile, half:])
-            plus = turned(left[0], perm_ref[0]) + turned(left[1], perm_ref[0])
-            minus = turned(right[0], perm_ref[1]) + turned(right[1], perm_ref[1])
-            for group in range(2):
-                lanes = slice(group * 128, (group + 1) * 128)
-                out_ref[part, group, tile * 128 : (tile + 1) * 128] = plus[:, lanes]
-                out_ref[2 + part, group, tile * 128 : (tile + 1) * 128] = minus[:, lanes]
-
-
-def fold_pieces_kernel(*refs):
-    quads, perm_ref, out_ref, scr = refs[:8], refs[8], refs[9], refs[10]
-    strip, group = lax.axis_index("strip"), lax.axis_index("frames")
-    for df in range(4):
-        for dx in range(2):
-            for j in range(4):
-                base = pl.multiple_of((strip ^ (2 * j + dx)) * BLK, BLK)
-                for part in range(2):
-                    scr[part, group ^ df, pl.ds(base, BLK)] = quads[2 * df + dx][j, part]
-    fold_tiles(scr, perm_ref, out_ref)
-
-
-def fold_whole_kernel(kern_ref, perm_ref, out_ref, scr):
-    for part in range(2):
-        for tile in range(scr.shape[1]):
-            scr[part, tile] = kern_ref[part, :, tile * 128 : (tile + 1) * 128]
-    fold_tiles(scr, perm_ref, out_ref)
-
-
-def rows_kernel(split_strip, lower_ref, upper_ref, row_ref, *rest):
-    out_ref = rest[-1]
+    for side in range(2):
+        for part in range(2):
+            for tile in range(2 * half // 128):
+                value = kern[0][part, side * half : (side + 1) * half, tile * 128 : (tile + 1) * 128]
+                fold_half(value, perm_ref[side], out_ref, part + 2 * side, tile)
+
+
+def rows_kernel(split_strip, lower_ref, upper_ref, row_ref, out_ref):
     rows, half = lower_ref.shape[0], lower_ref.shape[1] // 2
     one, two = lower_ref[...], upper_ref[...]
     diff = one - two
@@ -192,28 +181,27 @@
                 out_ref[i, parity, :, group * half : (group + 1) * half] = part[parity * rows : (parity + 1) * rows]
 
 
-def row_spectra(lower, upper, table, split_strip, flops, before=()):
+def row_spectra(lower, upper, table, split_strip, flops):
     rows, detector = lower.shape
     return pl.pallas_call(
         functools.partial(rows_kernel, split_strip),
         out_shape=jax.ShapeDtypeStruct((2, 2, rows, detector), BF16),
-        in_specs=[pl.BlockSpec(memory_space=VMEM)] * (3 + len(before)),
+        in_specs=[pl.BlockSpec(memory_space=VMEM)] * 3,
         out_specs=pl.BlockSpec(memory_space=VMEM),
         compiler_params=pltpu.CompilerParams(vmem_limit_bytes=16 << 20),
         cost_estimate=pl.CostEstimate(flops=flops, bytes_accessed=1024, transcendentals=0),
         name="rows",
-    )(lower, upper, table, *before)
+    )(lower, upper, table)
 
 
 def correlate_kernel(pieces, fold_body, *refs):
-    tables, lists, refs = refs[:3], refs[3:6], refs[6:]
-    spectra, kern, perm_ref, out_ref = refs[:pieces], refs[pieces:-15], refs[-15], refs[-14]
-    scr, fold_ref, spec, img, blocks, col_ref, inv_ref, fin_ref, *scalars, sems, list_sems = refs[-13:]
-    loads = [pltpu.make_async_copy(x, y, sems.at[i]) for i, (x, y) in enumerate(zip(tables, (col_ref, inv_ref, fin_ref)))]
+    (col_ref, inv_ref, fin_ref), lists, refs = refs[:3], refs[3:6], refs[6:]
+    spectra, kern, perm_ref, out_ref = refs[:pieces], refs[pieces:-11], refs[-11], refs[-10]
+    held, fold_ref, spec, img, blocks, *scalars, list_sems = refs[-9:]
     copies = [pltpu.make_async_copy(x, y, list_sems.at[i]) for i, (x, y) in enumerate(zip(lists, scalars))]
-    for copy in loads + copies:
+    for copy in copies:
         copy.start()
-    fold_body(*kern, perm_ref, fold_ref, scr)
+    fold_body(kern, perm_ref, fold_ref, held)
     detector = fold_ref.shape[2]
     half, quarter = detector // 2, detector // 4
     me = lax.axis_index("strip")
@@ -224,8 +212,6 @@
 
     lane = lax.broadcasted_iota(jnp.int32, (half, quarter), 1)
     back = []
-    loads[0].wait()
-    loads[1].wait()
     for parity in range(2):
         table = (col_ref[0, parity], col_ref[1, parity])
         parts = []
@@ -255,7 +241,6 @@
         table = (inv_ref[0, parity], inv_ref[1, parity])
         back.append([dot3(table, part) for part in parts])
 
-    loads[2].wait()
     for upper in range(2):
         ends = []
         for group in range(2):
@@ -299,19 +284,19 @@
     return pl.pallas_call(
         functools.partial(correlate_kernel, len(spectra), fold_body),
         out_shape=jax.ShapeDtypeStruct((1, MAXB, BLK * BLK), F32),
-        in_specs=[pl.BlockSpec(memory_space=pl.ANY)] * 6
+        in_specs=[pl.BlockSpec(memory_space=VMEM)] * 3
+        + [pl.BlockSpec(memory_space=pl.ANY)] * 3
         + [pl.BlockSpec(memory_space=VMEM)] * (len(spectra) + len(kern) + 1),
         out_specs=pl.BlockSpec(memory_space=VMEM),
         scratch_shapes=[
-            VMEM((2, detector // 128, detector, 128), F32),
+            VMEM((2, half, half), BF16),
             VMEM((4, 2, detector, detector // 4), F32),
             VMEM((2, 2, half, detector), BF16),
             VMEM((detector // 128, detector, 128), F32),
             VMEM((MAXB * BLK // 2, 2 * BLK), F32),
         ]
-        + [VMEM(x.shape, BF16) for x in consts]
         + [SMEM(x.shape, jnp.int32) for x in (owner_rank, block_ids, block_counts)]
-        + [pltpu.SemaphoreType.DMA((3,)), pltpu.SemaphoreType.DMA((3,))],
+        + [pltpu.SemaphoreType.DMA((3,))],
         compiler_params=pltpu.CompilerParams(vmem_limit_bytes=48 << 20),
         name="correlate",
     )(*consts, owner_rank, block_ids, block_counts, *spectra, *kern, perm)
@@ -319,67 +304,46 @@
 
 def swap(value, axis, size, bits):
     return lax.ppermute(value, axis, [(i, i ^ bits) for i in range(size)])
+
+
+def after(value, *others):
+    return lax.optimization_barrier((value, others))[0]
+
+
+def gather_and_spread(owner_rank, frames, kernel):
+    piece = jnp.swapaxes(kernel, 1, 2)
+    blocks = pack(prepare(owner_rank), frames)
+    far = swap(piece, "strip", 8, 4)
+    near = swap(piece, "strip", 8, 2)
+    both = swap(far, "strip", 8, 2)
+    quad = stack([piece, near, far, both])
+    quad_x = swap(quad, "strip", 8, 1)
+    quad_y = swap(quad, "frames", 4, 2)
+    quad_xy = swap(quad_x, "frames", 4, 2)
+    quads = [quad, quad_x, quad_y, quad_xy]
+    sibling = [swap(after(quad, quad_x), "frames", 4, 1)]
+    sibling += [swap(q, "frames", 4, 1) for q in quads[1:]]
+    strips = [blocks[0]]
+    for j in range(1, 8):
+        strips.append(swap(after(blocks[j], quad_y) if j == 5 else blocks[j], "strip", 8, j))
+    strips[0], strips[4] = after((strips[0], strips[4]), quad)
+    return strips, [(sibling if df % 2 else quads)[2 * (df // 2) + dx] for df in range(4) for dx in range(2)]
 
 
 def shards(strip_size, group_size, frames, kernel, owner_rank, block_ids, block_counts):
     detector = frames.shape[2]
     row_table, *consts, perm = tables(detector)
     if strip_size == 8 and group_size == 4:
-        piece = jnp.swapaxes(kernel, 1, 2)
-        needs = dict(OPS)
-        val, order = {}, []
-
-        def visit(name):
-            if name in val:
-                return
-            deps = needs[name] + [a for a, b in EDGES if b == name]
-            for d in deps:
-                visit(d)
-
-            def tied(value):
-                extra = [val[a] for a, b in EDGES if b == name]
-                return lax.optimization_barrier((value, extra))[0] if extra else value
-
-            natural = [val[d] for d in needs[name]]
-            if name == "pack":
-                val[name] = pack(tied(natural[0] if natural else owner_rank), frames)
-            elif name == "prep":
-                val[name] = prepare(tied(owner_rank))
-            elif name == "far":
-                val[name] = swap(tied(piece), "strip", 8, 4)
-            elif name == "near":
-                val[name] = swap(tied(piece), "strip", 8, 2)
-            elif name == "both":
-                val[name] = swap(tied(natural[0] if natural else piece), "strip", 8, {0: 2, 1: 6, 2: 4}[ZDIRECT])
-            elif name == "heap":
-                val[name] = heap([piece] + tied(natural))
-            elif name in ("kx", "kxy") and not (name == "kxy" and not XLAST):
-                val[name] = swap(tied(natural[0]), "strip", 8, 1)
-            elif name in ("ky", "kxy"):
-                val[name] = swap(tied(natural[0]), "frames", 4, 2)
-            elif name[:2] == "kc":
-                val[name] = swap(tied(natural[0]), "frames", 4, 1)
-            elif name[0] == "f":
-                val[name] = swap(tied(natural[0][int(name[1])]), "strip", 8, int(name[1]))
-            elif name[0] == "r":
-                j = int(name[1])
-                low = natural[0][0] if j == 0 else natural[0]
-                low, high = tied((low, natural[-1]))
-                val[name] = row_spectra(low, high, row_table, 4, COSTS[j], consts if TABLESAT == j else ())
-
-        for name in needs:
-            visit(name)
-        quads = [val["heap"], val["kx"], val["ky"], val["kxy"]] + [val["kc%d" % i] for i in range(4)]
-        kern = [quads[4 * (df % 2) + 2 * (df // 2) + dx] for df in range(4) for dx in range(2)]
-        fold_body = fold_pieces_kernel
-        spectra = [val["r%d" % j] for j in range(4)]
+        strips, kern = gather_and_spread(owner_rank, frames, kernel)
+        spectra = [row_spectra(strips[j], strips[j + 4], row_table, 4, ROW_COSTS[j]) for j in range(4)]
+        fold_body = fold_pieces
     else:
         places = jnp.argsort(owner_rank.reshape(-1))
         frame = lax.all_to_all(frames[places], "strip", split_axis=0, concat_axis=1, tiled=True)[0]
         whole = lax.all_gather(kernel, "strip", axis=2, tiled=True)
         whole = lax.all_gather(whole, "frames", axis=1, tiled=True)
-        fold_body, kern = fold_whole_kernel, [jnp.swapaxes(whole, 1, 2)]
-        spectra = [row_spectra(frame[: detector // 2], frame[detector // 2 :], row_table, 0, ROWCOST)]
+        fold_body, kern = fold_whole, [jnp.swapaxes(whole, 1, 2)]
+        spectra = [row_spectra(frame[: detector // 2], frame[detector // 2 :], row_table, 0, LITTLE)]
     return correlate(owner_rank, block_ids, block_counts, spectra, fold_body, kern, perm, consts)
 
 

time: 43.1 us -> 42.6 us (0.988)
  Pallas kernels: 6.72 us -> 6.16 us
    pallas_call x1, Pallas kernels: 5.33 us -> 4.77 us  [correlate(): pl.pallas_call(functools.partial(correlate_kernel, len(spectra), fold_bod...]
where the time goes in v3:
time: 42.6 us; the launch traced here: 42.4 us
  starting transfers between devices  27.4 us (64%)
  waiting for transfers between devices  8.52 us (20%)
  Pallas kernels  6.16 us (14%)
    ppermute x17, starting transfers between devices, swap(): return lax.ppermute(value, axis, [(i, i ^ bits) for i in range(size)])  27.4 us
    ppermute x17, waiting for transfers between devices, swap(): return lax.ppermute(value, axis, [(i, i ^ bits) for i in range(size)])  8.52 us
    pallas_call x1, Pallas kernels, correlate(): pl.pallas_call(functools.partial(correlate_kernel, len(spectra), fold_bod...  4.77 us
    pallas_call x4, Pallas kernels, row_spectra(): pl.pallas_call(functools.partial(rows_kernel, split_strip), out_shape=jax...  1.16 us
  transfers between devices with their start and end apart: 17, of which 4 were waited for; matrix products, arithmetic and copies ran while one was open for 0% of the time, Pallas kernels for 3%

profile of v3, /device:TPU:0, one launch (start us, length us, event | category | flops | bytes accessed | tf_op | source)
XLA Modules:
  0.0 42.4 jit_solution(13661342741362108724)
XLA Ops:
  0.0 4.0 %collective-permute-start.2 = (f32[2,64,128]{2,1,0:T(8,128)}, f32[2,64,128]{2,1,0:T(8,128)S(1)}, u32[]{:S(2)}, u32[]{:S(2)}) collective-permute-start(f32[2,64,128]{2,1,0:T(8,128)} %bitcast.1), channel_id=1, source_target_pairs={{0,16},{4,20},{8,24},{12,28},{16,0},{20,4},{24,8},{28,12},{1,17},{... | collective-permute-start | bytes 196616 | tf_op jit(solution)/shard_map/ppermute | solution.py:306
  4.1 0.2 pack.1
  4.3 1.3 %collective-permute-start = (f32[64,512]{1,0:T(8,128)S(1)}, f32[64,512]{1,0:T(8,128)S(1)}, u32[]{:S(2)}, u32[]{:S(2)}) collective-permute-start(f32[64,512]{1,0:T(8,128)S(1)} %get-tuple-element.18), channel_id=1, source_target_pairs={{0,16},{4,20},{8,24},{12,28},{16,0},{20,4},{24,8},{28,12},{1,17},{... | collective-permute-start | bytes 393224 | tf_op jit(solution)/shard_map/ppermute | solution.py:306
  5.6 1.6 %collective-permute-start.1 = (f32[2,64,128]{2,1,0:T(8,128)S(1)}, f32[2,64,128]{2,1,0:T(8,128)S(1)}, u32[]{:S(2)}, u32[]{:S(2)}) collective-permute-start(f32[2,64,128]{2,1,0:T(8,128)S(1)} %bitcast.2), channel_id=1, source_target_pairs={{0,8},{4,12},{8,0},{12,4},{16,24},{20,28},{24,16},{28,20},{1,9},{5... | collective-permute-start | bytes 196616 | tf_op jit(solution)/shard_map/ppermute | solution.py:306
  7.1 0.9 %collective-permute-done.2.refs_2_ = f32[2,64,128]{2,1,0:T(8,128)S(1)} collective-permute-done((f32[2,64,128]{2,1,0:T(8,128)}, f32[2,64,128]{2,1,0:T(8,128)S(1)}, u32[]{:S(2)}, u32[]{:S(2)}) %collective-permute-start.2) | collective-permute-done | bytes 65568 | tf_op jit(solution)/shard_map/ppermute | solution.py:306
  8.0 3.8 %collective-permute-start.3 = (f32[2,64,128]{2,1,0:T(8,128)S(1)}, f32[2,64,128]{2,1,0:T(8,128)S(1)}, u32[]{:S(2)}, u32[]{:S(2)}) collective-permute-start(f32[2,64,128]{2,1,0:T(8,128)S(1)} %collective-permute-done.2.refs_2_), channel_id=1, source_target_pairs={{0,8},{4,12},{8,0},{12,4},{16,24},{20,28},{24,16},{28,20},{1,9},{5... | collective-permute-start | bytes 196616 | tf_op jit(solution)/shard_map/ppermute | solution.py:306
  11.8 1.5 %collective-permute-start.4 = (f32[64,512]{1,0:T(8,128)S(1)}, f32[64,512]{1,0:T(8,128)S(1)}, u32[]{:S(2)}, u32[]{:S(2)}) collective-permute-start(f32[64,512]{1,0:T(8,128)S(1)} %get-tuple-element.21), channel_id=1, source_target_pairs={{0,4},{4,0},{8,12},{12,8},{16,20},{20,16},{24,28},{28,24},{1,5},{5... | collective-permute-start | bytes 393224 | tf_op jit(solution)/shard_map/ppermute | solution.py:306
  13.3 4.7 %collective-permute-start.8 = (f32[64,512]{1,0:T(8,128)S(1)}, f32[64,512]{1,0:T(8,128)S(1)}, u32[]{:S(2)}, u32[]{:S(2)}) collective-permute-start(f32[64,512]{1,0:T(8,128)S(1)} %get-tuple-element.25), channel_id=1, source_target_pairs={{0,24},{4,28},{8,16},{12,20},{16,8},{20,12},{24,0},{28,4},{1,25},{... | collective-permute-start | bytes 393224 | tf_op jit(solution)/shard_map/ppermute | solution.py:306
  18.1 0.6 %collective-permute-start.11 = (f32[4,2,64,128]{3,2,1,0:T(8,128)S(1)}, f32[4,2,64,128]{3,2,1,0:T(8,128)S(1)}, u32[]{:S(2)}, u32[]{:S(2)}) collective-permute-start(f32[4,2,64,128]{3,2,1,0:T(8,128)S(1)} %stack.1.refs_10_), channel_id=1, source_target_pairs={{0,4},{4,0},{8,12},{12,8},{16,20},{20,16},{24,28},{28,24},{1,5},{5... | collective-permute-start | bytes 786440 | tf_op jit(solution)/shard_map/ppermute | solution.py:306
  18.7 1.5 %collective-permute-start.5 = (f32[4,2,64,128]{3,2,1,0:T(8,128)S(1)}, f32[4,2,64,128]{3,2,1,0:T(8,128)S(1)}, u32[]{:S(2)}, u32[]{:S(2)}) collective-permute-start(f32[4,2,64,128]{3,2,1,0:T(8,128)S(1)} %stack.1.refs_10_), channel_id=1, source_target_pairs={{0,2},{1,3},{2,0},{3,1},{4,6},{5,7},{6,4},{7,5},{8,10},{9,11},{10,... | collective-permute-start | bytes 786440 | tf_op jit(solution)/shard_map/ppermute | solution.py:306
  20.2 0.3 rows.4.refs_6_
  20.5 0.1 collective-permute-start.9
  20.6 3.2 %collective-permute-done.8.upper_ref = f32[64,512]{1,0:T(8,128)S(1)} collective-permute-done((f32[64,512]{1,0:T(8,128)S(1)}, f32[64,512]{1,0:T(8,128)S(1)}, u32[]{:S(2)}, u32[]{:S(2)}) %collective-permute-start.8) | collective-permute-done | bytes 131104 | tf_op jit(solution)/shard_map/ppermute | solution.py:306
  23.8 2.2 %collective-permute-start.10 = (f32[64,512]{1,0:T(8,128)S(1)}, f32[64,512]{1,0:T(8,128)S(1)}, u32[]{:S(2)}, u32[]{:S(2)}) collective-permute-start(f32[64,512]{1,0:T(8,128)S(1)} %get-tuple-element.27), channel_id=1, source_target_pairs={{0,28},{4,24},{8,20},{12,16},{16,12},{20,8},{24,4},{28,0},{1,29},{... | collective-permute-start | bytes 393224 | tf_op jit(solution)/shard_map/ppermute | solution.py:306
  26.0 2.6 %collective-permute-done.11.refs_11_ = f32[4,2,64,128]{3,2,1,0:T(8,128)S(1)} collective-permute-done((f32[4,2,64,128]{3,2,1,0:T(8,128)S(1)}, f32[4,2,64,128]{3,2,1,0:T(8,128)S(1)}, u32[]{:S(2)}, u32[]{:S(2)}) %collective-permute-start.11) | collective-permute-done | bytes 262176 | tf_op jit(solution)/shard_map/ppermute | solution.py:306
  28.6 1.5 %collective-permute-start.14 = (f32[4,2,64,128]{3,2,1,0:T(8,128)S(1)}, f32[4,2,64,128]{3,2,1,0:T(8,128)S(1)}, u32[]{:S(2)}, u32[]{:S(2)}) collective-permute-start(f32[4,2,64,128]{3,2,1,0:T(8,128)S(1)} %collective-permute-done.11.refs_11_), channel_id=1, source_target_pairs={{0,2},{1,3},{2,0},{3,1},{4,6},{5,7},{6,4},{7,5},{8,10},{9,11},{10,... | collective-permute-start | bytes 786440 | tf_op jit(solution)/shard_map/ppermute | solution.py:306
  30.1 0.3 rows.6.refs_8_
  30.4 3.5 %collective-permute-start.6 = (f32[64,512]{1,0:T(8,128)S(1)}, f32[64,512]{1,0:T(8,128)S(1)}, u32[]{:S(2)}, u32[]{:S(2)}) collective-permute-start(f32[64,512]{1,0:T(8,128)S(1)} %get-tuple-element.23), channel_id=1, source_target_pairs={{0,20},{4,16},{8,28},{12,24},{16,4},{20,0},{24,12},{28,8},{1,21},{... | collective-permute-start | bytes 393224 | tf_op jit(solution)/shard_map/ppermute | solution.py:306
  33.9 0.3 rows.7.refs_9_
  34.4 0.5 %collective-permute-start.13 = (f32[4,2,64,128]{3,2,1,0:T(8,128)S(1)}, f32[4,2,64,128]{3,2,1,0:T(8,128)S(1)}, u32[]{:S(2)}, u32[]{:S(2)}) collective-permute-start(f32[4,2,64,128]{3,2,1,0:T(8,128)S(1)} %collective-permute-done.11.refs_11_), channel_id=1, source_target_pairs={{0,1},{1,0},{2,3},{3,2},{4,5},{5,4},{6,7},{7,6},{8,9},{9,8},{10,11... | collective-permute-start | bytes 786440 | tf_op jit(solution)/shard_map/ppermute | solution.py:306
  35.0 0.4 %collective-permute-start.16 = (f32[4,2,64,128]{3,2,1,0:T(8,128)S(1)}, f32[4,2,64,128]{3,2,1,0:T(8,128)S(1)}, u32[]{:S(2)}, u32[]{:S(2)}) collective-permute-start(f32[4,2,64,128]{3,2,1,0:T(8,128)S(1)} %collective-permute-done.14.refs_15_), channel_id=1, source_target_pairs={{0,1},{1,0},{2,3},{3,2},{4,5},{5,4},{6,7},{7,6},{8,9},{9,8},{10,11... | collective-permute-start | bytes 786440 | tf_op jit(solution)/shard_map/ppermute | solution.py:306
  35.4 1.8 %collective-permute-done.6.upper_ref = f32[64,512]{1,0:T(8,128)S(1)} collective-permute-done((f32[64,512]{1,0:T(8,128)S(1)}, f32[64,512]{1,0:T(8,128)S(1)}, u32[]{:S(2)}, u32[]{:S(2)}) %collective-permute-start.6) | collective-permute-done | bytes 131104 | tf_op jit(solution)/shard_map/ppermute | solution.py:306
  37.2 0.3 rows.5.refs_7_
  37.6 4.8 %correlate.1 = f32[1,16,4096]{2,1,0:T(8,128)} custom-call(bf16[2,2,512,256]{3,2,1,0:T(8,128)(2,1)S(1)} %copy-done.1, bf16[2,2,256,512]{3,2,1,0:T(8,128)(2,1)S(1)} %copy-done, bf16[2,2,256,256]{3,2,1,0:T(8,128)(2,1)S(1)} %copy-done.2, s32[1,8]{1,0:T(1,128)S(1)} %copy-done.6, s32[8,16]{1,0:T(8,128)S(1)} %copy-done.5, s32[8]{0:T(128)S(1)} %copy-done.7, ...), custom_call_target="tpu_custom_call" | custom-call | tf_op jit(solution)/shard_map/correlate/pallas_call | solution.py:284
  (38 shorter events, 0.3 us)
Async XLA Ops:
  0.0 4.0 %copy-start.6 = (s32[1,8]{1,0:T(1,128)S(1)}, s32[1,8]{1,0:T(1,128)}, u32[]{:S(2)}) copy-start(s32[1,8]{1,0:T(1,128)} %refs_3_.1) | copy-start | bytes 100
  0.0 4.0 %copy-start.8 = (f32[8,64,512]{2,1,0:T(8,128)S(1)}, f32[8,64,512]{2,1,0:T(8,128)}, u32[]{:S(2)}) copy-start(f32[8,64,512]{2,1,0:T(8,128)} %frames_ref.1) | copy-start | bytes 3145732
  0.0 8.0 %collective-permute-start.2 = (f32[2,64,128]{2,1,0:T(8,128)}, f32[2,64,128]{2,1,0:T(8,128)S(1)}, u32[]{:S(2)}, u32[]{:S(2)}) collective-permute-start(f32[2,64,128]{2,1,0:T(8,128)} %bitcast.1), channel_id=1, source_target_pairs={{0,16},{4,20},{8,24},{12,28},{16,0},{20,4},{24,8},{28,12},{1,17},{... | collective-permute-start | bytes 196616 | tf_op jit(solution)/shard_map/ppermute | solution.py:306
  4.3 15.9 %copy-start.9 = (bf16[2,2,256,256]{3,2,1,0:T(8,128)(2,1)S(1)}, bf16[2,2,256,256]{3,2,1,0:T(8,128)(2,1)}, u32[]{:S(2)}) copy-start(bf16[2,2,256,256]{3,2,1,0:T(8,128)(2,1)} %constant.10.clone.row_ref) | copy-start | bytes 1572868
  4.3 14.4 %collective-permute-start = (f32[64,512]{1,0:T(8,128)S(1)}, f32[64,512]{1,0:T(8,128)S(1)}, u32[]{:S(2)}, u32[]{:S(2)}) collective-permute-start(f32[64,512]{1,0:T(8,128)S(1)} %get-tuple-element.18), channel_id=1, source_target_pairs={{0,16},{4,20},{8,24},{12,28},{16,0},{20,4},{24,8},{28,12},{1,17},{... | collective-permute-start | bytes 393224 | tf_op jit(solution)/shard_map/ppermute | solution.py:306
  5.6 7.8 %collective-permute-start.1 = (f32[2,64,128]{2,1,0:T(8,128)S(1)}, f32[2,64,128]{2,1,0:T(8,128)S(1)}, u32[]{:S(2)}, u32[]{:S(2)}) collective-permute-start(f32[2,64,128]{2,1,0:T(8,128)S(1)} %bitcast.2), channel_id=1, source_target_pairs={{0,8},{4,12},{8,0},{12,4},{16,24},{20,28},{24,16},{28,20},{1,9},{5... | collective-permute-start | bytes 196616 | tf_op jit(solution)/shard_map/ppermute | solution.py:306
  8.0 10.1 %collective-permute-start.3 = (f32[2,64,128]{2,1,0:T(8,128)S(1)}, f32[2,64,128]{2,1,0:T(8,128)S(1)}, u32[]{:S(2)}, u32[]{:S(2)}) collective-permute-start(f32[2,64,128]{2,1,0:T(8,128)S(1)} %collective-permute-done.2.refs_2_), channel_id=1, source_target_pairs={{0,8},{4,12},{8,0},{12,4},{16,24},{20,28},{24,16},{28,20},{1,9},{5... | collective-permute-start | bytes 196616 | tf_op jit(solution)/shard_map/ppermute | solution.py:306
  11.8 23.1 %collective-permute-start.4 = (f32[64,512]{1,0:T(8,128)S(1)}, f32[64,512]{1,0:T(8,128)S(1)}, u32[]{:S(2)}, u32[]{:S(2)}) collective-permute-start(f32[64,512]{1,0:T(8,128)S(1)} %get-tuple-element.21), channel_id=1, source_target_pairs={{0,4},{4,0},{8,12},{12,8},{16,20},{20,16},{24,28},{28,24},{1,5},{5... | collective-permute-start | bytes 393224 | tf_op jit(solution)/shard_map/ppermute | solution.py:306
  13.3 7.2 %collective-permute-start.7 = (f32[64,512]{1,0:T(8,128)S(1)}, f32[64,512]{1,0:T(8,128)S(1)}, u32[]{:S(2)}, u32[]{:S(2)}) collective-permute-start(f32[64,512]{1,0:T(8,128)S(1)} %get-tuple-element.24), channel_id=1, source_target_pairs={{0,8},{4,12},{8,0},{12,4},{16,24},{20,28},{24,16},{28,20},{1,9},{5... | collective-permute-start | bytes 393224 | tf_op jit(solution)/shard_map/ppermute | solution.py:306
  13.3 10.5 %collective-permute-start.8 = (f32[64,512]{1,0:T(8,128)S(1)}, f32[64,512]{1,0:T(8,128)S(1)}, u32[]{:S(2)}, u32[]{:S(2)}) collective-permute-start(f32[64,512]{1,0:T(8,128)S(1)} %get-tuple-element.25), channel_id=1, source_target_pairs={{0,24},{4,28},{8,16},{12,20},{16,8},{20,12},{24,0},{28,4},{1,25},{... | collective-permute-start | bytes 393224 | tf_op jit(solution)/shard_map/ppermute | solution.py:306
  18.1 10.5 %collective-permute-start.11 = (f32[4,2,64,128]{3,2,1,0:T(8,128)S(1)}, f32[4,2,64,128]{3,2,1,0:T(8,128)S(1)}, u32[]{:S(2)}, u32[]{:S(2)}) collective-permute-start(f32[4,2,64,128]{3,2,1,0:T(8,128)S(1)} %stack.1.refs_10_), channel_id=1, source_target_pairs={{0,4},{4,0},{8,12},{12,8},{16,20},{20,16},{24,28},{28,24},{1,5},{5... | collective-permute-start | bytes 786440 | tf_op jit(solution)/shard_map/ppermute | solution.py:306
  18.7 11.7 %collective-permute-start.5 = (f32[4,2,64,128]{3,2,1,0:T(8,128)S(1)}, f32[4,2,64,128]{3,2,1,0:T(8,128)S(1)}, u32[]{:S(2)}, u32[]{:S(2)}) collective-permute-start(f32[4,2,64,128]{3,2,1,0:T(8,128)S(1)} %stack.1.refs_10_), channel_id=1, source_target_pairs={{0,2},{1,3},{2,0},{3,1},{4,6},{5,7},{6,4},{7,5},{8,10},{9,11},{10,... | collective-permute-start | bytes 786440 | tf_op jit(solution)/shard_map/ppermute | solution.py:306
  20.5 13.4 %collective-permute-start.9 = (f32[64,512]{1,0:T(8,128)S(1)}, f32[64,512]{1,0:T(8,128)S(1)}, u32[]{:S(2)}, u32[]{:S(2)}) collective-permute-start(f32[64,512]{1,0:T(8,128)S(1)} %get-tuple-element.26), channel_id=1, source_target_pairs={{0,12},{4,8},{8,4},{12,0},{16,28},{20,24},{24,20},{28,16},{1,13},{... | collective-permute-start | bytes 393224 | tf_op jit(solution)/shard_map/ppermute | solution.py:306
  23.8 10.1 %collective-permute-start.10 = (f32[64,512]{1,0:T(8,128)S(1)}, f32[64,512]{1,0:T(8,128)S(1)}, u32[]{:S(2)}, u32[]{:S(2)}) collective-permute-start(f32[64,512]{1,0:T(8,128)S(1)} %get-tuple-element.27), channel_id=1, source_target_pairs={{0,28},{4,24},{8,20},{12,16},{16,12},{20,8},{24,4},{28,0},{1,29},{... | collective-permute-start | bytes 393224 | tf_op jit(solution)/shard_map/ppermute | solution.py:306
  28.6 6.4 %collective-permute-start.14 = (f32[4,2,64,128]{3,2,1,0:T(8,128)S(1)}, f32[4,2,64,128]{3,2,1,0:T(8,128)S(1)}, u32[]{:S(2)}, u32[]{:S(2)}) collective-permute-start(f32[4,2,64,128]{3,2,1,0:T(8,128)S(1)} %collective-permute-done.11.refs_11_), channel_id=1, source_target_pairs={{0,2},{1,3},{2,0},{3,1},{4,6},{5,7},{6,4},{7,5},{8,10},{9,11},{10,... | collective-permute-start | bytes 786440 | tf_op jit(solution)/shard_map/ppermute | solution.py:306
  30.4 6.8 %collective-permute-start.6 = (f32[64,512]{1,0:T(8,128)S(1)}, f32[64,512]{1,0:T(8,128)S(1)}, u32[]{:S(2)}, u32[]{:S(2)}) collective-permute-start(f32[64,512]{1,0:T(8,128)S(1)} %get-tuple-element.23), channel_id=1, source_target_pairs={{0,20},{4,16},{8,28},{12,24},{16,4},{20,0},{24,12},{28,8},{1,21},{... | collective-permute-start | bytes 393224 | tf_op jit(solution)/shard_map/ppermute | solution.py:306
  34.2 3.3 %copy-start = (bf16[2,2,256,512]{3,2,1,0:T(8,128)(2,1)S(1)}, bf16[2,2,256,512]{3,2,1,0:T(8,128)(2,1)}, u32[]{:S(2)}) copy-start(bf16[2,2,256,512]{3,2,1,0:T(8,128)(2,1)} %constant.12.clone.refs_1_) | copy-start | bytes 3145732
  34.2 3.3 %copy-start.1 = (bf16[2,2,512,256]{3,2,1,0:T(8,128)(2,1)S(1)}, bf16[2,2,512,256]{3,2,1,0:T(8,128)(2,1)}, u32[]{:S(2)}) copy-start(bf16[2,2,512,256]{3,2,1,0:T(8,128)(2,1)} %constant.11.clone.refs_0_) | copy-start | bytes 3145732
  34.3 3.3 %copy-start.2 = (bf16[2,2,256,256]{3,2,1,0:T(8,128)(2,1)S(1)}, bf16[2,2,256,256]{3,2,1,0:T(8,128)(2,1)}, u32[]{:S(2)}) copy-start(bf16[2,2,256,256]{3,2,1,0:T(8,128)(2,1)} %constant.13.clone.refs_2_) | copy-start | bytes 1572868
  34.3 3.3 %copy-start.3 = (bf16[2,256,256]{2,1,0:T(8,128)(2,1)S(1)}, bf16[2,256,256]{2,1,0:T(8,128)(2,1)}, u32[]{:S(2)}) copy-start(bf16[2,256,256]{2,1,0:T(8,128)(2,1)} %constant.14.clone.refs_18_) | copy-start | bytes 786436
  34.3 3.2 %collective-permute-start.12 = (f32[4,2,64,128]{3,2,1,0:T(8,128)S(1)}, f32[4,2,64,128]{3,2,1,0:T(8,128)S(1)}, u32[]{:S(2)}, u32[]{:S(2)}) collective-permute-start(f32[4,2,64,128]{3,2,1,0:T(8,128)S(1)} %stack.1.refs_10_), channel_id=1, source_target_pairs={{0,1},{1,0},{2,3},{3,2},{4,5},{5,4},{6,7},{7,6},{8,9},{9,8},{10,11... | collective-permute-start | bytes 786440 | tf_op jit(solution)/shard_map/ppermute | solution.py:306
  34.4 3.2 %collective-permute-start.13 = (f32[4,2,64,128]{3,2,1,0:T(8,128)S(1)}, f32[4,2,64,128]{3,2,1,0:T(8,128)S(1)}, u32[]{:S(2)}, u32[]{:S(2)}) collective-permute-start(f32[4,2,64,128]{3,2,1,0:T(8,128)S(1)} %collective-permute-done.11.refs_11_), channel_id=1, source_target_pairs={{0,1},{1,0},{2,3},{3,2},{4,5},{5,4},{6,7},{7,6},{8,9},{9,8},{10,11... | collective-permute-start | bytes 786440 | tf_op jit(solution)/shard_map/ppermute | solution.py:306
  34.9 2.7 %collective-permute-start.15 = (f32[4,2,64,128]{3,2,1,0:T(8,128)S(1)}, f32[4,2,64,128]{3,2,1,0:T(8,128)S(1)}, u32[]{:S(2)}, u32[]{:S(2)}) collective-permute-start(f32[4,2,64,128]{3,2,1,0:T(8,128)S(1)} %collective-permute-done.5.refs_14_), channel_id=1, source_target_pairs={{0,1},{1,0},{2,3},{3,2},{4,5},{5,4},{6,7},{7,6},{8,9},{9,8},{10,11... | collective-permute-start | bytes 786440 | tf_op jit(solution)/shard_map/ppermute | solution.py:306
  35.0 2.6 %collective-permute-start.16 = (f32[4,2,64,128]{3,2,1,0:T(8,128)S(1)}, f32[4,2,64,128]{3,2,1,0:T(8,128)S(1)}, u32[]{:S(2)}, u32[]{:S(2)}) collective-permute-start(f32[4,2,64,128]{3,2,1,0:T(8,128)S(1)} %collective-permute-done.14.refs_15_), channel_id=1, source_target_pairs={{0,1},{1,0},{2,3},{3,2},{4,5},{5,4},{6,7},{7,6},{8,9},{9,8},{10,11... | collective-permute-start | bytes 786440 | tf_op jit(solution)/shard_map/ppermute | solution.py:306
  (3 other events, 8.2 us)

commit v4 on v3

--- a/solution.py
+++ b/solution.py
@@ -18,8 +18,8 @@
 
 LITTLE = 1024
 PREPARE_COST = 5_000_000_000
-PACK_COST = 2_000_000_000
-ROW_COSTS = (4_000_000_000, 6_000_000_000, 2_000_000_000, 1_500_000_000)
+STACK_COST = 2_000_000_000
+ROW_COSTS = (4_000_000_000, 6_000_000_000, 1_000_000_000, 1_500_000_000)
 F32 = jnp.float32
 
 
@@ -111,7 +111,7 @@
         in_specs=[pl.BlockSpec(memory_space=VMEM)] * 2,
         out_specs=[pl.BlockSpec(memory_space=VMEM)] * count,
         compiler_params=pltpu.CompilerParams(vmem_limit_bytes=16 << 20),
-        cost_estimate=pl.CostEstimate(flops=PACK_COST, bytes_accessed=1024, transcendentals=0),
+        cost_estimate=pl.CostEstimate(flops=LITTLE, bytes_accessed=1024, transcendentals=0),
         name="pack",
     )(owner_rank, frames)
 
@@ -128,7 +128,7 @@
         in_specs=[pl.BlockSpec(memory_space=VMEM)] * len(parts),
         out_specs=pl.BlockSpec(memory_space=VMEM),
         compiler_params=pltpu.CompilerParams(vmem_limit_bytes=8 << 20),
-        cost_estimate=pl.CostEstimate(flops=LITTLE, bytes_accessed=1024, transcendentals=0),
+        cost_estimate=pl.CostEstimate(flops=STACK_COST, bytes_accessed=1024, transcendentals=0),
         name="stack",
     )(*parts)
 
@@ -313,20 +313,28 @@
 def gather_and_spread(owner_rank, frames, kernel):
     piece = jnp.swapaxes(kernel, 1, 2)
     blocks = pack(prepare(owner_rank), frames)
+    strips = [blocks[0]] + [None] * 7
+
+    def send(j, *others):
+        strips[j] = swap(after(blocks[j], *others) if others else blocks[j], "strip", 8, j)
+
     far = swap(piece, "strip", 8, 4)
     near = swap(piece, "strip", 8, 2)
-    both = swap(far, "strip", 8, 2)
-    quad = stack([piece, near, far, both])
+    across = swap(piece, "strip", 8, 6)
+    quad = stack([piece, near, far, across])
     quad_x = swap(quad, "strip", 8, 1)
-    quad_y = swap(quad, "frames", 4, 2)
+    send(7)
+    quad_y = swap(after(quad, strips[7]), "frames", 4, 2)
     quad_xy = swap(quad_x, "frames", 4, 2)
     quads = [quad, quad_x, quad_y, quad_xy]
     sibling = [swap(after(quad, quad_x), "frames", 4, 1)]
     sibling += [swap(q, "frames", 4, 1) for q in quads[1:]]
-    strips = [blocks[0]]
-    for j in range(1, 8):
-        strips.append(swap(after(blocks[j], quad_y) if j == 5 else blocks[j], "strip", 8, j))
-    strips[0], strips[4] = after((strips[0], strips[4]), quad)
+    send(1)
+    send(2)
+    send(3)
+    send(4, far)
+    send(5, quad_y)
+    send(6)
     return strips, [(sibling if df % 2 else quads)[2 * (df // 2) + dx] for df in range(4) for dx in range(2)]
 
 

time: 42.6 us -> 40.5 us (0.951)
  starting transfers between devices: 27.4 us -> 25.7 us
    ppermute x17, starting transfers between devices: 27.4 us -> 25.7 us  [swap(): return lax.ppermute(value, axis, [(i, i ^ bits) for i in range(size)])]
  transfers between devices with their start and end apart: 17 -> 17, of which waited for: 4 -> 5; matrix products, arithmetic and copies ran while one was open for 0% -> 0% of each run, Pallas kernels for 3% -> 3%
where the time goes in v4:
time: 40.5 us; the launch traced here: 40.3 us
  starting transfers between devices  25.7 us (63%)
  waiting for transfers between devices  8.18 us (20%)
  Pallas kernels  6.17 us (15%)
    ppermute x17, starting transfers between devices, swap(): return lax.ppermute(value, axis, [(i, i ^ bits) for i in range(size)])  25.7 us
    ppermute x17, waiting for transfers between devices, swap(): return lax.ppermute(value, axis, [(i, i ^ bits) for i in range(size)])  8.18 us
    pallas_call x1, Pallas kernels, correlate(): pl.pallas_call(functools.partial(correlate_kernel, len(spectra), fold_bod...  4.78 us
    pallas_call x4, Pallas kernels, row_spectra(): pl.pallas_call(functools.partial(rows_kernel, split_strip), out_shape=jax...  1.16 us
  transfers between devices with their start and end apart: 17, of which 5 were waited for; matrix products, arithmetic and copies ran while one was open for 0% of the time, Pallas kernels for 3%

profile of v4, /device:TPU:0, one launch (start us, length us, event | category | flops | bytes accessed | tf_op | source)
XLA Modules:
  0.0 40.3 jit_solution(17727406974107471828)
XLA Ops:
  0.0 5.0 %collective-permute-start.4 = (f32[2,64,128]{2,1,0:T(8,128)}, f32[2,64,128]{2,1,0:T(8,128)S(1)}, u32[]{:S(2)}, u32[]{:S(2)}) collective-permute-start(f32[2,64,128]{2,1,0:T(8,128)} %bitcast.1), channel_id=1, source_target_pairs={{0,24},{4,28},{8,16},{12,20},{16,8},{20,12},{24,0},{28,4},{1,25},{... | collective-permute-start | bytes 196616 | tf_op jit(solution)/shard_map/ppermute | solution.py:306
  5.1 0.6 %collective-permute-start = (f32[2,64,128]{2,1,0:T(8,128)}, f32[2,64,128]{2,1,0:T(8,128)S(1)}, u32[]{:S(2)}, u32[]{:S(2)}) collective-permute-start(f32[2,64,128]{2,1,0:T(8,128)} %bitcast.3), channel_id=1, source_target_pairs={{0,16},{4,20},{8,24},{12,28},{16,0},{20,4},{24,8},{28,12},{1,17},{... | collective-permute-start | bytes 196616 | tf_op jit(solution)/shard_map/ppermute | solution.py:306
  5.7 0.2 pack.1
  5.9 4.7 %collective-permute-start.5 = (f32[64,512]{1,0:T(8,128)S(1)}, f32[64,512]{1,0:T(8,128)S(1)}, u32[]{:S(2)}, u32[]{:S(2)}) collective-permute-start(f32[64,512]{1,0:T(8,128)S(1)} %get-tuple-element.22), channel_id=1, source_target_pairs={{0,28},{4,24},{8,20},{12,16},{16,12},{20,8},{24,4},{28,0},{1,29},{... | collective-permute-start | bytes 393224 | tf_op jit(solution)/shard_map/ppermute | solution.py:306
  10.7 1.4 %collective-permute-start.9 = (f32[64,512]{1,0:T(8,128)S(1)}, f32[64,512]{1,0:T(8,128)S(1)}, u32[]{:S(2)}, u32[]{:S(2)}) collective-permute-start(f32[64,512]{1,0:T(8,128)S(1)} %get-tuple-element.26), channel_id=1, source_target_pairs={{0,24},{4,28},{8,16},{12,20},{16,8},{20,12},{24,0},{28,4},{1,25},{... | collective-permute-start | bytes 393224 | tf_op jit(solution)/shard_map/ppermute | solution.py:306
  12.1 0.7 %collective-permute-start.10 = (f32[64,512]{1,0:T(8,128)S(1)}, f32[64,512]{1,0:T(8,128)S(1)}, u32[]{:S(2)}, u32[]{:S(2)}) collective-permute-start(f32[64,512]{1,0:T(8,128)S(1)} %get-tuple-element.27), channel_id=1, source_target_pairs={{0,12},{4,8},{8,4},{12,0},{16,28},{20,24},{24,20},{28,16},{1,13},{... | collective-permute-start | bytes 393224 | tf_op jit(solution)/shard_map/ppermute | solution.py:306
  12.8 2.1 %collective-permute-done.refs_2_ = f32[2,64,128]{2,1,0:T(8,128)S(1)} collective-permute-done((f32[2,64,128]{2,1,0:T(8,128)}, f32[2,64,128]{2,1,0:T(8,128)S(1)}, u32[]{:S(2)}, u32[]{:S(2)}) %collective-permute-start) | collective-permute-done | bytes 65568 | tf_op jit(solution)/shard_map/ppermute | solution.py:306
  14.9 2.4 %collective-permute-start.11 = (f32[4,2,64,128]{3,2,1,0:T(8,128)S(1)}, f32[4,2,64,128]{3,2,1,0:T(8,128)S(1)}, u32[]{:S(2)}, u32[]{:S(2)}) collective-permute-start(f32[4,2,64,128]{3,2,1,0:T(8,128)S(1)} %stack.1.refs_10_), channel_id=1, source_target_pairs={{0,4},{4,0},{8,12},{12,8},{16,20},{20,16},{24,28},{28,24},{1,5},{5... | collective-permute-start | bytes 786440 | tf_op jit(solution)/shard_map/ppermute | solution.py:306
  17.3 1.5 %collective-permute-start.6 = (f32[4,2,64,128]{3,2,1,0:T(8,128)S(1)}, f32[4,2,64,128]{3,2,1,0:T(8,128)S(1)}, u32[]{:S(2)}, u32[]{:S(2)}) collective-permute-start(f32[4,2,64,128]{3,2,1,0:T(8,128)S(1)} %stack.1.refs_10_), channel_id=1, source_target_pairs={{0,2},{1,3},{2,0},{3,1},{4,6},{5,7},{6,4},{7,5},{8,10},{9,11},{10,... | collective-permute-start | bytes 786440 | tf_op jit(solution)/shard_map/ppermute | solution.py:306
  18.8 1.5 %collective-permute-done.8.lower_ref = f32[64,512]{1,0:T(8,128)S(1)} collective-permute-done((f32[64,512]{1,0:T(8,128)S(1)}, f32[64,512]{1,0:T(8,128)S(1)}, u32[]{:S(2)}, u32[]{:S(2)}) %collective-permute-start.8) | collective-permute-done | bytes 131104 | tf_op jit(solution)/shard_map/ppermute | solution.py:306
  20.3 1.1 %collective-permute-start.2 = (f32[64,512]{1,0:T(8,128)S(1)}, f32[64,512]{1,0:T(8,128)S(1)}, u32[]{:S(2)}, u32[]{:S(2)}) collective-permute-start(f32[64,512]{1,0:T(8,128)S(1)} %get-tuple-element.20), channel_id=1, source_target_pairs={{0,4},{4,0},{8,12},{12,8},{16,20},{20,16},{24,28},{28,24},{1,5},{5... | collective-permute-start | bytes 393224 | tf_op jit(solution)/shard_map/ppermute | solution.py:306
  21.4 2.7 %collective-permute-start.1 = (f32[64,512]{1,0:T(8,128)S(1)}, f32[64,512]{1,0:T(8,128)S(1)}, u32[]{:S(2)}, u32[]{:S(2)}) collective-permute-start(f32[64,512]{1,0:T(8,128)S(1)} %get-tuple-element.19), channel_id=1, source_target_pairs={{0,16},{4,20},{8,24},{12,28},{16,0},{20,4},{24,8},{28,12},{1,17},{... | collective-permute-start | bytes 393224 | tf_op jit(solution)/shard_map/ppermute | solution.py:306
  24.1 0.3 rows.6.refs_8_
  24.4 0.3 rows.7.refs_9_
  24.7 0.6 %collective-permute-done.11.refs_11_ = f32[4,2,64,128]{3,2,1,0:T(8,128)S(1)} collective-permute-done((f32[4,2,64,128]{3,2,1,0:T(8,128)S(1)}, f32[4,2,64,128]{3,2,1,0:T(8,128)S(1)}, u32[]{:S(2)}, u32[]{:S(2)}) %collective-permute-start.11) | collective-permute-done | bytes 262176 | tf_op jit(solution)/shard_map/ppermute | solution.py:306
  25.4 1.5 %collective-permute-start.14 = (f32[4,2,64,128]{3,2,1,0:T(8,128)S(1)}, f32[4,2,64,128]{3,2,1,0:T(8,128)S(1)}, u32[]{:S(2)}, u32[]{:S(2)}) collective-permute-start(f32[4,2,64,128]{3,2,1,0:T(8,128)S(1)} %collective-permute-done.11.refs_11_), channel_id=1, source_target_pairs={{0,2},{1,3},{2,0},{3,1},{4,6},{5,7},{6,4},{7,5},{8,10},{9,11},{10,... | collective-permute-start | bytes 786440 | tf_op jit(solution)/shard_map/ppermute | solution.py:306
  26.9 2.8 %collective-permute-start.7 = (f32[64,512]{1,0:T(8,128)S(1)}, f32[64,512]{1,0:T(8,128)S(1)}, u32[]{:S(2)}, u32[]{:S(2)}) collective-permute-start(f32[64,512]{1,0:T(8,128)S(1)} %get-tuple-element.24), channel_id=1, source_target_pairs={{0,20},{4,16},{8,28},{12,24},{16,4},{20,0},{24,12},{28,8},{1,21},{... | collective-permute-start | bytes 393224 | tf_op jit(solution)/shard_map/ppermute | solution.py:306
  29.7 2.5 %collective-permute-done.1.upper_ref = f32[64,512]{1,0:T(8,128)S(1)} collective-permute-done((f32[64,512]{1,0:T(8,128)S(1)}, f32[64,512]{1,0:T(8,128)S(1)}, u32[]{:S(2)}, u32[]{:S(2)}) %collective-permute-start.1) | collective-permute-done | bytes 131104 | tf_op jit(solution)/shard_map/ppermute | solution.py:306
  32.2 0.3 rows.4.refs_6_
  32.7 0.5 %collective-permute-start.13 = (f32[4,2,64,128]{3,2,1,0:T(8,128)S(1)}, f32[4,2,64,128]{3,2,1,0:T(8,128)S(1)}, u32[]{:S(2)}, u32[]{:S(2)}) collective-permute-start(f32[4,2,64,128]{3,2,1,0:T(8,128)S(1)} %collective-permute-done.11.refs_11_), channel_id=1, source_target_pairs={{0,1},{1,0},{2,3},{3,2},{4,5},{5,4},{6,7},{7,6},{8,9},{9,8},{10,11... | collective-permute-start | bytes 786440 | tf_op jit(solution)/shard_map/ppermute | solution.py:306
  33.3 0.4 %collective-permute-start.16 = (f32[4,2,64,128]{3,2,1,0:T(8,128)S(1)}, f32[4,2,64,128]{3,2,1,0:T(8,128)S(1)}, u32[]{:S(2)}, u32[]{:S(2)}) collective-permute-start(f32[4,2,64,128]{3,2,1,0:T(8,128)S(1)} %collective-permute-done.14.refs_15_), channel_id=1, source_target_pairs={{0,1},{1,0},{2,3},{3,2},{4,5},{5,4},{6,7},{7,6},{8,9},{9,8},{10,11... | collective-permute-start | bytes 786440 | tf_op jit(solution)/shard_map/ppermute | solution.py:306
  33.7 1.4 %collective-permute-done.7.upper_ref = f32[64,512]{1,0:T(8,128)S(1)} collective-permute-done((f32[64,512]{1,0:T(8,128)S(1)}, f32[64,512]{1,0:T(8,128)S(1)}, u32[]{:S(2)}, u32[]{:S(2)}) %collective-permute-start.7) | collective-permute-done | bytes 131104 | tf_op jit(solution)/shard_map/ppermute | solution.py:306
  35.1 0.3 rows.5.refs_7_
  35.5 4.8 %correlate.1 = f32[1,16,4096]{2,1,0:T(8,128)} custom-call(bf16[2,2,512,256]{3,2,1,0:T(8,128)(2,1)S(1)} %copy-done.2, bf16[2,2,256,512]{3,2,1,0:T(8,128)(2,1)S(1)} %copy-done.1, bf16[2,2,256,256]{3,2,1,0:T(8,128)(2,1)S(1)} %copy-done.3, s32[1,8]{1,0:T(1,128)S(1)} %copy-done.6, s32[8,16]{1,0:T(8,128)S(1)} %copy-done.5, s32[8]{0:T(128)S(1)} %copy-done.7, ...), custom_call_target="tpu_custom_call" | custom-call | tf_op jit(solution)/shard_map/correlate/pallas_call | solution.py:284
  (38 shorter events, 0.3 us)
Async XLA Ops:
  0.0 5.7 %copy-start.6 = (s32[1,8]{1,0:T(1,128)S(1)}, s32[1,8]{1,0:T(1,128)}, u32[]{:S(2)}) copy-start(s32[1,8]{1,0:T(1,128)} %refs_3_.1) | copy-start | bytes 100
  0.0 5.7 %copy-start = (f32[8,64,512]{2,1,0:T(8,128)S(1)}, f32[8,64,512]{2,1,0:T(8,128)}, u32[]{:S(2)}) copy-start(f32[8,64,512]{2,1,0:T(8,128)} %frames_ref.1) | copy-start | bytes 3145732
  0.0 10.7 %collective-permute-start.4 = (f32[2,64,128]{2,1,0:T(8,128)}, f32[2,64,128]{2,1,0:T(8,128)S(1)}, u32[]{:S(2)}, u32[]{:S(2)}) collective-permute-start(f32[2,64,128]{2,1,0:T(8,128)} %bitcast.1), channel_id=1, source_target_pairs={{0,24},{4,28},{8,16},{12,20},{16,8},{20,12},{24,0},{28,4},{1,25},{... | collective-permute-start | bytes 196616 | tf_op jit(solution)/shard_map/ppermute | solution.py:306
  5.1 7.0 %collective-permute-start.3 = (f32[2,64,128]{2,1,0:T(8,128)}, f32[2,64,128]{2,1,0:T(8,128)S(1)}, u32[]{:S(2)}, u32[]{:S(2)}) collective-permute-start(f32[2,64,128]{2,1,0:T(8,128)} %bitcast.2), channel_id=1, source_target_pairs={{0,8},{4,12},{8,0},{12,4},{16,24},{20,28},{24,16},{28,20},{1,9},{5... | collective-permute-start | bytes 196616 | tf_op jit(solution)/shard_map/ppermute | solution.py:306
  5.1 9.8 %collective-permute-start = (f32[2,64,128]{2,1,0:T(8,128)}, f32[2,64,128]{2,1,0:T(8,128)S(1)}, u32[]{:S(2)}, u32[]{:S(2)}) collective-permute-start(f32[2,64,128]{2,1,0:T(8,128)} %bitcast.3), channel_id=1, source_target_pairs={{0,16},{4,20},{8,24},{12,28},{16,0},{20,4},{24,8},{28,12},{1,17},{... | collective-permute-start | bytes 196616 | tf_op jit(solution)/shard_map/ppermute | solution.py:306
  5.7 9.2 %copy-start.8 = (f32[2,128,64]{1,2,0:T(8,128)S(1)}, f32[2,128,64]{1,2,0:T(8,128)}, u32[]{:S(2)}) copy-start(f32[2,128,64]{1,2,0:T(8,128)} %param.11) | copy-start | bytes 196612
  5.9 11.4 %collective-permute-start.5 = (f32[64,512]{1,0:T(8,128)S(1)}, f32[64,512]{1,0:T(8,128)S(1)}, u32[]{:S(2)}, u32[]{:S(2)}) collective-permute-start(f32[64,512]{1,0:T(8,128)S(1)} %get-tuple-element.22), channel_id=1, source_target_pairs={{0,28},{4,24},{8,20},{12,16},{16,12},{20,8},{24,4},{28,0},{1,29},{... | collective-permute-start | bytes 393224 | tf_op jit(solution)/shard_map/ppermute | solution.py:306
  10.7 9.6 %collective-permute-start.8 = (f32[64,512]{1,0:T(8,128)S(1)}, f32[64,512]{1,0:T(8,128)S(1)}, u32[]{:S(2)}, u32[]{:S(2)}) collective-permute-start(f32[64,512]{1,0:T(8,128)S(1)} %get-tuple-element.25), channel_id=1, source_target_pairs={{0,8},{4,12},{8,0},{12,4},{16,24},{20,28},{24,16},{28,20},{1,9},{5... | collective-permute-start | bytes 393224 | tf_op jit(solution)/shard_map/ppermute | solution.py:306
  10.7 10.7 %collective-permute-start.9 = (f32[64,512]{1,0:T(8,128)S(1)}, f32[64,512]{1,0:T(8,128)S(1)}, u32[]{:S(2)}, u32[]{:S(2)}) collective-permute-start(f32[64,512]{1,0:T(8,128)S(1)} %get-tuple-element.26), channel_id=1, source_target_pairs={{0,24},{4,28},{8,16},{12,20},{16,8},{20,12},{24,0},{28,4},{1,25},{... | collective-permute-start | bytes 393224 | tf_op jit(solution)/shard_map/ppermute | solution.py:306
  12.1 12.1 %copy-start.9 = (bf16[2,2,256,256]{3,2,1,0:T(8,128)(2,1)S(1)}, bf16[2,2,256,256]{3,2,1,0:T(8,128)(2,1)}, u32[]{:S(2)}) copy-start(bf16[2,2,256,256]{3,2,1,0:T(8,128)(2,1)} %constant.10.clone.row_ref) | copy-start | bytes 1572868
  12.1 12.4 %collective-permute-start.10 = (f32[64,512]{1,0:T(8,128)S(1)}, f32[64,512]{1,0:T(8,128)S(1)}, u32[]{:S(2)}, u32[]{:S(2)}) collective-permute-start(f32[64,512]{1,0:T(8,128)S(1)} %get-tuple-element.27), channel_id=1, source_target_pairs={{0,12},{4,8},{8,4},{12,0},{16,28},{20,24},{24,20},{28,16},{1,13},{... | collective-permute-start | bytes 393224 | tf_op jit(solution)/shard_map/ppermute | solution.py:306
  14.9 10.5 %collective-permute-start.11 = (f32[4,2,64,128]{3,2,1,0:T(8,128)S(1)}, f32[4,2,64,128]{3,2,1,0:T(8,128)S(1)}, u32[]{:S(2)}, u32[]{:S(2)}) collective-permute-start(f32[4,2,64,128]{3,2,1,0:T(8,128)S(1)} %stack.1.refs_10_), channel_id=1, source_target_pairs={{0,4},{4,0},{8,12},{12,8},{16,20},{20,16},{24,28},{28,24},{1,5},{5... | collective-permute-start | bytes 786440 | tf_op jit(solution)/shard_map/ppermute | solution.py:306
  17.3 9.6 %collective-permute-start.6 = (f32[4,2,64,128]{3,2,1,0:T(8,128)S(1)}, f32[4,2,64,128]{3,2,1,0:T(8,128)S(1)}, u32[]{:S(2)}, u32[]{:S(2)}) collective-permute-start(f32[4,2,64,128]{3,2,1,0:T(8,128)S(1)} %stack.1.refs_10_), channel_id=1, source_target_pairs={{0,2},{1,3},{2,0},{3,1},{4,6},{5,7},{6,4},{7,5},{8,10},{9,11},{10,... | collective-permute-start | bytes 786440 | tf_op jit(solution)/shard_map/ppermute | solution.py:306
  20.3 12.9 %collective-permute-start.2 = (f32[64,512]{1,0:T(8,128)S(1)}, f32[64,512]{1,0:T(8,128)S(1)}, u32[]{:S(2)}, u32[]{:S(2)}) collective-permute-start(f32[64,512]{1,0:T(8,128)S(1)} %get-tuple-element.20), channel_id=1, source_target_pairs={{0,4},{4,0},{8,12},{12,8},{16,20},{20,16},{24,28},{28,24},{1,5},{5... | collective-permute-start | bytes 393224 | tf_op jit(solution)/shard_map/ppermute | solution.py:306
  21.4 10.9 %collective-permute-start.1 = (f32[64,512]{1,0:T(8,128)S(1)}, f32[64,512]{1,0:T(8,128)S(1)}, u32[]{:S(2)}, u32[]{:S(2)}) collective-permute-start(f32[64,512]{1,0:T(8,128)S(1)} %get-tuple-element.19), channel_id=1, source_target_pairs={{0,16},{4,20},{8,24},{12,28},{16,0},{20,4},{24,8},{28,12},{1,17},{... | collective-permute-start | bytes 393224 | tf_op jit(solution)/shard_map/ppermute | solution.py:306
  25.4 7.9 %collective-permute-start.14 = (f32[4,2,64,128]{3,2,1,0:T(8,128)S(1)}, f32[4,2,64,128]{3,2,1,0:T(8,128)S(1)}, u32[]{:S(2)}, u32[]{:S(2)}) collective-permute-start(f32[4,2,64,128]{3,2,1,0:T(8,128)S(1)} %collective-permute-done.11.refs_11_), channel_id=1, source_target_pairs={{0,2},{1,3},{2,0},{3,1},{4,6},{5,7},{6,4},{7,5},{8,10},{9,11},{10,... | collective-permute-start | bytes 786440 | tf_op jit(solution)/shard_map/ppermute | solution.py:306
  26.9 8.2 %collective-permute-start.7 = (f32[64,512]{1,0:T(8,128)S(1)}, f32[64,512]{1,0:T(8,128)S(1)}, u32[]{:S(2)}, u32[]{:S(2)}) collective-permute-start(f32[64,512]{1,0:T(8,128)S(1)} %get-tuple-element.24), channel_id=1, source_target_pairs={{0,20},{4,16},{8,28},{12,24},{16,4},{20,0},{24,12},{28,8},{1,21},{... | collective-permute-start | bytes 393224 | tf_op jit(solution)/shard_map/ppermute | solution.py:306
  32.5 2.9 %copy-start.1 = (bf16[2,2,256,512]{3,2,1,0:T(8,128)(2,1)S(1)}, bf16[2,2,256,512]{3,2,1,0:T(8,128)(2,1)}, u32[]{:S(2)}) copy-start(bf16[2,2,256,512]{3,2,1,0:T(8,128)(2,1)} %constant.12.clone.refs_1_) | copy-start | bytes 3145732
  32.6 2.9 %copy-start.2 = (bf16[2,2,512,256]{3,2,1,0:T(8,128)(2,1)S(1)}, bf16[2,2,512,256]{3,2,1,0:T(8,128)(2,1)}, u32[]{:S(2)}) copy-start(bf16[2,2,512,256]{3,2,1,0:T(8,128)(2,1)} %constant.11.clone.refs_0_) | copy-start | bytes 3145732
  32.6 2.9 %copy-start.3 = (bf16[2,2,256,256]{3,2,1,0:T(8,128)(2,1)S(1)}, bf16[2,2,256,256]{3,2,1,0:T(8,128)(2,1)}, u32[]{:S(2)}) copy-start(bf16[2,2,256,256]{3,2,1,0:T(8,128)(2,1)} %constant.13.clone.refs_2_) | copy-start | bytes 1572868
  32.6 2.8 %collective-permute-start.12 = (f32[4,2,64,128]{3,2,1,0:T(8,128)S(1)}, f32[4,2,64,128]{3,2,1,0:T(8,128)S(1)}, u32[]{:S(2)}, u32[]{:S(2)}) collective-permute-start(f32[4,2,64,128]{3,2,1,0:T(8,128)S(1)} %stack.1.refs_10_), channel_id=1, source_target_pairs={{0,1},{1,0},{2,3},{3,2},{4,5},{5,4},{6,7},{7,6},{8,9},{9,8},{10,11... | collective-permute-start | bytes 786440 | tf_op jit(solution)/shard_map/ppermute | solution.py:306
  32.7 2.7 %collective-permute-start.13 = (f32[4,2,64,128]{3,2,1,0:T(8,128)S(1)}, f32[4,2,64,128]{3,2,1,0:T(8,128)S(1)}, u32[]{:S(2)}, u32[]{:S(2)}) collective-permute-start(f32[4,2,64,128]{3,2,1,0:T(8,128)S(1)} %collective-permute-done.11.refs_11_), channel_id=1, source_target_pairs={{0,1},{1,0},{2,3},{3,2},{4,5},{5,4},{6,7},{7,6},{8,9},{9,8},{10,11... | collective-permute-start | bytes 786440 | tf_op jit(solution)/shard_map/ppermute | solution.py:306
  33.2 2.2 %collective-permute-start.15 = (f32[4,2,64,128]{3,2,1,0:T(8,128)S(1)}, f32[4,2,64,128]{3,2,1,0:T(8,128)S(1)}, u32[]{:S(2)}, u32[]{:S(2)}) collective-permute-start(f32[4,2,64,128]{3,2,1,0:T(8,128)S(1)} %collective-permute-done.6.refs_14_), channel_id=1, source_target_pairs={{0,1},{1,0},{2,3},{3,2},{4,5},{5,4},{6,7},{7,6},{8,9},{9,8},{10,11... | collective-permute-start | bytes 786440 | tf_op jit(solution)/shard_map/ppermute | solution.py:306
  33.3 2.1 %collective-permute-start.16 = (f32[4,2,64,128]{3,2,1,0:T(8,128)S(1)}, f32[4,2,64,128]{3,2,1,0:T(8,128)S(1)}, u32[]{:S(2)}, u32[]{:S(2)}) collective-permute-start(f32[4,2,64,128]{3,2,1,0:T(8,128)S(1)} %collective-permute-done.14.refs_15_), channel_id=1, source_target_pairs={{0,1},{1,0},{2,3},{3,2},{4,5},{5,4},{6,7},{7,6},{8,9},{9,8},{10,11... | collective-permute-start | bytes 786440 | tf_op jit(solution)/shard_map/ppermute | solution.py:306
  (3 other events, 8.7 us)

commit v5 on v4

--- a/solution.py
+++ b/solution.py
@@ -331,7 +331,7 @@
     sibling += [swap(q, "frames", 4, 1) for q in quads[1:]]
     send(1)
     send(2)
-    send(3)
+    send(3, far)
     send(4, far)
     send(5, quad_y)
     send(6)

time: 40.5 us -> 47.7 us (1.18)
  waiting for transfers between devices: 8.18 us -> 13.8 us
  local copies, waits for them, and re-layouts: 0.05 us -> 0.89 us
  starting transfers between devices: 25.7 us -> 26.4 us
    ppermute x17, waiting for transfers between devices: 8.18 us -> 13.8 us  [swap(): return lax.ppermute(value, axis, [(i, i ^ bits) for i in range(size)])]
    unnamed x20, local copies, waits for them, and re-layouts: 0.05 us -> 0.89 us
    ppermute x17, starting transfers between devices: 25.7 us -> 26.4 us  [swap(): return lax.ppermute(value, axis, [(i, i ^ bits) for i in range(size)])]
  transfers between devices with their start and end apart: 17 -> 17, of which waited for: 5 -> 8; matrix products, arithmetic and copies ran while one was open for 0% -> 0% of each run, Pallas kernels for 3% -> 3%
where the time goes in v5:
time: 47.7 us; the launch traced here: 47.5 us
  starting transfers between devices  26.4 us (55%)
  waiting for transfers between devices  13.8 us (29%)
  Pallas kernels  6.16 us (13%)
  local copies, waits for them, and re-layouts  0.89 us (2%)
    ppermute x17, starting transfers between devices, swap(): return lax.ppermute(value, axis, [(i, i ^ bits) for i in range(size)])  26.4 us
    ppermute x17, waiting for transfers between devices, swap(): return lax.ppermute(value, axis, [(i, i ^ bits) for i in range(size)])  13.8 us
    pallas_call x1, Pallas kernels, correlate(): pl.pallas_call(functools.partial(correlate_kernel, len(spectra), fold_bod...  4.78 us
    pallas_call x4, Pallas kernels, row_spectra(): pl.pallas_call(functools.partial(rows_kernel, split_strip), out_shape=jax...  1.16 us
  transfers between devices with their start and end apart: 17, of which 8 were waited for; matrix products, arithmetic and copies ran while one was open for 0% of the time, Pallas kernels for 3%

profile of v5, /device:TPU:0, one launch (start us, length us, event | category | flops | bytes accessed | tf_op | source)
XLA Modules:
  0.0 47.5 jit_solution(10500959176397244266)
XLA Ops:
  0.0 5.0 %collective-permute-start.4 = (f32[2,64,128]{2,1,0:T(8,128)}, f32[2,64,128]{2,1,0:T(8,128)S(1)}, u32[]{:S(2)}, u32[]{:S(2)}) collective-permute-start(f32[2,64,128]{2,1,0:T(8,128)} %bitcast.1), channel_id=1, source_target_pairs={{0,24},{4,28},{8,16},{12,20},{16,8},{20,12},{24,0},{28,4},{1,25},{... | collective-permute-start | bytes 196616 | tf_op jit(solution)/shard_map/ppermute | solution.py:306
  5.1 0.6 %collective-permute-start = (f32[2,64,128]{2,1,0:T(8,128)}, f32[2,64,128]{2,1,0:T(8,128)S(1)}, u32[]{:S(2)}, u32[]{:S(2)}) collective-permute-start(f32[2,64,128]{2,1,0:T(8,128)} %bitcast.3), channel_id=1, source_target_pairs={{0,16},{4,20},{8,24},{12,28},{16,0},{20,4},{24,8},{28,12},{1,17},{... | collective-permute-start | bytes 196616 | tf_op jit(solution)/shard_map/ppermute | solution.py:306
  5.7 2.5 %collective-permute-done.4.refs_3_ = f32[2,64,128]{2,1,0:T(8,128)S(1)} collective-permute-done((f32[2,64,128]{2,1,0:T(8,128)}, f32[2,64,128]{2,1,0:T(8,128)S(1)}, u32[]{:S(2)}, u32[]{:S(2)}) %collective-permute-start.4) | collective-permute-done | bytes 65568 | tf_op jit(solution)/shard_map/ppermute | solution.py:306
  8.2 1.8 %collective-permute-done.3.refs_1_ = f32[2,64,128]{2,1,0:T(8,128)S(1)} collective-permute-done((f32[2,64,128]{2,1,0:T(8,128)}, f32[2,64,128]{2,1,0:T(8,128)S(1)}, u32[]{:S(2)}, u32[]{:S(2)}) %collective-permute-start.3) | collective-permute-done | bytes 65568 | tf_op jit(solution)/shard_map/ppermute | solution.py:306
  9.9 1.0 %collective-permute-done.refs_2_ = f32[2,64,128]{2,1,0:T(8,128)S(1)} collective-permute-done((f32[2,64,128]{2,1,0:T(8,128)}, f32[2,64,128]{2,1,0:T(8,128)S(1)}, u32[]{:S(2)}, u32[]{:S(2)}) %collective-permute-start) | collective-permute-done | bytes 65568 | tf_op jit(solution)/shard_map/ppermute | solution.py:306
  10.9 0.8 %copy-done.8 = f32[2,128,64]{1,2,0:T(8,128)S(1)} copy-done((f32[2,128,64]{1,2,0:T(8,128)S(1)}, f32[2,128,64]{1,2,0:T(8,128)}, u32[]{:S(2)}) %copy-start.8) | copy-done | bytes 65560
  11.8 1.6 %collective-permute-start.11 = (f32[4,2,64,128]{3,2,1,0:T(8,128)S(1)}, f32[4,2,64,128]{3,2,1,0:T(8,128)S(1)}, u32[]{:S(2)}, u32[]{:S(2)}) collective-permute-start(f32[4,2,64,128]{3,2,1,0:T(8,128)S(1)} %stack.1.refs_10_), channel_id=1, source_target_pairs={{0,4},{4,0},{8,12},{12,8},{16,20},{20,16},{24,28},{28,24},{1,5},{5... | collective-permute-start | bytes 786440 | tf_op jit(solution)/shard_map/ppermute | solution.py:306
  13.6 2.8 %collective-permute-start.5 = (f32[64,512]{1,0:T(8,128)S(1)}, f32[64,512]{1,0:T(8,128)S(1)}, u32[]{:S(2)}, u32[]{:S(2)}) collective-permute-start(f32[64,512]{1,0:T(8,128)S(1)} %get-tuple-element.23), channel_id=1, source_target_pairs={{0,28},{4,24},{8,20},{12,16},{16,12},{20,8},{24,4},{28,0},{1,29},{... | collective-permute-start | bytes 393224 | tf_op jit(solution)/shard_map/ppermute | solution.py:306
  16.3 0.4 collective-permute-start.8
  16.7 2.0 %collective-permute-start.9 = (f32[64,512]{1,0:T(8,128)S(1)}, f32[64,512]{1,0:T(8,128)S(1)}, u32[]{:S(2)}, u32[]{:S(2)}) collective-permute-start(f32[64,512]{1,0:T(8,128)S(1)} %get-tuple-element.27), channel_id=1, source_target_pairs={{0,24},{4,28},{8,16},{12,20},{16,8},{20,12},{24,0},{28,4},{1,25},{... | collective-permute-start | bytes 393224 | tf_op jit(solution)/shard_map/ppermute | solution.py:306
  18.7 1.2 %collective-permute-start.1 = (f32[64,512]{1,0:T(8,128)S(1)}, f32[64,512]{1,0:T(8,128)S(1)}, u32[]{:S(2)}, u32[]{:S(2)}) collective-permute-start(f32[64,512]{1,0:T(8,128)S(1)} %get-tuple-element.20), channel_id=1, source_target_pairs={{0,16},{4,20},{8,24},{12,28},{16,0},{20,4},{24,8},{28,12},{1,17},{... | collective-permute-start | bytes 393224 | tf_op jit(solution)/shard_map/ppermute | solution.py:306
  19.8 3.1 %collective-permute-done.5.upper_ref = f32[64,512]{1,0:T(8,128)S(1)} collective-permute-done((f32[64,512]{1,0:T(8,128)S(1)}, f32[64,512]{1,0:T(8,128)S(1)}, u32[]{:S(2)}, u32[]{:S(2)}) %collective-permute-start.5) | collective-permute-done | bytes 131104 | tf_op jit(solution)/shard_map/ppermute | solution.py:306
  22.9 1.1 %collective-permute-start.2 = (f32[64,512]{1,0:T(8,128)S(1)}, f32[64,512]{1,0:T(8,128)S(1)}, u32[]{:S(2)}, u32[]{:S(2)}) collective-permute-start(f32[64,512]{1,0:T(8,128)S(1)} %get-tuple-element.21), channel_id=1, source_target_pairs={{0,4},{4,0},{8,12},{12,8},{16,20},{20,16},{24,28},{28,24},{1,5},{5... | collective-permute-start | bytes 393224 | tf_op jit(solution)/shard_map/ppermute | solution.py:306
  24.0 0.4 collective-permute-done.8.lower_ref
  24.4 4.2 %collective-permute-start.10 = (f32[64,512]{1,0:T(8,128)S(1)}, f32[64,512]{1,0:T(8,128)S(1)}, u32[]{:S(2)}, u32[]{:S(2)}) collective-permute-start(f32[64,512]{1,0:T(8,128)S(1)} %get-tuple-element.29), channel_id=1, source_target_pairs={{0,12},{4,8},{8,4},{12,0},{16,28},{20,24},{24,20},{28,16},{1,13},{... | collective-permute-start | bytes 393224 | tf_op jit(solution)/shard_map/ppermute | solution.py:306
  28.6 1.5 %collective-permute-start.6 = (f32[4,2,64,128]{3,2,1,0:T(8,128)S(1)}, f32[4,2,64,128]{3,2,1,0:T(8,128)S(1)}, u32[]{:S(2)}, u32[]{:S(2)}) collective-permute-start(f32[4,2,64,128]{3,2,1,0:T(8,128)S(1)} %stack.1.refs_10_), channel_id=1, source_target_pairs={{0,2},{1,3},{2,0},{3,1},{4,6},{5,7},{6,4},{7,5},{8,10},{9,11},{10,... | collective-permute-start | bytes 786440 | tf_op jit(solution)/shard_map/ppermute | solution.py:306
  30.5 0.6 %collective-permute-start.14 = (f32[4,2,64,128]{3,2,1,0:T(8,128)S(1)}, f32[4,2,64,128]{3,2,1,0:T(8,128)S(1)}, u32[]{:S(2)}, u32[]{:S(2)}) collective-permute-start(f32[4,2,64,128]{3,2,1,0:T(8,128)S(1)} %collective-permute-done.11.refs_11_), channel_id=1, source_target_pairs={{0,2},{1,3},{2,0},{3,1},{4,6},{5,7},{6,4},{7,5},{8,10},{9,11},{10,... | collective-permute-start | bytes 786440 | tf_op jit(solution)/shard_map/ppermute | solution.py:306
  31.0 1.8 %collective-permute-done.1.upper_ref = f32[64,512]{1,0:T(8,128)S(1)} collective-permute-done((f32[64,512]{1,0:T(8,128)S(1)}, f32[64,512]{1,0:T(8,128)S(1)}, u32[]{:S(2)}, u32[]{:S(2)}) %collective-permute-start.1) | collective-permute-done | bytes 131104 | tf_op jit(solution)/shard_map/ppermute | solution.py:306
  33.1 1.9 %collective-permute-done.6.refs_14_ = f32[4,2,64,128]{3,2,1,0:T(8,128)S(1)} collective-permute-done((f32[4,2,64,128]{3,2,1,0:T(8,128)S(1)}, f32[4,2,64,128]{3,2,1,0:T(8,128)S(1)}, u32[]{:S(2)}, u32[]{:S(2)}) %collective-permute-start.6) | collective-permute-done | bytes 262176 | tf_op jit(solution)/shard_map/ppermute | solution.py:306
  35.0 4.4 %collective-permute-start.7 = (f32[64,512]{1,0:T(8,128)S(1)}, f32[64,512]{1,0:T(8,128)S(1)}, u32[]{:S(2)}, u32[]{:S(2)}) collective-permute-start(f32[64,512]{1,0:T(8,128)S(1)} %get-tuple-element.25), channel_id=1, source_target_pairs={{0,20},{4,16},{8,28},{12,24},{16,4},{20,0},{24,12},{28,8},{1,21},{... | collective-permute-start | bytes 393224 | tf_op jit(solution)/shard_map/ppermute | solution.py:306
  39.9 0.5 %collective-permute-start.13 = (f32[4,2,64,128]{3,2,1,0:T(8,128)S(1)}, f32[4,2,64,128]{3,2,1,0:T(8,128)S(1)}, u32[]{:S(2)}, u32[]{:S(2)}) collective-permute-start(f32[4,2,64,128]{3,2,1,0:T(8,128)S(1)} %collective-permute-done.11.refs_11_), channel_id=1, source_target_pairs={{0,1},{1,0},{2,3},{3,2},{4,5},{5,4},{6,7},{7,6},{8,9},{9,8},{10,11... | collective-permute-start | bytes 786440 | tf_op jit(solution)/shard_map/ppermute | solution.py:306
  40.4 0.4 collective-permute-start.16
  40.9 1.5 %collective-permute-done.7.upper_ref = f32[64,512]{1,0:T(8,128)S(1)} collective-permute-done((f32[64,512]{1,0:T(8,128)S(1)}, f32[64,512]{1,0:T(8,128)S(1)}, u32[]{:S(2)}, u32[]{:S(2)}) %collective-permute-start.7) | collective-permute-done | bytes 131104 | tf_op jit(solution)/shard_map/ppermute | solution.py:306
  42.8 4.8 %correlate.1 = f32[1,16,4096]{2,1,0:T(8,128)} custom-call(bf16[2,2,512,256]{3,2,1,0:T(8,128)(2,1)S(1)} %copy-done.2, bf16[2,2,256,512]{3,2,1,0:T(8,128)(2,1)S(1)} %copy-done.1, bf16[2,2,256,256]{3,2,1,0:T(8,128)(2,1)S(1)} %copy-done.3, s32[1,8]{1,0:T(1,128)S(1)} %copy-done.6, s32[8,16]{1,0:T(8,128)S(1)} %copy-done.5, s32[8]{0:T(128)S(1)} %copy-done.7, ...), custom_call_target="tpu_custom_call" | custom-call | tf_op jit(solution)/shard_map/correlate/pallas_call | solution.py:284
  (38 shorter events, 1.6 us)
Async XLA Ops:
  0.0 13.3 %copy-start.6 = (s32[1,8]{1,0:T(1,128)S(1)}, s32[1,8]{1,0:T(1,128)}, u32[]{:S(2)}) copy-start(s32[1,8]{1,0:T(1,128)} %refs_3_.1) | copy-start | bytes 100
  0.0 8.2 %collective-permute-start.4 = (f32[2,64,128]{2,1,0:T(8,128)}, f32[2,64,128]{2,1,0:T(8,128)S(1)}, u32[]{:S(2)}, u32[]{:S(2)}) collective-permute-start(f32[2,64,128]{2,1,0:T(8,128)} %bitcast.1), channel_id=1, source_target_pairs={{0,24},{4,28},{8,16},{12,20},{16,8},{20,12},{24,0},{28,4},{1,25},{... | collective-permute-start | bytes 196616 | tf_op jit(solution)/shard_map/ppermute | solution.py:306
  5.1 4.9 %collective-permute-start.3 = (f32[2,64,128]{2,1,0:T(8,128)}, f32[2,64,128]{2,1,0:T(8,128)S(1)}, u32[]{:S(2)}, u32[]{:S(2)}) collective-permute-start(f32[2,64,128]{2,1,0:T(8,128)} %bitcast.2), channel_id=1, source_target_pairs={{0,8},{4,12},{8,0},{12,4},{16,24},{20,28},{24,16},{28,20},{1,9},{5... | collective-permute-start | bytes 196616 | tf_op jit(solution)/shard_map/ppermute | solution.py:306
  5.1 5.8 %collective-permute-start = (f32[2,64,128]{2,1,0:T(8,128)}, f32[2,64,128]{2,1,0:T(8,128)S(1)}, u32[]{:S(2)}, u32[]{:S(2)}) collective-permute-start(f32[2,64,128]{2,1,0:T(8,128)} %bitcast.3), channel_id=1, source_target_pairs={{0,16},{4,20},{8,24},{12,28},{16,0},{20,4},{24,8},{28,12},{1,17},{... | collective-permute-start | bytes 196616 | tf_op jit(solution)/shard_map/ppermute | solution.py:306
  11.8 18.7 %collective-permute-start.11 = (f32[4,2,64,128]{3,2,1,0:T(8,128)S(1)}, f32[4,2,64,128]{3,2,1,0:T(8,128)S(1)}, u32[]{:S(2)}, u32[]{:S(2)}) collective-permute-start(f32[4,2,64,128]{3,2,1,0:T(8,128)S(1)} %stack.1.refs_10_), channel_id=1, source_target_pairs={{0,4},{4,0},{8,12},{12,8},{16,20},{20,16},{24,28},{28,24},{1,5},{5... | collective-permute-start | bytes 786440 | tf_op jit(solution)/shard_map/ppermute | solution.py:306
  13.3 16.8 %copy-start.9 = (bf16[2,2,256,256]{3,2,1,0:T(8,128)(2,1)S(1)}, bf16[2,2,256,256]{3,2,1,0:T(8,128)(2,1)}, u32[]{:S(2)}) copy-start(bf16[2,2,256,256]{3,2,1,0:T(8,128)(2,1)} %constant.10.clone.row_ref) | copy-start | bytes 1572868
  13.6 9.3 %collective-permute-start.5 = (f32[64,512]{1,0:T(8,128)S(1)}, f32[64,512]{1,0:T(8,128)S(1)}, u32[]{:S(2)}, u32[]{:S(2)}) collective-permute-start(f32[64,512]{1,0:T(8,128)S(1)} %get-tuple-element.23), channel_id=1, source_target_pairs={{0,28},{4,24},{8,20},{12,16},{16,12},{20,8},{24,4},{28,0},{1,29},{... | collective-permute-start | bytes 393224 | tf_op jit(solution)/shard_map/ppermute | solution.py:306
  16.3 8.1 %collective-permute-start.8 = (f32[64,512]{1,0:T(8,128)S(1)}, f32[64,512]{1,0:T(8,128)S(1)}, u32[]{:S(2)}, u32[]{:S(2)}) collective-permute-start(f32[64,512]{1,0:T(8,128)S(1)} %get-tuple-element.26), channel_id=1, source_target_pairs={{0,8},{4,12},{8,0},{12,4},{16,24},{20,28},{24,16},{28,20},{1,9},{5... | collective-permute-start | bytes 393224 | tf_op jit(solution)/shard_map/ppermute | solution.py:306
  16.7 11.9 %collective-permute-start.9 = (f32[64,512]{1,0:T(8,128)S(1)}, f32[64,512]{1,0:T(8,128)S(1)}, u32[]{:S(2)}, u32[]{:S(2)}) collective-permute-start(f32[64,512]{1,0:T(8,128)S(1)} %get-tuple-element.27), channel_id=1, source_target_pairs={{0,24},{4,28},{8,16},{12,20},{16,8},{20,12},{24,0},{28,4},{1,25},{... | collective-permute-start | bytes 393224 | tf_op jit(solution)/shard_map/ppermute | solution.py:306
  18.7 14.2 %collective-permute-start.1 = (f32[64,512]{1,0:T(8,128)S(1)}, f32[64,512]{1,0:T(8,128)S(1)}, u32[]{:S(2)}, u32[]{:S(2)}) collective-permute-start(f32[64,512]{1,0:T(8,128)S(1)} %get-tuple-element.20), channel_id=1, source_target_pairs={{0,16},{4,20},{8,24},{12,28},{16,0},{20,4},{24,8},{28,12},{1,17},{... | collective-permute-start | bytes 393224 | tf_op jit(solution)/shard_map/ppermute | solution.py:306
  22.9 17.5 %collective-permute-start.2 = (f32[64,512]{1,0:T(8,128)S(1)}, f32[64,512]{1,0:T(8,128)S(1)}, u32[]{:S(2)}, u32[]{:S(2)}) collective-permute-start(f32[64,512]{1,0:T(8,128)S(1)} %get-tuple-element.21), channel_id=1, source_target_pairs={{0,4},{4,0},{8,12},{12,8},{16,20},{20,16},{24,28},{28,24},{1,5},{5... | collective-permute-start | bytes 393224 | tf_op jit(solution)/shard_map/ppermute | solution.py:306
  24.4 15.0 %collective-permute-start.10 = (f32[64,512]{1,0:T(8,128)S(1)}, f32[64,512]{1,0:T(8,128)S(1)}, u32[]{:S(2)}, u32[]{:S(2)}) collective-permute-start(f32[64,512]{1,0:T(8,128)S(1)} %get-tuple-element.29), channel_id=1, source_target_pairs={{0,12},{4,8},{8,4},{12,0},{16,28},{20,24},{24,20},{28,16},{1,13},{... | collective-permute-start | bytes 393224 | tf_op jit(solution)/shard_map/ppermute | solution.py:306
  28.6 6.4 %collective-permute-start.6 = (f32[4,2,64,128]{3,2,1,0:T(8,128)S(1)}, f32[4,2,64,128]{3,2,1,0:T(8,128)S(1)}, u32[]{:S(2)}, u32[]{:S(2)}) collective-permute-start(f32[4,2,64,128]{3,2,1,0:T(8,128)S(1)} %stack.1.refs_10_), channel_id=1, source_target_pairs={{0,2},{1,3},{2,0},{3,1},{4,6},{5,7},{6,4},{7,5},{8,10},{9,11},{10,... | collective-permute-start | bytes 786440 | tf_op jit(solution)/shard_map/ppermute | solution.py:306
  30.5 10.0 %collective-permute-start.14 = (f32[4,2,64,128]{3,2,1,0:T(8,128)S(1)}, f32[4,2,64,128]{3,2,1,0:T(8,128)S(1)}, u32[]{:S(2)}, u32[]{:S(2)}) collective-permute-start(f32[4,2,64,128]{3,2,1,0:T(8,128)S(1)} %collective-permute-done.11.refs_11_), channel_id=1, source_target_pairs={{0,2},{1,3},{2,0},{3,1},{4,6},{5,7},{6,4},{7,5},{8,10},{9,11},{10,... | collective-permute-start | bytes 786440 | tf_op jit(solution)/shard_map/ppermute | solution.py:306
  35.0 7.4 %collective-permute-start.7 = (f32[64,512]{1,0:T(8,128)S(1)}, f32[64,512]{1,0:T(8,128)S(1)}, u32[]{:S(2)}, u32[]{:S(2)}) collective-permute-start(f32[64,512]{1,0:T(8,128)S(1)} %get-tuple-element.25), channel_id=1, source_target_pairs={{0,20},{4,16},{8,28},{12,24},{16,4},{20,0},{24,12},{28,8},{1,21},{... | collective-permute-start | bytes 393224 | tf_op jit(solution)/shard_map/ppermute | solution.py:306
  39.7 3.0 %copy-start.1 = (bf16[2,2,256,512]{3,2,1,0:T(8,128)(2,1)S(1)}, bf16[2,2,256,512]{3,2,1,0:T(8,128)(2,1)}, u32[]{:S(2)}) copy-start(bf16[2,2,256,512]{3,2,1,0:T(8,128)(2,1)} %constant.12.clone.refs_1_) | copy-start | bytes 3145732
  39.7 3.0 %copy-start.2 = (bf16[2,2,512,256]{3,2,1,0:T(8,128)(2,1)S(1)}, bf16[2,2,512,256]{3,2,1,0:T(8,128)(2,1)}, u32[]{:S(2)}) copy-start(bf16[2,2,512,256]{3,2,1,0:T(8,128)(2,1)} %constant.11.clone.refs_0_) | copy-start | bytes 3145732
  39.7 3.0 %copy-start.3 = (bf16[2,2,256,256]{3,2,1,0:T(8,128)(2,1)S(1)}, bf16[2,2,256,256]{3,2,1,0:T(8,128)(2,1)}, u32[]{:S(2)}) copy-start(bf16[2,2,256,256]{3,2,1,0:T(8,128)(2,1)} %constant.13.clone.refs_2_) | copy-start | bytes 1572868
  39.7 3.0 %copy-start.4 = (bf16[2,256,256]{2,1,0:T(8,128)(2,1)S(1)}, bf16[2,256,256]{2,1,0:T(8,128)(2,1)}, u32[]{:S(2)}) copy-start(bf16[2,256,256]{2,1,0:T(8,128)(2,1)} %constant.14.clone.refs_18_) | copy-start | bytes 786436
  39.8 3.0 %copy-start.5 = (s32[8,16]{1,0:T(8,128)S(1)}, s32[8,16]{1,0:T(8,128)}, u32[]{:S(2)}) copy-start(s32[8,16]{1,0:T(8,128)} %refs_4_.1) | copy-start | bytes 1540
  39.8 2.9 %collective-permute-start.12 = (f32[4,2,64,128]{3,2,1,0:T(8,128)S(1)}, f32[4,2,64,128]{3,2,1,0:T(8,128)S(1)}, u32[]{:S(2)}, u32[]{:S(2)}) collective-permute-start(f32[4,2,64,128]{3,2,1,0:T(8,128)S(1)} %stack.1.refs_10_), channel_id=1, source_target_pairs={{0,1},{1,0},{2,3},{3,2},{4,5},{5,4},{6,7},{7,6},{8,9},{9,8},{10,11... | collective-permute-start | bytes 786440 | tf_op jit(solution)/shard_map/ppermute | solution.py:306
  39.9 2.8 %collective-permute-start.13 = (f32[4,2,64,128]{3,2,1,0:T(8,128)S(1)}, f32[4,2,64,128]{3,2,1,0:T(8,128)S(1)}, u32[]{:S(2)}, u32[]{:S(2)}) collective-permute-start(f32[4,2,64,128]{3,2,1,0:T(8,128)S(1)} %collective-permute-done.11.refs_11_), channel_id=1, source_target_pairs={{0,1},{1,0},{2,3},{3,2},{4,5},{5,4},{6,7},{7,6},{8,9},{9,8},{10,11... | collective-permute-start | bytes 786440 | tf_op jit(solution)/shard_map/ppermute | solution.py:306
  40.4 2.3 %collective-permute-start.15 = (f32[4,2,64,128]{3,2,1,0:T(8,128)S(1)}, f32[4,2,64,128]{3,2,1,0:T(8,128)S(1)}, u32[]{:S(2)}, u32[]{:S(2)}) collective-permute-start(f32[4,2,64,128]{3,2,1,0:T(8,128)S(1)} %collective-permute-done.6.refs_14_), channel_id=1, source_target_pairs={{0,1},{1,0},{2,3},{3,2},{4,5},{5,4},{6,7},{7,6},{8,9},{9,8},{10,11... | collective-permute-start | bytes 786440 | tf_op jit(solution)/shard_map/ppermute | solution.py:306
  40.4 2.2 %collective-permute-start.16 = (f32[4,2,64,128]{3,2,1,0:T(8,128)S(1)}, f32[4,2,64,128]{3,2,1,0:T(8,128)S(1)}, u32[]{:S(2)}, u32[]{:S(2)}) collective-permute-start(f32[4,2,64,128]{3,2,1,0:T(8,128)S(1)} %collective-permute-done.14.refs_15_), channel_id=1, source_target_pairs={{0,1},{1,0},{2,3},{3,2},{4,5},{5,4},{6,7},{7,6},{8,9},{9,8},{10,11... | collective-permute-start | bytes 786440 | tf_op jit(solution)/shard_map/ppermute | solution.py:306
  (3 other events, 5.4 us)
